TPU v7x, 32 devices: a whole 2x2x4 slice. The times are simulated.
32 devices in a mesh: dp: 8 (over z, y), seq: 4 (over x, core).
Axes of the slice: x: 2, y: 2, z: 4, core: 2. Of those that a mesh axis runs over, the one named last changes fastest.
Arguments:
- cell_tokens: bfloat16 [16, 2048, 768], P('dp', 'seq'), may hold values from -6 to 6
- first_gain: float32 [2, 768], replicated, may hold values from 0.25 to 1.75
- first_bias: float32 [2, 768], replicated, may hold values from -1.75 to 1.75
- joined_weight: bfloat16 [2, 768, 2304], replicated, may hold values from -0.21875 to 0.21875
- query_value_bias: float32 [2, 1536], replicated, may hold values from -1.75 to 1.75
- output_weight: bfloat16 [2, 768, 768], replicated, may hold values from -0.875 to 0.875
- output_bias: float32 [2, 768], replicated, may hold values from -1.75 to 1.75
- second_gain: float32 [2, 768], replicated, may hold values from 0.25 to 1.75
- second_bias: float32 [2, 768], replicated, may hold values from -1.75 to 1.75
- up_weight: bfloat16 [2, 768, 3072], replicated, may hold values from -0.21875 to 0.21875
- up_bias: float32 [2, 3072], replicated, may hold values from -1.75 to 1.75
- down_weight: bfloat16 [2, 3072, 768], replicated, may hold values from -0.109375 to 0.109375
- down_bias: float32 [2, 768], replicated, may hold values from -1.75 to 1.75
- cotangent: bfloat16 [16, 2048, 768], P('dp', 'seq'), may hold values from -6 to 6
- gene_mask: int32 [16, 2048], P('dp', 'seq'), may hold values from 0 to 1, as said below
Outputs:
- block_output: float32 [16, 2048, 768], P('dp', 'seq')
- input_gradient: float32 [16, 2048, 768], P('dp', 'seq')
- first_gain_gradient: float32 [2, 768], P(None, ('dp', 'seq'))
- first_bias_gradient: float32 [2, 768], P(None, ('dp', 'seq'))
- joined_weight_gradient: float32 [2, 768, 2304], P(None, ('dp', 'seq'))
- query_value_bias_gradient: float32 [2, 1536], P(None, ('dp', 'seq'))
- output_weight_gradient: float32 [2, 768, 768], P(None, ('dp', 'seq'))
- output_bias_gradient: float32 [2, 768], P(None, ('dp', 'seq'))
- second_gain_gradient: float32 [2, 768], P(None, ('dp', 'seq'))
- second_bias_gradient: float32 [2, 768], P(None, ('dp', 'seq'))
- up_weight_gradient: float32 [2, 768, 3072], P(None, ('dp', 'seq'))
- up_bias_gradient: float32 [2, 3072], P(None, ('dp', 'seq'))
- down_weight_gradient: float32 [2, 3072, 768], P(None, ('dp', 'seq'))
- down_bias_gradient: float32 [2, 768], P(None, ('dp', 'seq'))
Inputs may be any that keep to these rules, and one draw needn't show every extreme that they name: `gene_mask`: 1 marks a masked gene, 0 a visible one; the share of masked genes differs from cell to cell.
All inputs are finite; a program needn't handle non-finite values.
Results may differ from a plain program's by a relative error of at most 0.014.
Values may be sent and summed in bfloat16 or wider, within the bound.
A program may use at most 320 MiB of HBM per device.

v0:
```python
import jax
import jax.numpy as jnp
from jax import lax
from jax.sharding import PartitionSpec as P

HEADS = 12


def layer_norm(stream, gain_row, bias_row):
    centre = jnp.mean(stream, axis=-1, keepdims=True)
    shifted = stream - centre
    spread = jnp.mean(shifted * shifted, axis=-1, keepdims=True)
    return shifted * lax.rsqrt(spread + 1e-05) * gain_row + bias_row


def gelu_exact(hidden):
    return jax.nn.gelu(hidden, approximate=False)


def project(normed, joined_mat, qv_row):
    model_width = normed.shape[-1]
    joined_bias = jnp.concatenate(
        [qv_row[:model_width], jnp.zeros((model_width,), jnp.float32), qv_row[model_width:]]
    )
    joined_rows = jnp.dot(normed, joined_mat, preferred_element_type=jnp.float32) + joined_bias
    return joined_rows.astype(jnp.bfloat16).reshape(
        normed.shape[0], normed.shape[1], 3, HEADS, model_width // HEADS
    )


def attend_forward(queries, key_rows, value_rows):
    cell_count, length, local_heads, head_size = queries.shape
    block_rows = min(512, length)
    blocks_cell = length // block_rows
    factor = head_size ** (-0.5)

    def attend_one_block(flat_index):
        cell_index = flat_index // blocks_cell
        first_row = flat_index % blocks_cell * block_rows
        query_block = lax.dynamic_slice(
            queries, (cell_index, first_row, 0, 0), (1, block_rows, local_heads, head_size)
        )[0]
        cell_keys = lax.dynamic_index_in_dim(key_rows, cell_index, 0, keepdims=False)
        cell_values = lax.dynamic_index_in_dim(value_rows, cell_index, 0, keepdims=False)
        scores = (
            jnp.einsum("qhd,khd->hqk", query_block, cell_keys, preferred_element_type=jnp.float32)
            * factor
        )
        highest = jnp.max(scores, axis=-1, keepdims=True)
        exponents = jnp.exp(scores - highest)
        totals = jnp.sum(exponents, axis=-1, keepdims=True)
        weights = (exponents / totals).astype(jnp.bfloat16)
        outcome = jnp.einsum(
            "hqk,khd->qhd", weights, cell_values, preferred_element_type=jnp.float32
        )
        return (outcome.astype(jnp.bfloat16), (highest + jnp.log(totals))[:, :, 0])

    outcome, log_sums = lax.map(attend_one_block, jnp.arange(cell_count * blocks_cell))
    return (
        outcome.reshape(cell_count, length, local_heads, head_size),
        log_sums.reshape(cell_count, blocks_cell, local_heads, block_rows),
    )


def attend_backward(queries, key_rows, value_rows, log_sums, upstream):
    cell_count, length, local_heads, head_size = queries.shape
    block_rows = min(512, length)
    blocks_cell = length // block_rows
    factor = head_size ** (-0.5)

    def one_cell(cell_index):
        cell_queries = lax.dynamic_index_in_dim(queries, cell_index, 0, keepdims=False)
        cell_keys = lax.dynamic_index_in_dim(key_rows, cell_index, 0, keepdims=False)
        cell_values = lax.dynamic_index_in_dim(value_rows, cell_index, 0, keepdims=False)
        cell_upstream = lax.dynamic_index_in_dim(upstream, cell_index, 0, keepdims=False)
        cell_sums = lax.dynamic_index_in_dim(log_sums, cell_index, 0, keepdims=False)

        def one_one_block(carry, block_index):
            key_delta, value_delta = carry
            first_row = block_index * block_rows
            query_block = lax.dynamic_slice_in_dim(cell_queries, first_row, block_rows, 0)
            upstream_block = lax.dynamic_slice_in_dim(cell_upstream, first_row, block_rows, 0)
            sums_block = lax.dynamic_index_in_dim(cell_sums, block_index, 0, keepdims=False)
            scores = (
                jnp.einsum(
                    "qhd,khd->hqk", query_block, cell_keys, preferred_element_type=jnp.float32
                )
                * factor
            )
            weights = jnp.exp(scores - sums_block[:, :, None])
            weight_delta = jnp.einsum(
                "qhd,khd->hqk", upstream_block, cell_values, preferred_element_type=jnp.float32
            )
            inner = jnp.sum(weights * weight_delta, axis=-1, keepdims=True)
            score_delta = (weights * (weight_delta - inner)).astype(jnp.bfloat16)
            query_delta = (
                jnp.einsum(
                    "hqk,khd->qhd", score_delta, cell_keys, preferred_element_type=jnp.float32
                )
                * factor
            ).astype(jnp.bfloat16)
            key_delta = (
                key_delta
                + jnp.einsum(
                    "hqk,qhd->khd", score_delta, query_block, preferred_element_type=jnp.float32
                )
                * factor
            )
            value_delta = value_delta + jnp.einsum(
                "hqk,qhd->khd",
                weights.astype(jnp.bfloat16),
                upstream_block,
                preferred_element_type=jnp.float32,
            )
            return ((key_delta, value_delta), query_delta)

        zero_delta = jnp.zeros((length, local_heads, head_size), jnp.float32)
        (key_delta, value_delta), query_delta = lax.scan(
            one_one_block, (zero_delta, zero_delta), jnp.arange(blocks_cell)
        )
        query_delta = query_delta.reshape(length, local_heads, head_size)
        return jnp.stack(
            [query_delta, key_delta.astype(jnp.bfloat16), value_delta.astype(jnp.bfloat16)], axis=1
        )

    return lax.map(one_cell, jnp.arange(cell_count))


def on_device(
    cell_tokens,
    first_gain,
    first_bias,
    joined_weight,
    query_value_bias,
    output_weight,
    output_bias,
    second_gain,
    second_bias,
    up_weight,
    up_bias,
    down_weight,
    down_bias,
    cotangent,
    gene_mask,
):
    stream = cell_tokens.astype(jnp.float32)
    cell_count, local_genes, model_width = stream.shape
    head_size = model_width // HEADS
    layer_count = joined_weight.shape[0]
    stored = []
    for layer_index in range(layer_count):
        normed_one, norm_one_back = jax.vjp(
            layer_norm, stream, first_gain[layer_index], first_bias[layer_index]
        )
        normed_one = normed_one.astype(jnp.bfloat16)
        joined_rows = project(normed_one, joined_weight[layer_index], query_value_bias[layer_index])
        head_rows = lax.all_to_all(joined_rows, "seq", split_axis=3, concat_axis=1, tiled=True)
        attended, log_sums = attend_forward(
            head_rows[:, :, 0], head_rows[:, :, 1], head_rows[:, :, 2]
        )
        returned = lax.all_to_all(attended, "seq", split_axis=1, concat_axis=2, tiled=True).reshape(
            cell_count, local_genes, model_width
        )
        middle = stream + (
            jnp.dot(returned, output_weight[layer_index], preferred_element_type=jnp.float32)
            + output_bias[layer_index]
        )
        normed_two, norm_two_back = jax.vjp(
            layer_norm, middle, second_gain[layer_index], second_bias[layer_index]
        )
        normed_two = normed_two.astype(jnp.bfloat16)
        hidden = (
            jnp.dot(normed_two, up_weight[layer_index], preferred_element_type=jnp.float32)
            + up_bias[layer_index]
        )
        active, gelu_back = jax.vjp(gelu_exact, hidden)
        active = active.astype(jnp.bfloat16)
        stream = middle + (
            jnp.dot(active, down_weight[layer_index], preferred_element_type=jnp.float32)
            + down_bias[layer_index]
        )
        saved_heads = head_rows
        stored.append(
            (
                norm_one_back,
                normed_one,
                saved_heads,
                log_sums,
                returned,
                norm_two_back,
                normed_two,
                gelu_back,
                active,
            )
        )
    carried = cotangent.astype(jnp.float32) * gene_mask.astype(jnp.float32)[:, :, None]
    per_layer = [None] * layer_count
    for layer_index in reversed(range(layer_count)):
        (
            norm_one_back,
            normed_one,
            saved_heads,
            log_sums,
            returned,
            norm_two_back,
            normed_two,
            gelu_back,
            active,
        ) = stored[layer_index]
        branch_delta = carried.astype(jnp.bfloat16)
        down_bias_delta = jnp.sum(branch_delta.astype(jnp.float32), axis=(0, 1))
        down_delta = jnp.einsum(
            "csf,csd->fd", active, branch_delta, preferred_element_type=jnp.float32
        )
        active_delta = jnp.einsum(
            "csd,fd->csf",
            branch_delta,
            down_weight[layer_index],
            preferred_element_type=jnp.float32,
        )
        (hidden_delta,) = gelu_back(active_delta)
        hidden_delta = hidden_delta.astype(jnp.bfloat16)
        up_bias_delta = jnp.sum(hidden_delta.astype(jnp.float32), axis=(0, 1))
        up_delta = jnp.einsum(
            "csd,csf->df", normed_two, hidden_delta, preferred_element_type=jnp.float32
        )
        normed_two_delta = jnp.einsum(
            "csf,df->csd", hidden_delta, up_weight[layer_index], preferred_element_type=jnp.float32
        )
        middle_delta, gain_two_delta, bias_two_delta = norm_two_back(normed_two_delta)
        middle_delta = carried + middle_delta
        output_delta_rows = middle_delta.astype(jnp.bfloat16)
        output_bias_delta = jnp.sum(output_delta_rows.astype(jnp.float32), axis=(0, 1))
        output_delta = jnp.einsum(
            "csd,cse->de", returned, output_delta_rows, preferred_element_type=jnp.float32
        )
        returned_delta = jnp.einsum(
            "cse,de->csd",
            output_delta_rows,
            output_weight[layer_index],
            preferred_element_type=jnp.float32,
        ).astype(jnp.bfloat16)
        head_upstream = lax.all_to_all(
            returned_delta.reshape(cell_count, local_genes, HEADS, head_size),
            "seq",
            split_axis=2,
            concat_axis=1,
            tiled=True,
        )
        head_delta = attend_backward(
            saved_heads[:, :, 0],
            saved_heads[:, :, 1],
            saved_heads[:, :, 2],
            log_sums,
            head_upstream,
        )
        joined_delta_rows = lax.all_to_all(
            head_delta, "seq", split_axis=1, concat_axis=3, tiled=True
        ).reshape(cell_count, local_genes, 3 * model_width)
        joined_delta = jnp.einsum(
            "csd,cse->de", normed_one, joined_delta_rows, preferred_element_type=jnp.float32
        )
        joined_sums = jnp.sum(joined_delta_rows.astype(jnp.float32), axis=(0, 1))
        query_value_delta = jnp.concatenate(
            [joined_sums[:model_width], joined_sums[2 * model_width :]]
        )
        normed_one_delta = jnp.einsum(
            "cse,de->csd",
            joined_delta_rows,
            joined_weight[layer_index],
            preferred_element_type=jnp.float32,
        )
        stream_delta, gain_one_delta, bias_one_delta = norm_one_back(normed_one_delta)
        carried = middle_delta + stream_delta
        per_layer[layer_index] = (
            gain_one_delta,
            bias_one_delta,
            joined_delta,
            query_value_delta,
            output_delta,
            output_bias_delta,
            gain_two_delta,
            bias_two_delta,
            up_delta,
            up_bias_delta,
            down_delta,
            down_bias_delta,
        )
    stacked = [
        jnp.stack([per_layer[layer_index][member] for layer_index in range(layer_count)])
        for member in range(12)
    ]
    (
        gain_one_all,
        bias_one_all,
        joined_all,
        query_value_all,
        output_all,
        output_bias_all,
        gain_two_all,
        bias_two_all,
        up_all,
        up_bias_all,
        down_all,
        down_bias_all,
    ) = stacked
    finals = (
        lax.psum_scatter(gain_one_all, ("dp", "seq"), scatter_dimension=1, tiled=True),
        lax.psum_scatter(bias_one_all, ("dp", "seq"), scatter_dimension=1, tiled=True),
        lax.psum_scatter(joined_all, ("dp", "seq"), scatter_dimension=1, tiled=True),
        lax.psum_scatter(query_value_all, ("dp", "seq"), scatter_dimension=1, tiled=True),
        lax.psum_scatter(output_all, ("dp", "seq"), scatter_dimension=1, tiled=True),
        lax.psum_scatter(output_bias_all, ("dp", "seq"), scatter_dimension=1, tiled=True),
        lax.psum_scatter(gain_two_all, ("dp", "seq"), scatter_dimension=1, tiled=True),
        lax.psum_scatter(bias_two_all, ("dp", "seq"), scatter_dimension=1, tiled=True),
        lax.psum_scatter(up_all, ("dp", "seq"), scatter_dimension=1, tiled=True),
        lax.psum_scatter(up_bias_all, ("dp", "seq"), scatter_dimension=1, tiled=True),
        lax.psum_scatter(down_all, ("dp", "seq"), scatter_dimension=1, tiled=True),
        lax.psum_scatter(down_bias_all, ("dp", "seq"), scatter_dimension=1, tiled=True),
    )
    return (
        stream,
        carried,
        finals[0],
        finals[1],
        finals[2],
        finals[3],
        finals[4],
        finals[5],
        finals[6],
        finals[7],
        finals[8],
        finals[9],
        finals[10],
        finals[11],
    )


def solution(mesh):
    placed = (
        P("dp", "seq", None),
        P(),
        P(),
        P(),
        P(),
        P(),
        P(),
        P(),
        P(),
        P(),
        P(),
        P(),
        P(),
        P("dp", "seq", None),
        P("dp", "seq"),
    )
    return jax.shard_map(
        on_device,
        mesh=mesh,
        in_specs=placed,
        out_specs=(
            P("dp", "seq", None),
            P("dp", "seq", None),
            P(None, ("dp", "seq")),
            P(None, ("dp", "seq")),
            P(None, ("dp", "seq"), None),
            P(None, ("dp", "seq")),
            P(None, ("dp", "seq"), None),
            P(None, ("dp", "seq")),
            P(None, ("dp", "seq")),
            P(None, ("dp", "seq")),
            P(None, ("dp", "seq"), None),
            P(None, ("dp", "seq")),
            P(None, ("dp", "seq"), None),
            P(None, ("dp", "seq")),
        ),
        check_vma=False,
    )
```

profile of v0, /device:TPU:0, one launch (start us, length us, event | category | flops | bytes accessed | tf_op | source)
XLA Modules:
  0.0 2588.9 jit_solution(1116177262080354117)
XLA Ops:
  14.4 8.8 add_convert_fusion.3
  40.1 54.4 %all-to-all-done = bf16[2,512,3,12,64]{1,4,2,0,3:T(8,128)(2,1)} async-done(((bf16[2,512,3,12,64]{1,4,2,0,3:T(8,128)(2,1)}), bf16[2,512,3,12,64]{1,4,2,0,3:T(8,128)(2,1)}, u32[]{:S(2)}, u32[]{:S(2)}) %all-to-all-start) | async-done | bytes 4718624 | tf_op jit(solution)/shard_map/all_to_all | solution.py:157
  103.2 8.7 all_to_all.99
  117.5 110.1 %while.78 = (s32[]{:T(128)}, bf16[8,512,3,64]{1,3,2,0:T(8,128)(2,1)S(1)}, f32[8,3,512]{2,1,0:T(4,128)}, s32[8]{0:T(128)S(1)}, bf16[2,2048,3,64]{1,3,2,0:T(8,128)...) while((s32[]{:T(128)}, ...), condition=%wide.region_5.6_spmd, body=%wide.region_2.5_spmd.sunk | while | flops 833714688 | bytes 39773096 | solution.py:58
  248.7 17.5 all-to-all-done.1
  282.7 15.3 fusion.140
  298.0 31.9 %multiply_convert_fusion.3 = (bf16[2,512,3072]{2,1,0:T(8,128)(2,1)S(1)}, f32[2,512,3072]{2,1,0:T(8,128)}) fusion(f32[2,512,3072]{2,1,0:T(8,128)} %get-tuple-element.651, f32[3072]{0:T(1024)S(1)} %bitcast.462, u8[512,3072]{1,0:T(8,128)(4,1)S(1)} %get-tuple-element.467, u8[512,3072]{1,0:T(8,128)(4,1)S(1)} %get-tuple-element.466), kind=kLoop, calls=%fused_computation.145 | loop fusion | flops 223346688 | bytes 34615296 | tf_op jit(solution)/shard_map/convert_element_type | solution.py:177
  330.0 9.9 fusion.186
  364.7 53.8 %all-to-all-done.2 = bf16[2,512,3,12,64]{1,4,2,0,3:T(8,128)(2,1)} async-done(((bf16[2,512,3,12,64]{1,4,2,0,3:T(8,128)(2,1)}), bf16[2,512,3,12,64]{1,4,2,0,3:T(8,128)(2,1)}, u32[]{:S(2)}, u32[]{:S(2)}) %all-to-all-start.2) | async-done | bytes 4718624 | tf_op jit(solution)/shard_map/all_to_all | solution.py:157
  427.0 8.8 all_to_all.106
  441.8 110.4 %while.79 = (s32[]{:T(128)}, bf16[8,512,3,64]{1,3,2,0:T(8,128)(2,1)}, f32[8,3,512]{2,1,0:T(4,128)S(1)}, s32[8]{0:T(128)S(1)}, bf16[2,2048,3,64]{1,3,2,0:T(8,128)...) while((s32[]{:T(128)}, ...), condition=%wide.region_13.14_spmd, body=%wide.region_10.13_spmd.sunk | while | flops 833714688 | bytes 39772588 | solution.py:58
  559.2 8.8 copy.163
  577.9 20.1 all-to-all-done.3
  602.9 8.7 copy.210
  617.5 15.3 fusion.141
  632.9 32.0 %multiply_convert_fusion.2 = (bf16[2,512,3072]{2,1,0:T(8,128)(2,1)}, f32[2,512,3072]{2,1,0:T(8,128)}) fusion(f32[2,512,3072]{2,1,0:T(8,128)} %get-tuple-element.656, f32[3072]{0:T(1024)S(1)} %bitcast.465, u8[512,3072]{1,0:T(8,128)(4,1)S(1)} %get-tuple-element.465, u8[512,3072]{1,0:T(8,128)(4,1)S(1)} %get-tuple-element.464), kind=kLoop, calls=%fused_computation.132 | loop fusion | flops 223346688 | bytes 34615296 | tf_op jit(solution)/shard_map/convert_element_type | solution.py:177
  664.9 17.4 convert_reduce_fusion
  682.3 9.8 multiply_reduce_fusion.4
  704.7 20.0 all-to-all-done.4
  731.7 343.7 %while.81 = (s32[]{:T(128)}, bf16[2,2048,3,3,64]{1,4,3,2,0:T(8,128)(2,1)}, s32[2]{0:T(128)}, bf16[2,2048,3,64]{1,3,2,0:T(8,128)(2,1)}, bf16[2,2048,3,64]{1,3,2,0...) while((s32[]{:T(128)}, ...), condition=%wide.region_22.23_spmd, body=%wide.region_18.22_spmd.sunk | while | flops 2061040128 | bytes 186281744 | solution.py:126
  740.0 158.1 %while.84 = (s32[]{:T(128)}, f32[2048,3,64]{0,2,1:T(8,128)S(1)}, f32[2048,3,64]{0,2,1:T(8,128)}, bf16[4,512,3,64]{1,3,2,0:T(8,128)(2,1)}, s32[4]{0:T(128)S(1)}, ...) while((s32[]{:T(128)}, f32[2048,3,64]{0,2,1:T(8,128)S(1)}, ...), condition=%wide.region_21.21_spmd.clone, body=%wide.region_19.20_spmd.clone.sunk | while | flops 2053175808 | bytes 166964080 | solution.py:118
  911.7 158.1 %while.84 = (s32[]{:T(128)}, f32[2048,3,64]{0,2,1:T(8,128)S(1)}, f32[2048,3,64]{0,2,1:T(8,128)}, bf16[4,512,3,64]{1,3,2,0:T(8,128)(2,1)}, s32[4]{0:T(128)S(1)}, ...) while((s32[]{:T(128)}, f32[2048,3,64]{0,2,1:T(8,128)S(1)}, ...), condition=%wide.region_21.21_spmd.clone, body=%wide.region_19.20_spmd.clone.sunk | while | flops 2053175808 | bytes 166964080 | solution.py:118
  1075.3 23.2 copy.171
  1098.5 10.8 reshape.357
  1109.3 59.8 %all_to_all.132 = bf16[4,2,294912]{2,1,0:T(2,128)(2,1)} all-to-all(bf16[4,2,294912]{2,1,0:T(2,128)(2,1)} %reshape.357), channel_id=1, replica_groups=mesh['dp'=8,'seq'=4] {'seq'}, dimensions={0} | all-to-all | bytes 9437184 | tf_op jit(solution)/shard_map/all_to_all | solution.py:257
  1169.1 10.1 reshape.358
  1179.2 23.8 copy.212
  1206.6 9.0 fusion.175
  1220.2 18.1 convert_reduce_fusion.1
  1238.4 10.4 multiply_reduce_fusion.5
  1260.3 20.0 all-to-all-done.6
  1287.2 345.0 %while.83 = (s32[]{:T(128)}, bf16[2,2048,3,3,64]{1,4,3,2,0:T(8,128)(2,1)}, s32[2]{0:T(128)}, bf16[2,2048,3,64]{1,3,2,0:T(8,128)(2,1)}, bf16[2,2048,3,64]{1,3,2,0...) while((s32[]{:T(128)}, ...), condition=%wide.region_31.32_spmd, body=%wide.region_27.31_spmd.sunk | while | flops 2061040128 | bytes 185888464 | solution.py:126
  1296.2 158.1 %while.85 = (s32[]{:T(128)}, f32[2048,3,64]{0,2,1:T(8,128)S(1)}, f32[2048,3,64]{0,2,1:T(8,128)}, bf16[4,512,3,64]{1,3,2,0:T(8,128)(2,1)}, s32[4]{0:T(128)S(1)}, ...) while((s32[]{:T(128)}, f32[2048,3,64]{0,2,1:T(8,128)S(1)}, ...), condition=%wide.region_30.30_spmd.clone, body=%wide.region_28.29_spmd.clone.sunk | while | flops 2053175808 | bytes 166964080 | solution.py:118
  1468.5 158.1 %while.85 = (s32[]{:T(128)}, f32[2048,3,64]{0,2,1:T(8,128)S(1)}, f32[2048,3,64]{0,2,1:T(8,128)}, bf16[4,512,3,64]{1,3,2,0:T(8,128)(2,1)}, s32[4]{0:T(128)S(1)}, ...) while((s32[]{:T(128)}, f32[2048,3,64]{0,2,1:T(8,128)S(1)}, ...), condition=%wide.region_30.30_spmd.clone, body=%wide.region_28.29_spmd.clone.sunk | while | flops 2053175808 | bytes 166964080 | solution.py:118
  1632.2 23.2 copy.179
  1655.4 10.8 reshape.359
  1685.7 39.2 %all-to-all-done.7 = bf16[4,2,294912]{2,1,0:T(2,128)(2,1)} async-done(((bf16[4,2,294912]{2,1,0:T(2,128)(2,1)}), bf16[4,2,294912]{2,1,0:T(2,128)(2,1)}, u32[]{:S(2)}, u32[]{:S(2)}) %all-to-all-start.7) | async-done | bytes 4718624 | tf_op jit(solution)/shard_map/all_to_all | solution.py:257
  1725.0 10.2 reshape.360
  1735.2 23.8 copy.214
  1770.9 9.1 convolution_bitcast_fusion.4
  1792.7 11.1 pad_maximum_fusion.2
  1827.5 9.3 convolution_bitcast_fusion.2
  1852.6 10.4 add_add_fusion.8
  1875.0 41.1 %all-reduce.6 = (f32[2,768]{1,0:T(2,128)S(1)}, f32[2,768]{1,0:T(2,128)S(1)}, f32[2,768]{1,0:T(2,128)S(1)}, f32[2,768]{1,0:T(2,128)S(1)}, f32[2,768]{1,0:T(2,128)S(1)}, /*index=5*/f32[2,768]{1,0:T(2,128)S(1)}) all-reduce(f32[2,768]{1,0:T(2,128)S(1)} %pad_maximum_fusion.10, ...), channel_id=2, replica_groups=mesh['dp'=8,'seq'=4] {'dp','seq'}, use_global_device_ids=true, to_apply=%region_36.37.clone | all-reduce | flops 9216 | bytes 73728
  1926.4 62.2 %reduce-scatter.19.cloned.1.call-done = f32[2,24,768]{2,1,0:T(8,128)} async-done(((f32[2,768,768]{2,1,0:T(8,128)}), f32[2,24,768]{2,1,0:T(8,128)}) %reduce-scatter.19.cloned.1.call-update) | async-done | bytes 147472 | tf_op jit(solution)/shard_map/reduce_scatter | solution.py:312
  1988.6 169.4 %reduce-scatter.17.cloned.1.call-done = f32[2,24,2304]{2,1,0:T(8,128)} async-done(((f32[2,768,2304]{2,1,0:T(8,128)}), f32[2,24,2304]{2,1,0:T(8,128)}) %reduce-scatter.17.cloned.1.call-update) | async-done | bytes 442384 | tf_op jit(solution)/shard_map/reduce_scatter | solution.py:310
  2158.1 211.8 %reduce-scatter.23.cloned.1.call-done = f32[2,96,768]{2,1,0:T(8,128)} async-done(((f32[2,3072,768]{2,1,0:T(8,128)}), f32[2,96,768]{2,1,0:T(8,128)}) %reduce-scatter.23.cloned.1.call-update) | async-done | bytes 589840 | tf_op jit(solution)/shard_map/reduce_scatter | solution.py:318
  2369.9 211.9 %reduce-scatter.21.cloned.1.call-done = f32[2,24,3072]{2,1,0:T(8,128)} async-done(((f32[2,768,3072]{2,1,0:T(8,128)}), f32[2,24,3072]{2,1,0:T(8,128)}) %reduce-scatter.21.cloned.1.call-update) | async-done | bytes 589840 | tf_op jit(solution)/shard_map/reduce_scatter | solution.py:316
  (783 shorter events, 1109.7 us)
Async XLA Ops:
  34.9 59.7 %all-to-all-start = ((bf16[2,512,3,12,64]{1,4,2,0,3:T(8,128)(2,1)}), bf16[2,512,3,12,64]{1,4,2,0,3:T(8,128)(2,1)}, u32[]{:S(2)}, u32[]{:S(2)}) async-start(bf16[2,512,3,12,64]{1,4,2,0,3:T(8,128)(2,1)} %copy.150), calls=%async_computation | async-start | bytes 9437184 | tf_op jit(solution)/shard_map/all_to_all | solution.py:157
  242.1 24.1 all-to-all-start.1
  248.1 34.6 %copy-start.30 = (f32[768]{0:T(1024)}, f32[768]{0:T(1024)S(1)}, u32[]{:S(2)}) copy-start(f32[768]{0:T(1024)S(1)} %get-tuple-element.667) | copy-start | bytes 9220
  248.1 34.6 %copy-start.35 = (f32[768]{0:T(1024)}, f32[768]{0:T(1024)S(1)}, u32[]{:S(2)}) copy-start(f32[768]{0:T(1024)S(1)} %get-tuple-element.491) | copy-start | bytes 9220
  248.7 49.3 %copy-start.54 = (f32[1,3072]{1,0:T(1,128)}, f32[1,3072]{1,0:T(1,128)S(1)}, u32[]{:S(2)}) copy-start(f32[1,3072]{1,0:T(1,128)S(1)} %get-tuple-element.646) | copy-start | bytes 36868
  281.2 48.8 %copy-start.9 = (f32[2,512,768]{2,1,0:T(8,128)}, f32[2,512,768]{2,1,0:T(8,128)S(1)}, u32[]{:S(2)}) copy-start(f32[2,512,768]{2,1,0:T(8,128)S(1)} %get-tuple-element.650) | copy-start | bytes 9437188
  281.2 16.8 copy-start.39
  281.7 16.2 copy-start.44
  298.0 43.9 %slice-start.6 = ((s8[7077888]{0:T(1024)(128)(4,1)}), s8[4194304]{0:T(1024)(128)(4,1)S(1)}, s32[]{:S(2)}) async-start(s8[7077888]{0:T(1024)(128)(4,1)} %bitcast.471), calls=%async_computation.26 | async-start | bytes 8388608
  330.0 12.0 copy-start.57
  330.0 12.0 copy-start.88
  330.0 12.0 copy-start.95
  330.0 12.0 slice-start.7
  339.9 273.5 %copy-start.2 = (f32[2,512,768]{2,1,0:T(8,128)}, f32[2,512,768]{2,1,0:T(8,128)S(1)}, u32[]{:S(2)}) copy-start(f32[2,512,768]{2,1,0:T(8,128)S(1)} %get-tuple-element.653) | copy-start | bytes 9437188
  359.4 59.1 %all-to-all-start.2 = ((bf16[2,512,3,12,64]{1,4,2,0,3:T(8,128)(2,1)}), bf16[2,512,3,12,64]{1,4,2,0,3:T(8,128)(2,1)}, u32[]{:S(2)}, u32[]{:S(2)}) async-start(bf16[2,512,3,12,64]{1,4,2,0,3:T(8,128)(2,1)} %copy.159), calls=%async_computation.2 | async-start | bytes 9437184 | tf_op jit(solution)/shard_map/all_to_all | solution.py:157
  573.1 24.9 all-to-all-start.3
  577.9 115.6 %copy-start.63 = (f32[2,512]{1,0:T(2,128)}, f32[2,512]{1,0:T(2,128)S(1)}, u32[]{:S(2)}) copy-start(f32[2,512]{1,0:T(2,128)S(1)} %convert_element_type.159) | copy-start | bytes 12292
  602.9 10.5 copy-start.98
  617.0 15.9 copy-start.12
  617.0 75.2 %copy-start.42 = (f32[2,512]{1,0:T(2,128)}, f32[2,512]{1,0:T(2,128)S(1)}, u32[]{:S(2)}) copy-start(f32[2,512]{1,0:T(2,128)S(1)} %broadcast_multiply_fusion) | copy-start | bytes 12292
  617.5 74.7 %copy-start.50 = (f32[2,512]{1,0:T(2,128)}, f32[2,512]{1,0:T(2,128)S(1)}, u32[]{:S(2)}) copy-start(f32[2,512]{1,0:T(2,128)S(1)} %fusion.171) | copy-start | bytes 12292
  632.9 32.0 %copy-start.20 = (bf16[2,512,768]{2,1,0:T(8,128)(2,1)S(1)}, bf16[2,512,768]{2,1,0:T(8,128)(2,1)}, u32[]{:S(2)}) copy-start(bf16[2,512,768]{2,1,0:T(8,128)(2,1)} %param.40) | copy-start | bytes 4718596
  664.9 17.4 copy-start.13
  701.1 23.6 all-to-all-start.4
  1220.2 29.9 %copy-start.7 = (f32[2,512,768]{2,1,0:T(8,128)}, f32[2,512,768]{2,1,0:T(8,128)S(1)}, u32[]{:S(2)}) copy-start(f32[2,512,768]{2,1,0:T(8,128)S(1)} %get-tuple-element.605) | copy-start | bytes 9437188
  1220.2 18.1 copy-start.31
  1220.2 18.1 copy-start.40
  1220.2 18.1 copy-start.45
  1238.3 10.4 copy-start.71
  1238.3 10.5 copy-start.10
  1256.7 23.6 all-to-all-start.6
  1666.1 58.8 %all-to-all-start.7 = ((bf16[4,2,294912]{2,1,0:T(2,128)(2,1)}), bf16[4,2,294912]{2,1,0:T(2,128)(2,1)}, u32[]{:S(2)}, u32[]{:S(2)}) async-start(bf16[4,2,294912]{2,1,0:T(2,128)(2,1)} %reshape.359), calls=%async_computation.7 | async-start | bytes 9437184 | tf_op jit(solution)/shard_map/all_to_all | solution.py:257
  1671.1 192.1 %reduce-scatter.27.cloned.1.call-start = ((), (), s32[]{:S(2)}) async-start(), calls=%async_computation.19 | async-start | bytes 1622016
  1676.2 248.8 %reduce-scatter.25.cloned.1.call-start = ((), (), s32[]{:S(2)}) async-start(), calls=%async_computation.18 | async-start | bytes 811008
  1764.9 223.8 %reduce-scatter.19.cloned.1.call-start = ((), (), s32[]{:S(2)}) async-start(), calls=%async_computation.15 | async-start | bytes 4866048 | tf_op jit(solution)/shard_map/reduce_scatter | solution.py:312
  1769.1 389.0 %reduce-scatter.17.cloned.1.call-start = ((), (), s32[]{:S(2)}) async-start(), calls=%async_computation.14 | async-start | bytes 14598144 | tf_op jit(solution)/shard_map/reduce_scatter | solution.py:310
  1803.7 566.1 %reduce-scatter.23.cloned.1.call-start = ((), (), s32[]{:S(2)}) async-start(), calls=%async_computation.17 | async-start | bytes 19464192 | tf_op jit(solution)/shard_map/reduce_scatter | solution.py:318
  1826.9 10.0 copy-start.32
  1826.9 10.0 copy-start.36
  1826.9 10.0 copy-start.41
  1826.9 754.9 %reduce-scatter.21.cloned.1.call-start = ((), (), s32[]{:S(2)}) async-start(), calls=%async_computation.16 | async-start | bytes 19464192 | tf_op jit(solution)/shard_map/reduce_scatter | solution.py:316
  1852.5 10.5 copy-start.84
  1852.5 10.5 copy-start.103
  1852.6 10.5 copy-start.102
  1852.6 10.5 copy-start.85
  1852.6 10.6 copy-start.101
  1852.6 10.6 copy-start.83
  1873.2 46.7 %copy-start.79 = (f32[2,512]{1,0:T(2,128)S(1)}, f32[2,512]{1,0:T(2,128)}, u32[]{:S(2)}) copy-start(f32[2,512]{1,0:T(2,128)} %copy-done.78) | copy-start | bytes 12292
  (138 other events, 729.1 us)
Sparse Core Ops, SparseCore 0:
  1677.2 99.5 reduce-scatter.26
  1781.9 94.5 reduce-scatter.24
  1882.5 106.0 reduce-scatter.18
  1996.1 161.9 reduce-scatter.16
  2166.0 203.7 reduce-scatter.22
  2377.8 203.9 reduce-scatter.20
where the time goes:
time: 2600 us; the launch traced here: 2590 us
  waiting for transfers between devices  881 us (34%)
  matrix products  808 us (31%)
  local copies, waits for them, and re-layouts  403 us (16%)
  other arithmetic  256 us (10%)
  blocking collectives  101 us (4%)
  loops' own time  93.2 us (4%)
  starting transfers between devices  31.7 us (1%)
    reduce_scatter x1, waiting for transfers between devices, on_device(): lax.psum_scatter(up_all, ('dp', 'seq'), scatter_dimension=1, tiled=True)  212 us
    reduce_scatter x1, waiting for transfers between devices, on_device(): lax.psum_scatter(down_all, ('dp', 'seq'), scatter_dimension=1, tiled=True)  212 us
    reduce_scatter x1, waiting for transfers between devices, on_device(): lax.psum_scatter(joined_all, ('dp', 'seq'), scatter_dimension=1, tiled=True)  169 us
    dot_general x16, matrix products, one_one_block(): jnp.einsum('hqk,qhd->khd', weights.astype(jnp.bfloat16), upstream_block,...  137 us
    dot_general x16, matrix products, one_one_block(): jnp.einsum('qhd,khd->hqk', query_block, cell_keys, preferred_element_type...  117 us
    dot_general x16, matrix products, one_one_block(): jnp.einsum('qhd,khd->hqk', upstream_block, cell_values, preferred_element...  110 us
    all_to_all x2, waiting for transfers between devices, on_device(): lax.all_to_all(joined_rows, 'seq', split_axis=3, concat_axis=1, tiled=True)  108 us
    unnamed x228, local copies, waits for them, and re-layouts  82 us
  transfers between devices with their start and end apart: 13, of which 11 were waited for; matrix products, arithmetic and copies ran while one was open for 7% of the time, Pallas kernels for 0%

commit v1 on v0

v1 whole, which is shorter than its diff:
```python
import functools

import jax
import jax.numpy as jnp
from jax import lax
from jax.experimental import pallas as pl
from jax.experimental.pallas import tpu as pltpu
from jax.sharding import PartitionSpec as P

HEAD = 64
LOG2E = 1.4426950408889634
BF = jnp.bfloat16
F32 = jnp.float32
NN = ((1,), (0,))
NT = ((1,), (1,))
SAFE = 80.0


def dot(a, b, dims):
    return lax.dot_general(a, b, (dims, ((), ())), preferred_element_type=F32)


def params(mib):
    return pltpu.CompilerParams(vmem_limit_bytes=mib << 20)


def row(index):
    return pl.BlockSpec((1, index[1]), lambda *_: (index[0], 0))


def normalise(x):
    n = x.shape[-1]
    centred = x - jnp.sum(x, axis=-1, keepdims=True) * (1.0 / n)
    inverse = lax.rsqrt(jnp.sum(centred * centred, axis=-1, keepdims=True) * (1.0 / n) + 1e-05)
    return centred * inverse, inverse


def norm_back(upstream, gain, unit, inverse):
    n = unit.shape[-1]
    e = upstream * gain
    mean_e = jnp.sum(e, axis=-1, keepdims=True) * (1.0 / n)
    mean_eu = jnp.sum(e * unit, axis=-1, keepdims=True) * (1.0 / n)
    return inverse * (e - mean_e - unit * mean_eu)


def column_sum(x):
    return jnp.sum(x, axis=0, keepdims=True)


def gelu_pair(x):
    a = jnp.abs(x)
    base = 1.0 + 0.23164190 * a
    t = pl.reciprocal(base, approx=True)
    t = t * (2.0 - base * t)
    poly = t * (0.127414796 + t * (-0.142248368 + t * (0.7107068705 + t * (-0.7265760135 + t * 0.5307027145))))
    u = jnp.exp2(x * x * (-0.5 * LOG2E))
    half = poly * u
    cdf = jnp.where(x >= 0, 1.0 - half, half)
    return x * cdf, cdf + x * (u * 0.3989422804014327)


def qkv_tile(x, gain, bias, weight, row_bias, normed_ref, q_ref, kv_ref):
    d = x.shape[-1]
    unit, _ = normalise(x)
    normed = (unit * gain + bias).astype(BF)
    normed_ref[...] = normed
    for part in range(3):
        cols = slice(part * d, (part + 1) * d)
        out = dot(normed, weight[:, cols], NN)
        if part != 1:
            out = out + row_bias[:, cols]
        if part == 0:
            q_ref[...] = out.astype(BF)
        else:
            kv_ref[part - 1] = out.astype(BF)


def first_kernel(x, gain, bias, weight, row_bias, normed, q, kv):
    qkv_tile(x[...].astype(F32), gain[...], bias[...], weight, row_bias, normed, q, kv)


def first_call(x, layer, gain, bias, weight, row_bias, tile):
    t, d = x.shape
    return pl.pallas_call(
        first_kernel,
        grid=(t // tile,),
        in_specs=[
            pl.BlockSpec((tile, d), lambda i: (i, 0)),
            pl.BlockSpec((None, 1, d), lambda i: (layer, 0, 0)),
            pl.BlockSpec((None, 1, d), lambda i: (layer, 0, 0)),
            pl.BlockSpec((None, d, 3 * d), lambda i: (layer, 0, 0)),
            pl.BlockSpec((None, 1, 3 * d), lambda i: (layer, 0, 0)),
        ],
        out_specs=[
            pl.BlockSpec((tile, d), lambda i: (i, 0)),
            pl.BlockSpec((tile, d), lambda i: (i, 0)),
            pl.BlockSpec((2, tile, d), lambda i: (0, i, 0)),
        ],
        out_shape=[
            jax.ShapeDtypeStruct((t, d), BF),
            jax.ShapeDtypeStruct((t, d), BF),
            jax.ShapeDtypeStruct((2, t, d), BF),
        ],
        compiler_params=params(56),
        name="norm_qkv",
    )(x, gain, bias, weight, row_bias)


def attend_kernel(q, kv, kvo, out, lse, *, chunk):
    t = q.shape[0]
    c = LOG2E * HEAD**-0.5
    lane = lax.broadcasted_iota(jnp.int32, (128, 128), 0) // HEAD
    pick = (lane == lax.broadcasted_iota(jnp.int32, (128, 128), 1)).astype(BF)

    def squares(x):
        x = x.astype(F32)
        return jnp.max(dot((x * x).astype(BF), pick, NN), axis=0, keepdims=True)

    bound = squares(q[...]) * jnp.maximum(squares(kv[0]), squares(kvo[0]))
    fast = jnp.max(bound) * (c * c * 1.05) < SAFE * SAFE

    def run(stable):
        for head in range(2):
            ls = slice(HEAD * head, HEAD * head + HEAD)
            values = []
            for ref in (kv, kvo):
                v = ref[1, :, ls].astype(F32).T.astype(BF)
                values.append(jnp.concatenate([v, jnp.ones((16, t), BF)], axis=0))

            def score(j):
                block = q[j * chunk : (j + 1) * chunk, ls]
                return [dot(ref[0, :, ls], block, NT) for ref in (kv, kvo)]

            ahead = score(0)
            for j in range(t // chunk):
                s = ahead
                if j + 1 < t // chunk:
                    ahead = score(j + 1)
                if stable:
                    shift = c * jnp.maximum(
                        jnp.max(s[0], axis=0, keepdims=True), jnp.max(s[1], axis=0, keepdims=True)
                    )
                    p = [jnp.exp2(x * c - shift).astype(BF) for x in s]
                else:
                    shift = 0.0
                    p = [jnp.exp2(x * c).astype(BF) for x in s]
                total = dot(values[0], p[0], NN) + dot(values[1], p[1], NN)
                level = total[HEAD : HEAD + 1]
                cols = slice(j * chunk, (j + 1) * chunk)
                out[cols, ls] = (total[:HEAD] / level).T.astype(BF)
                lse[0, head : head + 1, cols] = shift + jnp.log2(level)

    pl.when(fast)(lambda: run(False))
    pl.when(jnp.logical_not(fast))(lambda: run(True))


def attend_call(q, kv, kvo):
    t, d = q.shape
    pairs = d // 128
    both = pl.BlockSpec((2, t, 128), lambda h: (0, 0, h))
    one = pl.BlockSpec((t, 128), lambda h: (0, h))
    return pl.pallas_call(
        functools.partial(attend_kernel, chunk=min(256, t)),
        grid=(pairs,),
        in_specs=[one, both, both],
        out_specs=[one, pl.BlockSpec((1, 8, t), lambda h: (h, 0, 0))],
        out_shape=[jax.ShapeDtypeStruct((t, d), BF), jax.ShapeDtypeStruct((pairs, 8, t), F32)],
        compiler_params=params(56),
        name="attend",
    )(q, kv, kvo)


def attend_back_kernel(q, kv, kvo, up, out, lse, dq, dkv, dkvo, *, chunk):
    t = q.shape[0]
    scale = HEAD**-0.5
    c = LOG2E * scale
    for head in range(2):
        ls = slice(HEAD * head, HEAD * head + HEAD)
        qh = q[:, ls]
        uh = up[:, ls]
        q_t = qh.astype(F32).T.astype(BF)
        u_t = uh.astype(F32).T.astype(BF)
        level = lse[0].T[:, head : head + 1]
        inner = jnp.sum(uh.astype(F32) * out[:, ls].astype(F32), axis=1, keepdims=True)
        blocks = [
            (src, dst, slice(i * chunk, (i + 1) * chunk))
            for src, dst in ((kvo, dkvo), (kv, dkv))
            for i in range(t // chunk)
        ]

        def products(block):
            src, _, rows = block
            return dot(qh, src[0, rows, ls], NT), dot(uh, src[1, rows, ls], NT)

        total = None
        ahead = products(blocks[0])
        for at, (src, dst, rows) in enumerate(blocks):
            s, dp = ahead
            if at + 1 < len(blocks):
                ahead = products(blocks[at + 1])
            p = jnp.exp2(s * c - level)
            ds = (p * (dp - inner)).astype(BF)
            dst[1, rows, ls] = dot(u_t, p.astype(BF), NN).T.astype(BF)
            dst[0, rows, ls] = (dot(q_t, ds, NN).T * scale).astype(BF)
            part = dot(ds, src[0, rows, ls], NN)
            total = part if total is None else total + part
        dq[:, ls] = (total * scale).astype(BF)


def attend_back_call(q, kv, kvo, up, out, lse):
    t, d = q.shape
    pairs = d // 128
    both = pl.BlockSpec((2, t, 128), lambda h: (0, 0, h))
    one = pl.BlockSpec((t, 128), lambda h: (0, h))
    return pl.pallas_call(
        functools.partial(attend_back_kernel, chunk=min(256, t)),
        grid=(pairs,),
        in_specs=[one, both, both, one, one, pl.BlockSpec((1, 8, t), lambda h: (h, 0, 0))],
        out_specs=[one, both, both],
        out_shape=[
            jax.ShapeDtypeStruct((t, d), BF),
            jax.ShapeDtypeStruct((2, t, d), BF),
            jax.ShapeDtypeStruct((2, t, d), BF),
        ],
        compiler_params=params(56),
        name="attend_back",
    )(q, kv, kvo, up, out, lse)


def forward_kernel(
    att, x, wo_h, wu_h, wd_h, bo, g2, b2, bu, bd, middle_o, n2_o, act_o, slope_o, next_o, wo, wu, wd, sems, *, layer, cut
):
    first = pl.program_id(0) == 0
    copies = [
        pltpu.make_async_copy(src.at[layer], dst, sems.at[i])
        for i, (src, dst) in enumerate(((wo_h, wo), (wu_h, wu), (wd_h, wd)))
    ]

    @pl.when(first)
    def _():
        for copy in copies:
            copy.start()
        copies[0].wait()

    middle = x[...].astype(F32) + (dot(att[...], wo[...], NN) + bo[...])
    middle_o[...] = middle
    unit, _ = normalise(middle)
    n2 = (unit * g2[...] + b2[...]).astype(BF)
    n2_o[...] = n2

    @pl.when(first)
    def _():
        copies[1].wait()
        copies[2].wait()

    ff = wu.shape[1]
    count = ff // cut

    def up(j):
        cols = slice(j * cut, (j + 1) * cut)
        return dot(n2, wu[:, cols], NN) + bu[:, cols]

    ahead = up(0)
    total = None
    for j in range(count):
        hidden = ahead
        if j + 1 < count:
            ahead = up(j + 1)
        cols = slice(j * cut, (j + 1) * cut)
        act, slope = gelu_pair(hidden)
        act = act.astype(BF)
        act_o[:, cols] = act
        slope_o[:, cols] = slope.astype(BF)
        part = dot(act, wd[cols, :], NN)
        total = part if total is None else total + part
    next_o[...] = middle + (total + bd[...])


def forward_call(att, x, layer, wo, wu, wd, bo, g2, b2, bu, bd, tile):
    t, d = att.shape
    ff = wu.shape[2]
    tok = pl.BlockSpec((tile, d), lambda i: (i, 0))
    wide = pl.BlockSpec((tile, ff), lambda i: (i, 0))
    vec = pl.BlockSpec((None, 1, d), lambda i: (layer, 0, 0))
    vec_ff = pl.BlockSpec((None, 1, ff), lambda i: (layer, 0, 0))
    hbm = pl.BlockSpec(memory_space=pl.ANY)
    return pl.pallas_call(
        functools.partial(forward_kernel, layer=layer, cut=512),
        grid=(t // tile,),
        in_specs=[tok, tok, hbm, hbm, hbm, vec, vec, vec, vec_ff, vec],
        out_specs=[tok, tok, wide, wide, tok],
        out_shape=[
            jax.ShapeDtypeStruct((t, d), F32),
            jax.ShapeDtypeStruct((t, d), BF),
            jax.ShapeDtypeStruct((t, ff), BF),
            jax.ShapeDtypeStruct((t, ff), BF),
            jax.ShapeDtypeStruct((t, d), F32),
        ],
        scratch_shapes=[
            pltpu.VMEM((d, d), BF),
            pltpu.VMEM((d, ff), BF),
            pltpu.VMEM((ff, d), BF),
            pltpu.SemaphoreType.DMA((3,)),
        ],
        compiler_params=params(58),
        name="feed_forward",
    )(att, x, wo, wu, wd, bo, g2, b2, bu, bd)


def add_row(ref, at, value, first):
    ref[at : at + 1, :] = jnp.where(first, 0.0, ref[at : at + 1, :]) + value


def backward_kernel(
    g, slope, middle, wo_h, wu_h, wd_h, g2, dz_o, dh_o, dm_o, dy_o, da_o, sums, sums_ff, wo, wu, wd, sems, *, layer, cut
):
    first = pl.program_id(0) == 0
    copies = [
        pltpu.make_async_copy(src.at[layer], dst, sems.at[i])
        for i, (src, dst) in enumerate(((wd_h, wd), (wu_h, wu), (wo_h, wo)))
    ]

    @pl.when(first)
    def _():
        for copy in copies:
            copy.start()
        sums[...] = jnp.zeros_like(sums)
        sums_ff[...] = jnp.zeros_like(sums_ff)
        copies[0].wait()
        copies[1].wait()

    dz = g[...].astype(BF)
    dz_o[...] = dz
    sums[0:1, :] += column_sum(dz.astype(F32))
    ff = wu.shape[1]
    count = ff // cut

    def spread(j):
        return dot(dz, wd[j * cut : (j + 1) * cut, :], NT)

    ahead = spread(0)
    total = None
    for j in range(count):
        da = ahead
        if j + 1 < count:
            ahead = spread(j + 1)
        cols = slice(j * cut, (j + 1) * cut)
        dh = (da * slope[:, cols].astype(F32)).astype(BF)
        dh_o[:, cols] = dh
        sums_ff[0:1, cols] += column_sum(dh.astype(F32))
        part = dot(dh, wu[:, cols], NT)
        total = part if total is None else total + part
    unit, inverse = normalise(middle[...])
    sums[1:2, :] += column_sum(total * unit)
    sums[2:3, :] += column_sum(total)
    dm = g[...].astype(F32) + norm_back(total, g2[...], unit, inverse)
    dm_o[...] = dm
    dy = dm.astype(BF)
    dy_o[...] = dy
    sums[3:4, :] += column_sum(dy.astype(F32))

    @pl.when(first)
    def _():
        copies[2].wait()

    da_o[...] = dot(dy, wo[...], NT).astype(BF)


def backward_call(g, slope, middle, layer, wo, wu, wd, g2, tile):
    t, d = middle.shape
    ff = wu.shape[2]
    tok = pl.BlockSpec((tile, d), lambda i: (i, 0))
    wide = pl.BlockSpec((tile, ff), lambda i: (i, 0))
    vec = pl.BlockSpec((None, 1, d), lambda i: (layer, 0, 0))
    hbm = pl.BlockSpec(memory_space=pl.ANY)
    return pl.pallas_call(
        functools.partial(backward_kernel, layer=layer, cut=512),
        grid=(t // tile,),
        in_specs=[tok, wide, tok, hbm, hbm, hbm, vec],
        out_specs=[
            tok,
            wide,
            tok,
            tok,
            tok,
            pl.BlockSpec((8, d), lambda i: (0, 0)),
            pl.BlockSpec((8, ff), lambda i: (0, 0)),
        ],
        out_shape=[
            jax.ShapeDtypeStruct((t, d), BF),
            jax.ShapeDtypeStruct((t, ff), BF),
            jax.ShapeDtypeStruct((t, d), F32),
            jax.ShapeDtypeStruct((t, d), BF),
            jax.ShapeDtypeStruct((t, d), BF),
            jax.ShapeDtypeStruct((8, d), F32),
            jax.ShapeDtypeStruct((8, ff), F32),
        ],
        scratch_shapes=[
            pltpu.VMEM((d, d), BF),
            pltpu.VMEM((d, ff), BF),
            pltpu.VMEM((ff, d), BF),
            pltpu.SemaphoreType.DMA((3,)),
        ],
        compiler_params=params(58),
        name="feed_forward_back",
    )(g, slope, middle, wo, wu, wd, g2)


def joined_back_kernel(dq, dkv, dkv_in, x, dm, weight, gain, df_o, g_o, sums):
    d = dq.shape[-1]

    @pl.when(pl.program_id(0) == 0)
    def _():
        sums[...] = jnp.zeros_like(sums)

    parts = [dq[...]]
    for i in range(2):
        parts.append((dkv[i].astype(F32) + dkv_in[i].astype(F32)).astype(BF))
    total = None
    for i, part in enumerate(parts):
        cols = slice(i * d, (i + 1) * d)
        df_o[:, cols] = part
        piece = dot(part, weight[:, cols], NT)
        total = piece if total is None else total + piece
    sums[2:3, :] += column_sum(parts[0].astype(F32))
    sums[3:4, :] += column_sum(parts[2].astype(F32))
    unit, inverse = normalise(x[...].astype(F32))
    sums[0:1, :] += column_sum(total * unit)
    sums[1:2, :] += column_sum(total)
    g_o[...] = dm[...] + norm_back(total, gain[...], unit, inverse)


def joined_back_call(dq, dkv, dkv_in, x, dm, layer, weight, gain, tile):
    t, d = dq.shape
    tok = pl.BlockSpec((tile, d), lambda i: (i, 0))
    both = pl.BlockSpec((2, tile, d), lambda i: (0, i, 0))
    return pl.pallas_call(
        joined_back_kernel,
        grid=(t // tile,),
        in_specs=[
            tok,
            both,
            both,
            tok,
            tok,
            pl.BlockSpec((None, d, 3 * d), lambda i: (layer, 0, 0)),
            pl.BlockSpec((None, 1, d), lambda i: (layer, 0, 0)),
        ],
        out_specs=[
            pl.BlockSpec((tile, 3 * d), lambda i: (i, 0)),
            tok,
            pl.BlockSpec((8, d), lambda i: (0, 0)),
        ],
        out_shape=[
            jax.ShapeDtypeStruct((t, 3 * d), BF),
            jax.ShapeDtypeStruct((t, d), F32),
            jax.ShapeDtypeStruct((8, d), F32),
        ],
        compiler_params=params(56),
        name="joined_back",
    )(dq, dkv, dkv_in, x, dm, weight, gain)


def weight_grad_kernel(core, a, b, keep, send, turned, *, rows, fixed_a):
    def turn():
        turned[...] = a[...].astype(F32).T.astype(BF)

    if fixed_a:
        pl.when(pl.program_id(0) == 0)(turn)
    else:
        turn()
    out = dot(turned[...], b[...], NN)
    n, cols = out.shape
    even = jnp.concatenate([out[i : i + rows] for i in range(0, n, 2 * rows)], axis=0).astype(BF)
    odd = jnp.concatenate([out[i + rows : i + 2 * rows] for i in range(0, n, 2 * rows)], axis=0).astype(BF)

    @pl.when(core[0] == 0)
    def _():
        keep[...] = even
        send[...] = odd

    @pl.when(core[0] == 1)
    def _():
        keep[...] = odd
        send[...] = even


def weight_grad_call(core, a, b, chunks, block):
    t, n = a.shape
    cols = b.shape[1]
    fixed_a = n == block
    steps = cols // block if fixed_a else n // block
    half = block // 2
    if fixed_a:
        a_at, b_at, o_at = (lambda i: (0, 0)), (lambda i: (0, i)), (lambda i: (0, i))
    else:
        a_at, b_at, o_at = (lambda i: (0, i)), (lambda i: (0, 0)), (lambda i: (i, 0))
    shape = jax.ShapeDtypeStruct((n // 2, cols), BF)
    keep, send = pl.pallas_call(
        functools.partial(weight_grad_kernel, rows=n // chunks, fixed_a=fixed_a),
        grid=(steps,),
        in_specs=[
            pl.BlockSpec(memory_space=pltpu.SMEM),
            pl.BlockSpec((t, block), a_at),
            pl.BlockSpec((t, block), b_at),
        ],
        out_specs=[pl.BlockSpec((half, block), o_at)] * 2,
        out_shape=[shape, shape],
        scratch_shapes=[pltpu.VMEM((block, t), BF)],
        compiler_params=params(56),
        name="weight_grad",
    )(core, a, b)
    split = (chunks // 2, n // chunks, cols)
    return keep.reshape(split), send.reshape(split)


def flip(device_count, bit):
    return [(i, i ^ (1 << bit)) for i in range(device_count)]


class Reducer:
    def __init__(self, device_count, index):
        self.count, self.index = device_count, index
        self.bits = device_count.bit_length() - 1

    def swap(self, array, bit):
        return lax.ppermute(array, ("dp", "seq"), flip(self.count, bit))

    def begin(self, keep, send):
        return [keep, self.swap(send, 0)], list(range(self.bits - 1, 0, -1))

    def half(self, terms, bits, bit, which):
        at = bits.index(bit)
        out = []
        for term in terms:
            n = term.shape[0]
            lo = 1 << (len(bits) - 1 - at)
            view = term.reshape(n // (2 * lo), 2, lo, *term.shape[1:])
            out.append(lax.dynamic_index_in_dim(view, which, 1, keepdims=False).reshape(n // 2, *term.shape[1:]))
        return out

    def run(self, terms, bits, order, dtype):
        for bit in order:
            mine = (self.index >> bit) & 1
            total = sum(t.astype(F32) for t in self.half(terms, bits, bit, 1 - mine)).astype(dtype)
            kept = self.half(terms, bits, bit, mine)
            terms = [sum(t.astype(F32) for t in kept).astype(dtype), self.swap(total, bit)]
            bits = [b for b in bits if b != bit]
        return sum(t.astype(F32) for t in terms)[0]

    def small(self, rows):
        flat = jnp.concatenate([r.reshape(self.count, -1) for r in rows], axis=1)[:, None, :]
        width = flat.shape[2]
        pad = -width % 128
        flat = jnp.pad(flat, ((0, 0), (0, 0), (0, pad)))
        bits = list(range(self.bits - 1, -1, -1))
        return self.run([flat], bits, list(range(self.bits)), F32)[0, :width]


def on_device(
    device_count,
    cell_tokens,
    first_gain,
    first_bias,
    joined_weight,
    query_value_bias,
    output_weight,
    output_bias,
    second_gain,
    second_bias,
    up_weight,
    up_bias,
    down_weight,
    down_bias,
    cotangent,
    gene_mask,
):
    _, genes, d = cell_tokens.shape
    layers = joined_weight.shape[0]
    seq = lax.axis_index("seq")
    index = lax.axis_index("dp") * 4 + seq
    chip, core = seq // 2, seq % 2
    core_ref = core.astype(jnp.int32).reshape(1)
    across = [(0, 2), (1, 3), (2, 0), (3, 1)]
    beside = [(0, 1), (1, 0), (2, 3), (3, 2)]
    tile = genes
    reducer = Reducer(device_count, index)

    def rows(v):
        return v[:, None, :]

    def trade(pair):
        mine = lax.dynamic_index_in_dim(pair, chip, 0, keepdims=False)
        other = lax.dynamic_index_in_dim(pair, 1 - chip, 0, keepdims=False)
        return jnp.concatenate([mine, lax.ppermute(other, "seq", across)], axis=0)

    def trade_back(held):
        own = held[:genes]
        got = lax.ppermute(held[genes:].astype(BF), "seq", across).astype(F32)
        return jnp.where(chip == 0, jnp.stack([own, got]), jnp.stack([got, own]))

    g1, b1 = rows(first_gain), rows(first_bias)
    g2, b2 = rows(second_gain), rows(second_bias)
    bo, bu, bd = rows(output_bias), rows(up_bias), rows(down_bias)
    qkv_bias = rows(
        jnp.concatenate(
            [query_value_bias[:, :d], jnp.zeros((layers, d), F32), query_value_bias[:, d:]], axis=1
        )
    )

    x = trade(cell_tokens)
    seeded = cotangent * gene_mask.astype(BF)[:, :, None]
    g = trade(seeded)

    saved = []
    for layer in range(layers):
        normed, q, kv = first_call(x, layer, g1, b1, joined_weight, qkv_bias, tile)
        kvo = lax.ppermute(kv, "seq", beside)
        att, lse = attend_call(q, kv, kvo)
        middle, n2, act, slope, following = forward_call(
            att, x, layer, output_weight, up_weight, down_weight, bo, g2, b2, bu, bd, tile
        )
        saved.append((x, normed, q, kv, kvo, att, lse, middle, n2, act, slope))
        x = following
    block_output = trade_back(x)

    chunks = device_count
    grads = [None] * layers
    vectors = [None] * layers
    dp_bits = list(range(2, reducer.bits))
    for layer in reversed(range(layers)):
        x, normed, q, kv, kvo, att, lse, middle, n2, act, slope = saved[layer]
        dz, dh, dm, dy, da, sums, sums_ff = backward_call(
            g, slope, middle, layer, output_weight, up_weight, down_weight, g2, tile
        )
        w_down = reducer.begin(*weight_grad_call(core_ref, act, dz, chunks, d))
        w_up = reducer.begin(*weight_grad_call(core_ref, n2, dh, chunks, d))
        w_out = reducer.begin(*weight_grad_call(core_ref, att, dy, chunks, d))
        dq, dkv, dkvo = attend_back_call(q, kv, kvo, da, att, lse)
        dkv_in = lax.ppermute(dkvo, "seq", beside)
        df, g, sums_in = joined_back_call(dq, dkv, dkv_in, x, dm, layer, joined_weight, g1, tile)
        w_joined = reducer.begin(*weight_grad_call(core_ref, normed, df, chunks, d))
        grads[layer] = [
            reducer.run(*w_joined, dp_bits + [1], BF),
            reducer.run(*w_out, dp_bits + [1], BF),
            reducer.run(*w_up, [1] + dp_bits, BF),
            reducer.run(*w_down, dp_bits + [1], BF),
        ]
        vectors[layer] = [
            sums_in[0],
            sums_in[1],
            sums_in[2],
            sums_in[3],
            sums[3],
            sums[1],
            sums[2],
            sums_ff[0],
            sums[0],
        ]
    input_gradient = trade_back(g)

    qv = [jnp.concatenate([v[2], v[3]]) for v in vectors]
    plain = [0, 1, 4, 5, 6, 8]
    rows_out = [vectors[l][i] for l in range(layers) for i in plain]
    rows_out += qv + [v[7] for v in vectors]
    summed = reducer.small(rows_out)
    piece = d // device_count
    at = 0
    small = {}
    for l in range(layers):
        for i in plain:
            small[l, i] = summed[at : at + piece]
            at += piece
    for key, width in (("qv", 2 * piece), ("up", up_bias.shape[1] // device_count)):
        for l in range(layers):
            small[l, key] = summed[at : at + width]
            at += width

    def vec(key):
        return jnp.stack([small[l, key] for l in range(layers)])

    def mat(i):
        return jnp.stack([grads[l][i] for l in range(layers)])

    return (
        block_output,
        input_gradient,
        vec(0),
        vec(1),
        mat(0),
        vec("qv"),
        mat(1),
        vec(4),
        vec(5),
        vec(6),
        mat(2),
        vec("up"),
        mat(3),
        vec(8),
    )


def solution(mesh):
    split = P(None, ("dp", "seq"))
    split_rows = P(None, ("dp", "seq"), None)
    tokens = P("dp", "seq", None)
    return jax.shard_map(
        functools.partial(on_device, mesh.size),
        mesh=mesh,
        in_specs=(tokens,) + (P(),) * 12 + (tokens, P("dp", "seq")),
        out_specs=(
            tokens,
            tokens,
            split,
            split,
            split_rows,
            split,
            split_rows,
            split,
            split,
            split,
            split_rows,
            split,
            split_rows,
            split,
        ),
        check_vma=False,
    )
```

time: 2600 us -> 719 us (0.28)
  matrix products: 808 us -> 0 us
  waiting for transfers between devices: 881 us -> 194 us
  Pallas kernels: 0 us -> 396 us
  local copies, waits for them, and re-layouts: 403 us -> 30 us
  other arithmetic: 256 us -> 38.9 us
  blocking collectives: 101 us -> 0 us
  loops' own time: 93.2 us -> 0 us
    dot_general x136 -> x0, matrix products: 808 us -> none  [the longest x16 137 us: one_one_block(): jnp.einsum('hqk,qhd->khd', weights.astype(jnp.bfloat16), upstream_block,...]
    reduce_scatter x4 -> x0, waiting for transfers between devices: 655 us -> none  [the longest x1 212 us: on_device(): lax.psum_scatter(up_all, ('dp', 'seq'), scatter_dimension=1, tiled=True)]
    pallas_call x0 -> x20, Pallas kernels: none -> 396 us  [the longest x2 130 us: attend_back_call(): pl.pallas_call(functools.partial(attend_back_kernel, chunk=min(256, t)),...]
    all_to_all x7 -> x0, waiting for transfers between devices: 225 us -> none  [the longest x2 108 us: on_device(): lax.all_to_all(joined_rows, 'seq', split_axis=3, concat_axis=1, tiled=True)]
    ppermute x0 -> x53, waiting for transfers between devices: none -> 194 us  [the longest x45 157 us: swap(): return lax.ppermute(array, ('dp', 'seq'), flip(self.count, bit))]
    convert_element_type x19 -> x30, other arithmetic: 139 us -> 21.6 us  [the longest x19 21.2 us: run(): sum((t.astype(F32) for t in kept)).astype(dtype)]
    all_to_all x16 -> x0, local copies, waits for them, and re-layouts: 115 us -> none  [the longest x4 54.7 us: on_device(): lax.all_to_all(head_delta, 'seq', split_axis=1, concat_axis=3, tiled=True)]
    another operation x8 -> x0, loops' own time: 93.2 us -> none  [the longest x4 42.6 us: one_cell(): lax.scan(one_one_block, (zero_delta, zero_delta), jnp.arange(blocks_cell))]
  transfers between devices with their start and end apart: 13 -> 53, of which waited for: 11 -> 23; matrix products, arithmetic and copies ran while one was open for 7% -> 9% of each run, Pallas kernels for 0% -> 25%
where the time goes in v1:
time: 719 us; the launch traced here: 709 us
  Pallas kernels  396 us (55%)
  waiting for transfers between devices  194 us (27%)
  starting transfers between devices  49 us (7%)
  other arithmetic  38.9 us (5%)
  local copies, waits for them, and re-layouts  30 us (4%)
    ppermute x45, waiting for transfers between devices, swap(): return lax.ppermute(array, ('dp', 'seq'), flip(self.count, bit))  157 us
    pallas_call x2, Pallas kernels, attend_back_call(): pl.pallas_call(functools.partial(attend_back_kernel, chunk=min(256, t)),...  130 us
    pallas_call x8, Pallas kernels, weight_grad_call(): pl.pallas_call(functools.partial(weight_grad_kernel, rows=n // chunks, fi...  65.3 us
    pallas_call x2, Pallas kernels, attend_call(): pl.pallas_call(functools.partial(attend_kernel, chunk=min(256, t)), grid=...  59.1 us
    pallas_call x2, Pallas kernels, forward_call(): pl.pallas_call(functools.partial(forward_kernel, layer=layer, cut=512), g...  55.9 us
    pallas_call x2, Pallas kernels, backward_call(): pl.pallas_call(functools.partial(backward_kernel, layer=layer, cut=512),...  47 us
    ppermute x45, starting transfers between devices, swap(): return lax.ppermute(array, ('dp', 'seq'), flip(self.count, bit))  41 us
    ppermute x2, waiting for transfers between devices, trade(): return jnp.concatenate([mine, lax.ppermute(other, 'seq', across)], axis=0)  33.7 us
  transfers between devices with their start and end apart: 53, of which 23 were waited for; matrix products, arithmetic and copies ran while one was open for 9% of the time, Pallas kernels for 25%

profile of v1, /device:TPU:0, one launch (start us, length us, event | category | flops | bytes accessed | tf_op | source)
XLA Modules:
  0.0 709.4 jit_solution(11942438720092149357)
XLA Ops:
  2.2 3.0 collective-permute-start
  7.1 15.7 %collective-permute-done = bf16[512,768]{1,0:T(8,128)(2,1)S(1)} collective-permute-done((bf16[512,768]{1,0:T(8,128)(2,1)S(1)}, bf16[512,768]{1,0:T(8,128)(2,1)S(1)}, u32[]{:S(2)}, u32[]{:S(2)}) %collective-permute-start) | collective-permute-done | bytes 786464 | tf_op jit(solution)/shard_map/ppermute | solution.py:595
  24.0 8.3 %norm_qkv.2 = (bf16[1024,768]{1,0:T(8,128)(2,1)}, bf16[1024,768]{1,0:T(8,128)(2,1)}, bf16[2,1024,768]{2,1,0:T(8,128)(2,1)}) custom-call(bf16[1024,768]{1,0:T(8,128)(2,1)} %pad_maximum_fusion.x, f32[2,1,768]{2,1,0:T(1,128)} %broadcast_in_dim.31.gain, f32[2,1,768]{2,1,0:T(1,128)} %broadcast_in_dim.32.bias, bf16[2,768,2304]{2,1,0:T(8,128)(2,1)} %weight.7, ...), custom_call_target="tpu_custom_call" | custom-call | tf_op jit(solution)/shard_map/norm_qkv/pallas_call | solution.py:84
  35.3 2.8 collective-permute-done.1.kvo
  39.8 29.5 %attend.2 = (bf16[1024,768]{1,0:T(8,128)(2,1)}, f32[6,8,1024]{2,1,0:T(8,128)}) custom-call(bf16[1024,768]{1,0:T(8,128)(2,1)} %get-tuple-element.76.q, bf16[2,1024,768]{2,1,0:T(8,128)(2,1)} %get-tuple-element.77.kv, bf16[2,1024,768]{2,1,0:T(8,128)(2,1)} %copy-done), custom_call_target="tpu_custom_call" | custom-call | tf_op jit(solution)/shard_map/attend/pallas_call | solution.py:162
  69.3 27.8 %feed_forward.2 = (f32[1024,768]{1,0:T(8,128)}, bf16[1024,768]{1,0:T(8,128)(2,1)}, bf16[1024,3072]{1,0:T(8,128)(2,1)}, bf16[1024,3072]{1,0:T(8,128)(2,1)}, f32[1024,768]{1,0:T(8,128)}) custom-call(bf16[1024,768]{1,0:T(8,128)(2,1)} %get-tuple-element.78.att.out.a, bf16[1024,768]{1,0:T(8,128)(2,1)} %pad_maximum_fusion.x, bf16[2,768,768]{2,1,0:T(8,128)(2,1)} %wo_h.7, ...), custom_call_target="tpu_custom_call" | custom-call | tf_op jit(solution)/shard_map/feed_forward/pallas_call | solution.py:287
  97.1 8.9 %norm_qkv.3 = (bf16[1024,768]{1,0:T(8,128)(2,1)}, bf16[1024,768]{1,0:T(8,128)(2,1)}, bf16[2,1024,768]{2,1,0:T(8,128)(2,1)}) custom-call(f32[1024,768]{1,0:T(8,128)} %get-tuple-element.79.x, f32[2,1,768]{2,1,0:T(1,128)} %broadcast_in_dim.31.gain, f32[2,1,768]{2,1,0:T(1,128)} %broadcast_in_dim.32.bias, bf16[2,768,2304]{2,1,0:T(8,128)(2,1)} %weight.7, ...), custom_call_target="tpu_custom_call" | custom-call | tf_op jit(solution)/shard_map/norm_qkv/pallas_call | solution.py:84
  108.5 18.1 %collective-permute-done.4 = bf16[512,768]{1,0:T(8,128)(2,1)S(1)} collective-permute-done((bf16[512,768]{1,0:T(8,128)(2,1)S(1)}, bf16[512,768]{1,0:T(8,128)(2,1)S(1)}, u32[]{:S(2)}, u32[]{:S(2)}) %collective-permute-start.4) | collective-permute-done | bytes 786464 | tf_op jit(solution)/shard_map/ppermute | solution.py:595
  129.5 29.6 %attend.3 = (bf16[1024,768]{1,0:T(8,128)(2,1)}, f32[6,8,1024]{2,1,0:T(8,128)}) custom-call(bf16[1024,768]{1,0:T(8,128)(2,1)} %get-tuple-element.80.q, bf16[2,1024,768]{2,1,0:T(8,128)(2,1)} %get-tuple-element.81.kv, bf16[2,1024,768]{2,1,0:T(8,128)(2,1)} %copy-done.1), custom_call_target="tpu_custom_call" | custom-call | tf_op jit(solution)/shard_map/attend/pallas_call | solution.py:162
  159.0 28.1 %feed_forward.3 = (f32[1024,768]{1,0:T(8,128)}, bf16[1024,768]{1,0:T(8,128)(2,1)}, bf16[1024,3072]{1,0:T(8,128)(2,1)}, bf16[1024,3072]{1,0:T(8,128)(2,1)}, f32[1024,768]{1,0:T(8,128)}) custom-call(bf16[1024,768]{1,0:T(8,128)(2,1)} %get-tuple-element.82.att.out.a, f32[1024,768]{1,0:T(8,128)} %get-tuple-element.79.x, bf16[2,768,768]{2,1,0:T(8,128)(2,1)} %wo_h.7, ...), custom_call_target="tpu_custom_call" | custom-call | tf_op jit(solution)/shard_map/feed_forward/pallas_call | solution.py:287
  187.2 23.2 %feed_forward_back.2 = (bf16[1024,768]{1,0:T(8,128)(2,1)}, bf16[1024,3072]{1,0:T(8,128)(2,1)}, f32[1024,768]{1,0:T(8,128)}, bf16[1024,768]{1,0:T(8,128)(2,1)}, b...) custom-call(bf16[1024,768]{1,0:T(8,128)(2,1)} %pad_maximum_fusion.1.g, ...), custom_call_target="tpu_custom_call" | custom-call | tf_op jit(solution)/shard_map/feed_forward_back/pallas_call | solution.py:376
  210.4 65.1 %attend_back.2 = (bf16[1024,768]{1,0:T(8,128)(2,1)}, bf16[2,1024,768]{2,1,0:T(8,128)(2,1)}, bf16[2,1024,768]{2,1,0:T(8,128)(2,1)}) custom-call(bf16[1024,768]{1,0:T(8,128)(2,1)} %get-tuple-element.80.q, bf16[2,1024,768]{2,1,0:T(8,128)(2,1)} %get-tuple-element.81.kv, bf16[2,1024,768]{2,1,0:T(8,128)(2,1)} %copy-done.1, ...), custom_call_target="tpu_custom_call" | custom-call | tf_op jit(solution)/shard_map/attend_back/pallas_call | solution.py:215
  275.6 10.2 %weight_grad.13 = (bf16[384,3072]{1,0:T(8,128)(2,1)}, bf16[384,3072]{1,0:T(8,128)(2,1)}) custom-call(s32[1]{0:T(128)} %bitcast.26.core, bf16[1024,768]{1,0:T(8,128)(2,1)} %get-tuple-element.126.a, bf16[1024,3072]{1,0:T(8,128)(2,1)} %get-tuple-element.127.b), custom_call_target="tpu_custom_call" | custom-call | tf_op jit(solution)/shard_map/weight_grad/pallas_call | solution.py:499
  286.3 2.4 slice.236
  291.4 3.6 add_convert_fusion.5
  299.5 9.5 %weight_grad.15 = (bf16[1536,768]{1,0:T(8,128)(2,1)}, bf16[1536,768]{1,0:T(8,128)(2,1)}) custom-call(s32[1]{0:T(128)} %bitcast.26.core, bf16[1024,3072]{1,0:T(8,128)(2,1)} %get-tuple-element.134.a, bf16[1024,768]{1,0:T(8,128)(2,1)} %get-tuple-element.135.b), custom_call_target="tpu_custom_call" | custom-call | tf_op jit(solution)/shard_map/weight_grad/pallas_call | solution.py:499
  309.1 4.4 weight_grad.11
  315.5 10.7 %joined_back.2 = (bf16[1024,2304]{1,0:T(8,128)(2,1)}, f32[1024,768]{1,0:T(8,128)}, f32[8,768]{1,0:T(8,128)}) custom-call(bf16[1024,768]{1,0:T(8,128)(2,1)} %get-tuple-element.88.dq, bf16[2,1024,768]{2,1,0:T(8,128)(2,1)} %get-tuple-element.89.dkv, bf16[2,1024,768]{2,1,0:T(8,128)(2,1)} %collective-permute-done.5.dkv_in, f32[1024,768]{1,0:T(8,128)} %get-tuple-element.79.x, ...), custom_call_target="tpu_custom_call" | custom-call | tf_op jit(solution)/shard_map/joined_back/pallas_call | solution.py:437
  326.2 23.7 %feed_forward_back.3 = (bf16[1024,768]{1,0:T(8,128)(2,1)}, bf16[1024,3072]{1,0:T(8,128)(2,1)}, f32[1024,768]{1,0:T(8,128)}, bf16[1024,768]{1,0:T(8,128)(2,1)}, b...) custom-call(f32[1024,768]{1,0:T(8,128)} %get-tuple-element.92.g, ...), custom_call_target="tpu_custom_call" | custom-call | tf_op jit(solution)/shard_map/feed_forward_back/pallas_call | solution.py:376
  349.9 64.9 %attend_back.3 = (bf16[1024,768]{1,0:T(8,128)(2,1)}, bf16[2,1024,768]{2,1,0:T(8,128)(2,1)}, bf16[2,1024,768]{2,1,0:T(8,128)(2,1)}) custom-call(bf16[1024,768]{1,0:T(8,128)(2,1)} %get-tuple-element.76.q, bf16[2,1024,768]{2,1,0:T(8,128)(2,1)} %get-tuple-element.77.kv, bf16[2,1024,768]{2,1,0:T(8,128)(2,1)} %copy-done, bf16[1024,768]{1,0:T(8,128)(2,1)} %get-tuple-element.95.up, ...), custom_call_target="tpu_custom_call" | custom-call | tf_op jit(solution)/shard_map/attend_back/pallas_call | solution.py:215
  414.9 4.9 weight_grad.10
  429.4 5.8 collective-permute-done.24
  437.0 4.6 collective-permute-done.29
  449.5 9.6 %weight_grad.14 = (bf16[1536,768]{1,0:T(8,128)(2,1)}, bf16[1536,768]{1,0:T(8,128)(2,1)}) custom-call(s32[1]{0:T(128)} %bitcast.26.core, bf16[1024,3072]{1,0:T(8,128)(2,1)} %get-tuple-element.130.a, bf16[1024,768]{1,0:T(8,128)(2,1)} %get-tuple-element.131.b), custom_call_target="tpu_custom_call" | custom-call | tf_op jit(solution)/shard_map/weight_grad/pallas_call | solution.py:499
  459.1 10.0 %weight_grad.12 = (bf16[384,3072]{1,0:T(8,128)(2,1)}, bf16[384,3072]{1,0:T(8,128)(2,1)}) custom-call(s32[1]{0:T(128)} %bitcast.26.core, bf16[1024,768]{1,0:T(8,128)(2,1)} %get-tuple-element.122.a, bf16[1024,3072]{1,0:T(8,128)(2,1)} %get-tuple-element.123.b), custom_call_target="tpu_custom_call" | custom-call | tf_op jit(solution)/shard_map/weight_grad/pallas_call | solution.py:499
  469.1 8.3 %weight_grad.9 = (bf16[384,2304]{1,0:T(8,128)(2,1)}, bf16[384,2304]{1,0:T(8,128)(2,1)}) custom-call(s32[1]{0:T(128)} %bitcast.26.core, bf16[1024,768]{1,0:T(8,128)(2,1)} %get-tuple-element.112.a, bf16[1024,2304]{1,0:T(8,128)(2,1)} %get-tuple-element.113.b), custom_call_target="tpu_custom_call" | custom-call | tf_op jit(solution)/shard_map/weight_grad/pallas_call | solution.py:499
  477.5 2.7 collective-permute-start.26
  480.2 4.4 collective-permute-done.26
  485.9 5.1 collective-permute-done.31
  496.1 8.4 %collective-permute-done.41 = bf16[2,24,3072]{2,1,0:T(8,128)(2,1)S(1)} collective-permute-done((bf16[2,24,3072]{2,1,0:T(8,128)(2,1)S(1)}, bf16[2,24,3072]{2,1,0:T(8,128)(2,1)S(1)}, u32[]{:S(2)}, u32[]{:S(2)}) %collective-permute-start.41) | collective-permute-done | bytes 294944 | tf_op jit(solution)/shard_map/ppermute | solution.py:527
  505.4 10.8 %joined_back.3 = (bf16[1024,2304]{1,0:T(8,128)(2,1)}, f32[1024,768]{1,0:T(8,128)}, f32[8,768]{1,0:T(8,128)}) custom-call(bf16[1024,768]{1,0:T(8,128)(2,1)} %get-tuple-element.97.dq, bf16[2,1024,768]{2,1,0:T(8,128)(2,1)} %get-tuple-element.98.dkv, bf16[2,1024,768]{2,1,0:T(8,128)(2,1)} %collective-permute-done.6.dkv_in, bf16[1024,768]{1,0:T(8,128)(2,1)} %pad_maximum_fusion.x, ...), custom_call_target="tpu_custom_call" | custom-call | tf_op jit(solution)/shard_map/joined_back/pallas_call | solution.py:437
  527.5 5.9 add_convert_fusion.1
  537.2 3.8 add_convert_fusion.7
  543.0 8.3 %weight_grad.8 = (bf16[384,2304]{1,0:T(8,128)(2,1)}, bf16[384,2304]{1,0:T(8,128)(2,1)}) custom-call(s32[1]{0:T(128)} %bitcast.26.core, bf16[1024,768]{1,0:T(8,128)(2,1)} %get-tuple-element.108.a, bf16[1024,2304]{1,0:T(8,128)(2,1)} %get-tuple-element.109.b), custom_call_target="tpu_custom_call" | custom-call | tf_op jit(solution)/shard_map/weight_grad/pallas_call | solution.py:499
  556.5 6.1 collective-permute-done.44
  564.1 21.5 %collective-permute-done.49 = bf16[8,96,768]{2,1,0:T(8,128)(2,1)S(1)} collective-permute-done((bf16[8,96,768]{2,1,0:T(8,128)(2,1)S(1)}, bf16[8,96,768]{2,1,0:T(8,128)(2,1)S(1)}, u32[]{:S(2)}, u32[]{:S(2)}) %collective-permute-start.49) | collective-permute-done | bytes 1179680 | tf_op jit(solution)/shard_map/ppermute | solution.py:527
  591.0 14.1 %collective-permute-done.45 = bf16[4,96,768]{2,1,0:T(8,128)(2,1)S(1)} collective-permute-done((bf16[4,96,768]{2,1,0:T(8,128)(2,1)S(1)}, bf16[4,96,768]{2,1,0:T(8,128)(2,1)S(1)}, u32[]{:S(2)}, u32[]{:S(2)}) %collective-permute-start.45) | collective-permute-done | bytes 589856 | tf_op jit(solution)/shard_map/ppermute | solution.py:527
  605.3 12.9 %collective-permute-done.50 = bf16[4,96,768]{2,1,0:T(8,128)(2,1)S(1)} collective-permute-done((bf16[4,96,768]{2,1,0:T(8,128)(2,1)S(1)}, bf16[4,96,768]{2,1,0:T(8,128)(2,1)S(1)}, u32[]{:S(2)}, u32[]{:S(2)}) %collective-permute-start.50) | collective-permute-done | bytes 589856 | tf_op jit(solution)/shard_map/ppermute | solution.py:527
  618.6 2.5 collective-permute-start.36
  624.1 8.0 %collective-permute-done.51 = bf16[2,96,768]{2,1,0:T(8,128)(2,1)S(1)} collective-permute-done((bf16[2,96,768]{2,1,0:T(8,128)(2,1)S(1)}, bf16[2,96,768]{2,1,0:T(8,128)(2,1)S(1)}, u32[]{:S(2)}, u32[]{:S(2)}) %collective-permute-start.51) | collective-permute-done | bytes 294944 | tf_op jit(solution)/shard_map/ppermute | solution.py:527
  633.4 2.4 add_convert_fusion.9
  636.4 5.8 collective-permute-done.37
  643.8 14.6 %collective-permute-done.14 = bf16[8,24,2304]{2,1,0:T(8,128)(2,1)S(1)} collective-permute-done((bf16[8,24,2304]{2,1,0:T(8,128)(2,1)S(1)}, bf16[8,24,2304]{2,1,0:T(8,128)(2,1)S(1)}, u32[]{:S(2)}, u32[]{:S(2)}) %collective-permute-start.14) | collective-permute-done | bytes 884768 | tf_op jit(solution)/shard_map/ppermute | solution.py:527
  658.7 2.6 collective-permute-start.15
  661.3 14.9 %collective-permute-done.19 = bf16[8,24,2304]{2,1,0:T(8,128)(2,1)S(1)} collective-permute-done((bf16[8,24,2304]{2,1,0:T(8,128)(2,1)S(1)}, bf16[8,24,2304]{2,1,0:T(8,128)(2,1)S(1)}, u32[]{:S(2)}, u32[]{:S(2)}) %collective-permute-start.19) | collective-permute-done | bytes 884768 | tf_op jit(solution)/shard_map/ppermute | solution.py:527
  680.1 12.2 %collective-permute-done.20 = bf16[4,24,2304]{2,1,0:T(8,128)(2,1)S(1)} collective-permute-done((bf16[4,24,2304]{2,1,0:T(8,128)(2,1)S(1)}, bf16[4,24,2304]{2,1,0:T(8,128)(2,1)S(1)}, u32[]{:S(2)}, u32[]{:S(2)}) %collective-permute-start.20) | collective-permute-done | bytes 442400 | tf_op jit(solution)/shard_map/ppermute | solution.py:527
  693.6 9.7 %collective-permute-done.21 = bf16[2,24,2304]{2,1,0:T(8,128)(2,1)S(1)} collective-permute-done((bf16[2,24,2304]{2,1,0:T(8,128)(2,1)S(1)}, bf16[2,24,2304]{2,1,0:T(8,128)(2,1)S(1)}, u32[]{:S(2)}, u32[]{:S(2)}) %collective-permute-start.21) | collective-permute-done | bytes 221216 | tf_op jit(solution)/shard_map/ppermute | solution.py:527
  704.5 3.9 collective-permute-done.22
  (256 shorter events, 94.4 us)
Async XLA Ops:
  2.2 20.5 %collective-permute-start = (bf16[512,768]{1,0:T(8,128)(2,1)S(1)}, bf16[512,768]{1,0:T(8,128)(2,1)S(1)}, u32[]{:S(2)}, u32[]{:S(2)}) collective-permute-start(bf16[512,768]{1,0:T(8,128)(2,1)S(1)} %get-tuple-element.181), channel_id=1, source_target_pairs={{0,2},{1,3},{2,0},{3,1},{4,6},{5,7},{6,4},{7,5},{8,10},{9,11},{10,... | collective-permute-start | bytes 2359304 | tf_op jit(solution)/shard_map/ppermute | solution.py:595
  32.3 5.9 collective-permute-start.1
  106.1 21.7 %collective-permute-start.2 = (bf16[2,1024,768]{2,1,0:T(8,128)(2,1)}, bf16[2,1024,768]{2,1,0:T(8,128)(2,1)S(1)}, u32[]{:S(2)}, u32[]{:S(2)}) collective-permute-start(bf16[2,1024,768]{2,1,0:T(8,128)(2,1)} %get-tuple-element.81.kv), channel_id=1, source_target_pairs={{0,1},{1,0},{2,3},{3,2},{4,5},{5,4},{6,7},{7,6},{8,9},{9,8},{10,11... | collective-permute-start | bytes 9437192 | tf_op jit(solution)/shard_map/ppermute | solution.py:618
  106.6 19.9 %collective-permute-start.4 = (bf16[512,768]{1,0:T(8,128)(2,1)S(1)}, bf16[512,768]{1,0:T(8,128)(2,1)S(1)}, u32[]{:S(2)}, u32[]{:S(2)}) collective-permute-start(bf16[512,768]{1,0:T(8,128)(2,1)S(1)} %get-tuple-element.179), channel_id=1, source_target_pairs={{0,2},{1,3},{2,0},{3,1},{4,6},{5,7},{6,4},{7,5},{8,10},{9,11},{10,... | collective-permute-start | bytes 2359304 | tf_op jit(solution)/shard_map/ppermute | solution.py:595
  275.5 40.0 %collective-permute-start.5 = (bf16[2,1024,768]{2,1,0:T(8,128)(2,1)}, bf16[2,1024,768]{2,1,0:T(8,128)(2,1)}, u32[]{:S(2)}, u32[]{:S(2)}) collective-permute-start(bf16[2,1024,768]{2,1,0:T(8,128)(2,1)} %get-tuple-element.90), channel_id=1, source_target_pairs={{0,1},{1,0},{2,3},{3,2},{4,5},{5,4},{6,7},{7,6},{8,9},{9,8},{10,11... | collective-permute-start | bytes 9437192 | tf_op jit(solution)/shard_map/ppermute | solution.py:640
  285.8 5.6 collective-permute-start.38
  288.7 131.0 %collective-permute-start.3 = (bf16[512,768]{1,0:T(8,128)(2,1)}, bf16[512,768]{1,0:T(8,128)(2,1)}, u32[]{:S(2)}, u32[]{:S(2)}) collective-permute-start(bf16[512,768]{1,0:T(8,128)(2,1)} %slice.236), channel_id=1, source_target_pairs={{0,2},{1,3},{2,0},{3,1},{4,6},{5,7},{6,4},{7,5},{8,10},{9,11},{10,... | collective-permute-start | bytes 2359304 | tf_op jit(solution)/shard_map/ppermute | solution.py:599
  295.0 132.4 %collective-permute-start.39 = (bf16[8,24,3072]{2,1,0:T(8,128)(2,1)}, bf16[8,24,3072]{2,1,0:T(8,128)(2,1)S(1)}, u32[]{:S(2)}, u32[]{:S(2)}) collective-permute-start(bf16[8,24,3072]{2,1,0:T(8,128)(2,1)} %get-tuple-element.161), channel_id=1, source_target_pairs={{0,2},{1,3},{2,0},{3,1},{4,6},{5,7},{6,4},{7,5},{8,10},{9,11},{10,... | collective-permute-start | bytes 3538952 | tf_op jit(solution)/shard_map/ppermute | solution.py:527
  309.0 218.5 %collective-permute-start.48 = (bf16[16,96,768]{2,1,0:T(8,128)(2,1)}, bf16[16,96,768]{2,1,0:T(8,128)(2,1)}, u32[]{:S(2)}, u32[]{:S(2)}) collective-permute-start(bf16[16,96,768]{2,1,0:T(8,128)(2,1)} %bitcast.268), channel_id=1, source_target_pairs={{0,1},{1,0},{2,3},{3,2},{4,5},{5,4},{6,7},{7,6},{8,9},{9,8},{10,11... | collective-permute-start | bytes 7077896 | tf_op jit(solution)/shard_map/ppermute | solution.py:527
  313.5 111.4 %collective-permute-start.28 = (bf16[16,24,768]{2,1,0:T(8,128)(2,1)}, bf16[16,24,768]{2,1,0:T(8,128)(2,1)S(1)}, u32[]{:S(2)}, u32[]{:S(2)}) collective-permute-start(bf16[16,24,768]{2,1,0:T(8,128)(2,1)} %bitcast.272), channel_id=1, source_target_pairs={{0,1},{1,0},{2,3},{3,2},{4,5},{5,4},{6,7},{7,6},{8,9},{9,8},{10,11... | collective-permute-start | bytes 1769480 | tf_op jit(solution)/shard_map/ppermute | solution.py:527
  414.8 90.6 %collective-permute-start.6 = (bf16[2,1024,768]{2,1,0:T(8,128)(2,1)}, bf16[2,1024,768]{2,1,0:T(8,128)(2,1)}, u32[]{:S(2)}, u32[]{:S(2)}) collective-permute-start(bf16[2,1024,768]{2,1,0:T(8,128)(2,1)} %get-tuple-element.99), channel_id=1, source_target_pairs={{0,1},{1,0},{2,3},{3,2},{4,5},{5,4},{6,7},{7,6},{8,9},{9,8},{10,11... | collective-permute-start | bytes 9437192 | tf_op jit(solution)/shard_map/ppermute | solution.py:640
  419.8 5.1 collective-permute-start.23
  425.3 9.9 %collective-permute-start.24 = (bf16[8,24,768]{2,1,0:T(8,128)(2,1)S(1)}, bf16[8,24,768]{2,1,0:T(8,128)(2,1)S(1)}, u32[]{:S(2)}, u32[]{:S(2)}) collective-permute-start(bf16[8,24,768]{2,1,0:T(8,128)(2,1)S(1)} %bitcast.256), channel_id=1, source_target_pairs={{0,4},{1,5},{2,6},{3,7},{4,0},{5,1},{6,2},{7,3},{8,12},{9,13},{10,... | collective-permute-start | bytes 884744 | tf_op jit(solution)/shard_map/ppermute | solution.py:527
  426.9 14.7 %collective-permute-start.29 = (bf16[8,24,768]{2,1,0:T(8,128)(2,1)S(1)}, bf16[8,24,768]{2,1,0:T(8,128)(2,1)S(1)}, u32[]{:S(2)}, u32[]{:S(2)}) collective-permute-start(bf16[8,24,768]{2,1,0:T(8,128)(2,1)S(1)} %bitcast.254), channel_id=1, source_target_pairs={{0,4},{1,5},{2,6},{3,7},{4,0},{5,1},{6,2},{7,3},{8,12},{9,13},{10,... | collective-permute-start | bytes 884744 | tf_op jit(solution)/shard_map/ppermute | solution.py:527
  427.9 64.1 %collective-permute-start.40 = (bf16[4,24,3072]{2,1,0:T(8,128)(2,1)S(1)}, bf16[4,24,3072]{2,1,0:T(8,128)(2,1)S(1)}, u32[]{:S(2)}, u32[]{:S(2)}) collective-permute-start(bf16[4,24,3072]{2,1,0:T(8,128)(2,1)S(1)} %get-tuple-element.173), channel_id=1, source_target_pairs={{0,4},{1,5},{2,6},{3,7},{4,0},{5,1},{6,2},{7,3},{8,12},{9,13},{10,... | collective-permute-start | bytes 1769480 | tf_op jit(solution)/shard_map/ppermute | solution.py:527
  435.3 42.1 %collective-permute-start.25 = (bf16[4,24,768]{2,1,0:T(8,128)(2,1)S(1)}, bf16[4,24,768]{2,1,0:T(8,128)(2,1)S(1)}, u32[]{:S(2)}, u32[]{:S(2)}) collective-permute-start(bf16[4,24,768]{2,1,0:T(8,128)(2,1)S(1)} %bitcast.261), channel_id=1, source_target_pairs={{0,8},{1,9},{2,10},{3,11},{4,12},{5,13},{6,14},{7,15},{8,0},{9,1},... | collective-permute-start | bytes 442376 | tf_op jit(solution)/shard_map/ppermute | solution.py:527
  441.7 35.9 %collective-permute-start.30 = (bf16[4,24,768]{2,1,0:T(8,128)(2,1)S(1)}, bf16[4,24,768]{2,1,0:T(8,128)(2,1)S(1)}, u32[]{:S(2)}, u32[]{:S(2)}) collective-permute-start(bf16[4,24,768]{2,1,0:T(8,128)(2,1)S(1)} %bitcast.262), channel_id=1, source_target_pairs={{0,8},{1,9},{2,10},{3,11},{4,12},{5,13},{6,14},{7,15},{8,0},{9,1},... | collective-permute-start | bytes 442376 | tf_op jit(solution)/shard_map/ppermute | solution.py:527
  477.5 50.0 %collective-permute-start.43 = (bf16[16,96,768]{2,1,0:T(8,128)(2,1)}, bf16[16,96,768]{2,1,0:T(8,128)(2,1)}, u32[]{:S(2)}, u32[]{:S(2)}) collective-permute-start(bf16[16,96,768]{2,1,0:T(8,128)(2,1)} %bitcast.96), channel_id=1, source_target_pairs={{0,1},{1,0},{2,3},{3,2},{4,5},{5,4},{6,7},{7,6},{8,9},{9,8},{10,11... | collective-permute-start | bytes 7077896 | tf_op jit(solution)/shard_map/ppermute | solution.py:527
  477.5 7.1 %collective-permute-start.26 = (bf16[2,24,768]{2,1,0:T(8,128)(2,1)S(1)}, bf16[2,24,768]{2,1,0:T(8,128)(2,1)S(1)}, u32[]{:S(2)}, u32[]{:S(2)}) collective-permute-start(bf16[2,24,768]{2,1,0:T(8,128)(2,1)S(1)} %get-tuple-element.202), channel_id=1, source_target_pairs={{0,16},{1,17},{2,18},{3,19},{4,20},{5,21},{6,22},{7,23},{8,24},{9,... | collective-permute-start | bytes 221192 | tf_op jit(solution)/shard_map/ppermute | solution.py:527
  484.6 6.3 collective-permute-start.31
  495.1 42.2 %collective-permute-start.33 = (bf16[16,24,3072]{2,1,0:T(8,128)(2,1)}, bf16[16,24,3072]{2,1,0:T(8,128)(2,1)}, u32[]{:S(2)}, u32[]{:S(2)}) collective-permute-start(bf16[16,24,3072]{2,1,0:T(8,128)(2,1)} %bitcast.72), channel_id=1, source_target_pairs={{0,1},{1,0},{2,3},{3,2},{4,5},{5,4},{6,7},{7,6},{8,9},{9,8},{10,11... | collective-permute-start | bytes 7077896 | tf_op jit(solution)/shard_map/ppermute | solution.py:527
  496.0 8.5 %collective-permute-start.41 = (bf16[2,24,3072]{2,1,0:T(8,128)(2,1)S(1)}, bf16[2,24,3072]{2,1,0:T(8,128)(2,1)S(1)}, u32[]{:S(2)}, u32[]{:S(2)}) collective-permute-start(bf16[2,24,3072]{2,1,0:T(8,128)(2,1)S(1)} %get-tuple-element.189), channel_id=1, source_target_pairs={{0,8},{1,9},{2,10},{3,11},{4,12},{5,13},{6,14},{7,15},{8,0},{9,1},... | collective-permute-start | bytes 884744 | tf_op jit(solution)/shard_map/ppermute | solution.py:527
  504.6 17.5 %collective-permute-start.42 = (bf16[1,24,3072]{2,1,0:T(8,128)(2,1)S(1)}, bf16[1,24,3072]{2,1,0:T(8,128)(2,1)S(1)}, u32[]{:S(2)}, u32[]{:S(2)}) collective-permute-start(bf16[1,24,3072]{2,1,0:T(8,128)(2,1)S(1)} %fusion.12), channel_id=1, source_target_pairs={{0,16},{1,17},{2,18},{3,19},{4,20},{5,21},{6,22},{7,23},{8,24},{9,... | collective-permute-start | bytes 442376 | tf_op jit(solution)/shard_map/ppermute | solution.py:527
  521.8 111.5 %collective-permute-start.18 = (bf16[16,24,2304]{2,1,0:T(8,128)(2,1)}, bf16[16,24,2304]{2,1,0:T(8,128)(2,1)}, u32[]{:S(2)}, u32[]{:S(2)}) collective-permute-start(bf16[16,24,2304]{2,1,0:T(8,128)(2,1)} %bitcast.270), channel_id=1, source_target_pairs={{0,1},{1,0},{2,3},{3,2},{4,5},{5,4},{6,7},{7,6},{8,9},{9,8},{10,11... | collective-permute-start | bytes 5308424 | tf_op jit(solution)/shard_map/ppermute | solution.py:527
  525.9 9.5 %collective-permute-start.10 = (f32[4,1,640]{2,1,0:T(1,128)S(1)}, f32[4,1,640]{2,1,0:T(1,128)S(1)}, u32[]{:S(2)}, u32[]{:S(2)}) collective-permute-start(f32[4,1,640]{2,1,0:T(1,128)S(1)} %get-tuple-element.210), channel_id=1, source_target_pairs={{0,4},{1,5},{2,6},{3,7},{4,0},{5,1},{6,2},{7,3},{8,12},{9,13},{10,... | collective-permute-start | bytes 30728 | tf_op jit(solution)/shard_map/ppermute | solution.py:527
  533.4 29.2 %collective-permute-start.44 = (bf16[8,96,768]{2,1,0:T(8,128)(2,1)}, bf16[8,96,768]{2,1,0:T(8,128)(2,1)}, u32[]{:S(2)}, u32[]{:S(2)}) collective-permute-start(bf16[8,96,768]{2,1,0:T(8,128)(2,1)} %bitcast.99), channel_id=1, source_target_pairs={{0,4},{1,5},{2,6},{3,7},{4,0},{5,1},{6,2},{7,3},{8,12},{9,13},{10,... | collective-permute-start | bytes 3538952 | tf_op jit(solution)/shard_map/ppermute | solution.py:527
  533.9 51.8 %collective-permute-start.49 = (bf16[8,96,768]{2,1,0:T(8,128)(2,1)S(1)}, bf16[8,96,768]{2,1,0:T(8,128)(2,1)S(1)}, u32[]{:S(2)}, u32[]{:S(2)}) collective-permute-start(bf16[8,96,768]{2,1,0:T(8,128)(2,1)S(1)} %bitcast.230), channel_id=1, source_target_pairs={{0,4},{1,5},{2,6},{3,7},{4,0},{5,1},{6,2},{7,3},{8,12},{9,13},{10,... | collective-permute-start | bytes 3538952 | tf_op jit(solution)/shard_map/ppermute | solution.py:527
  535.4 6.6 collective-permute-start.11
  541.0 46.7 %collective-permute-start.34 = (bf16[8,24,3072]{2,1,0:T(8,128)(2,1)}, bf16[8,24,3072]{2,1,0:T(8,128)(2,1)}, u32[]{:S(2)}, u32[]{:S(2)}) collective-permute-start(bf16[8,24,3072]{2,1,0:T(8,128)(2,1)} %get-tuple-element.159), channel_id=1, source_target_pairs={{0,2},{1,3},{2,0},{3,1},{4,6},{5,7},{6,4},{7,5},{8,10},{9,11},{10,... | collective-permute-start | bytes 3538952 | tf_op jit(solution)/shard_map/ppermute | solution.py:527
  542.0 9.2 %collective-permute-start.12 = (f32[1,1,640]{2,1,0:T(1,128)S(1)}, f32[1,1,640]{2,1,0:T(1,128)S(1)}, u32[]{:S(2)}, u32[]{:S(2)}) collective-permute-start(f32[1,1,640]{2,1,0:T(1,128)S(1)} %fusion.45), channel_id=1, source_target_pairs={{0,16},{1,17},{2,18},{3,19},{4,20},{5,21},{6,22},{7,23},{8,24},{9,... | collective-permute-start | bytes 7688 | tf_op jit(solution)/shard_map/ppermute | solution.py:527
  551.3 38.4 %collective-permute-start.7 = (bf16[512,768]{1,0:T(8,128)(2,1)S(1)}, bf16[512,768]{1,0:T(8,128)(2,1)S(1)}, u32[]{:S(2)}, u32[]{:S(2)}) collective-permute-start(bf16[512,768]{1,0:T(8,128)(2,1)S(1)} %slice.235), channel_id=1, source_target_pairs={{0,2},{1,3},{2,0},{3,1},{4,6},{5,7},{6,4},{7,5},{8,10},{9,11},{10,... | collective-permute-start | bytes 2359304 | tf_op jit(solution)/shard_map/ppermute | solution.py:599
  562.6 70.7 %collective-permute-start.13 = (bf16[16,24,2304]{2,1,0:T(8,128)(2,1)}, bf16[16,24,2304]{2,1,0:T(8,128)(2,1)S(1)}, u32[]{:S(2)}, u32[]{:S(2)}) collective-permute-start(bf16[16,24,2304]{2,1,0:T(8,128)(2,1)} %bitcast.271), channel_id=1, source_target_pairs={{0,1},{1,0},{2,3},{3,2},{4,5},{5,4},{6,7},{7,6},{8,9},{9,8},{10,11... | collective-permute-start | bytes 5308424 | tf_op jit(solution)/shard_map/ppermute | solution.py:527
  585.7 19.4 %collective-permute-start.45 = (bf16[4,96,768]{2,1,0:T(8,128)(2,1)S(1)}, bf16[4,96,768]{2,1,0:T(8,128)(2,1)S(1)}, u32[]{:S(2)}, u32[]{:S(2)}) collective-permute-start(bf16[4,96,768]{2,1,0:T(8,128)(2,1)S(1)} %bitcast.245), channel_id=1, source_target_pairs={{0,8},{1,9},{2,10},{3,11},{4,12},{5,13},{6,14},{7,15},{8,0},{9,1},... | collective-permute-start | bytes 1769480 | tf_op jit(solution)/shard_map/ppermute | solution.py:527
  587.7 30.5 %collective-permute-start.50 = (bf16[4,96,768]{2,1,0:T(8,128)(2,1)S(1)}, bf16[4,96,768]{2,1,0:T(8,128)(2,1)S(1)}, u32[]{:S(2)}, u32[]{:S(2)}) collective-permute-start(bf16[4,96,768]{2,1,0:T(8,128)(2,1)S(1)} %bitcast.246), channel_id=1, source_target_pairs={{0,8},{1,9},{2,10},{3,11},{4,12},{5,13},{6,14},{7,15},{8,0},{9,1},... | collective-permute-start | bytes 1769480 | tf_op jit(solution)/shard_map/ppermute | solution.py:527
  589.7 28.7 %collective-permute-start.35 = (bf16[4,24,3072]{2,1,0:T(8,128)(2,1)S(1)}, bf16[4,24,3072]{2,1,0:T(8,128)(2,1)S(1)}, u32[]{:S(2)}, u32[]{:S(2)}) collective-permute-start(bf16[4,24,3072]{2,1,0:T(8,128)(2,1)S(1)} %get-tuple-element.171), channel_id=1, source_target_pairs={{0,4},{1,5},{2,6},{3,7},{4,0},{5,1},{6,2},{7,3},{8,12},{9,13},{10,... | collective-permute-start | bytes 1769480 | tf_op jit(solution)/shard_map/ppermute | solution.py:527
  605.2 17.7 %collective-permute-start.46 = (bf16[2,96,768]{2,1,0:T(8,128)(2,1)S(1)}, bf16[2,96,768]{2,1,0:T(8,128)(2,1)S(1)}, u32[]{:S(2)}, u32[]{:S(2)}) collective-permute-start(bf16[2,96,768]{2,1,0:T(8,128)(2,1)S(1)} %get-tuple-element.183), channel_id=1, source_target_pairs={{0,16},{1,17},{2,18},{3,19},{4,20},{5,21},{6,22},{7,23},{8,24},{9,... | collective-permute-start | bytes 884744 | tf_op jit(solution)/shard_map/ppermute | solution.py:527
  618.3 13.8 %collective-permute-start.51 = (bf16[2,96,768]{2,1,0:T(8,128)(2,1)S(1)}, bf16[2,96,768]{2,1,0:T(8,128)(2,1)S(1)}, u32[]{:S(2)}, u32[]{:S(2)}) collective-permute-start(bf16[2,96,768]{2,1,0:T(8,128)(2,1)S(1)} %get-tuple-element.185), channel_id=1, source_target_pairs={{0,16},{1,17},{2,18},{3,19},{4,20},{5,21},{6,22},{7,23},{8,24},{9,... | collective-permute-start | bytes 884744 | tf_op jit(solution)/shard_map/ppermute | solution.py:527
  618.6 14.6 %collective-permute-start.36 = (bf16[2,24,3072]{2,1,0:T(8,128)(2,1)S(1)}, bf16[2,24,3072]{2,1,0:T(8,128)(2,1)S(1)}, u32[]{:S(2)}, u32[]{:S(2)}) collective-permute-start(bf16[2,24,3072]{2,1,0:T(8,128)(2,1)S(1)} %get-tuple-element.187), channel_id=1, source_target_pairs={{0,8},{1,9},{2,10},{3,11},{4,12},{5,13},{6,14},{7,15},{8,0},{9,1},... | collective-permute-start | bytes 884744 | tf_op jit(solution)/shard_map/ppermute | solution.py:527
  623.0 19.3 %collective-permute-start.47 = (bf16[1,96,768]{2,1,0:T(8,128)(2,1)S(1)}, bf16[1,96,768]{2,1,0:T(8,128)(2,1)S(1)}, u32[]{:S(2)}, u32[]{:S(2)}) collective-permute-start(bf16[1,96,768]{2,1,0:T(8,128)(2,1)S(1)} %fusion.10), channel_id=1, source_target_pairs={{0,2},{1,3},{2,0},{3,1},{4,6},{5,7},{6,4},{7,5},{8,10},{9,11},{10,... | collective-permute-start | bytes 442376 | tf_op jit(solution)/shard_map/ppermute | solution.py:527
  632.1 10.8 %collective-permute-start.52 = (bf16[1,96,768]{2,1,0:T(8,128)(2,1)S(1)}, bf16[1,96,768]{2,1,0:T(8,128)(2,1)S(1)}, u32[]{:S(2)}, u32[]{:S(2)}) collective-permute-start(bf16[1,96,768]{2,1,0:T(8,128)(2,1)S(1)} %fusion.8), channel_id=1, source_target_pairs={{0,2},{1,3},{2,0},{3,1},{4,6},{5,7},{6,4},{7,5},{8,10},{9,11},{10,... | collective-permute-start | bytes 442376 | tf_op jit(solution)/shard_map/ppermute | solution.py:527
  633.2 9.0 %collective-permute-start.37 = (bf16[1,24,3072]{2,1,0:T(8,128)(2,1)S(1)}, bf16[1,24,3072]{2,1,0:T(8,128)(2,1)S(1)}, u32[]{:S(2)}, u32[]{:S(2)}) collective-permute-start(bf16[1,24,3072]{2,1,0:T(8,128)(2,1)S(1)} %fusion.14), channel_id=1, source_target_pairs={{0,16},{1,17},{2,18},{3,19},{4,20},{5,21},{6,22},{7,23},{8,24},{9,... | collective-permute-start | bytes 442376 | tf_op jit(solution)/shard_map/ppermute | solution.py:527
  635.8 22.6 %collective-permute-start.14 = (bf16[8,24,2304]{2,1,0:T(8,128)(2,1)S(1)}, bf16[8,24,2304]{2,1,0:T(8,128)(2,1)S(1)}, u32[]{:S(2)}, u32[]{:S(2)}) collective-permute-start(bf16[8,24,2304]{2,1,0:T(8,128)(2,1)S(1)} %bitcast.238), channel_id=1, source_target_pairs={{0,4},{1,5},{2,6},{3,7},{4,0},{5,1},{6,2},{7,3},{8,12},{9,13},{10,... | collective-permute-start | bytes 2654216 | tf_op jit(solution)/shard_map/ppermute | solution.py:527
  642.3 33.8 %collective-permute-start.19 = (bf16[8,24,2304]{2,1,0:T(8,128)(2,1)S(1)}, bf16[8,24,2304]{2,1,0:T(8,128)(2,1)S(1)}, u32[]{:S(2)}, u32[]{:S(2)}) collective-permute-start(bf16[8,24,2304]{2,1,0:T(8,128)(2,1)S(1)} %bitcast.237), channel_id=1, source_target_pairs={{0,4},{1,5},{2,6},{3,7},{4,0},{5,1},{6,2},{7,3},{8,12},{9,13},{10,... | collective-permute-start | bytes 2654216 | tf_op jit(solution)/shard_map/ppermute | solution.py:527
  658.7 20.8 %collective-permute-start.15 = (bf16[4,24,2304]{2,1,0:T(8,128)(2,1)S(1)}, bf16[4,24,2304]{2,1,0:T(8,128)(2,1)S(1)}, u32[]{:S(2)}, u32[]{:S(2)}) collective-permute-start(bf16[4,24,2304]{2,1,0:T(8,128)(2,1)S(1)} %bitcast.251), channel_id=1, source_target_pairs={{0,8},{1,9},{2,10},{3,11},{4,12},{5,13},{6,14},{7,15},{8,0},{9,1},... | collective-permute-start | bytes 1327112 | tf_op jit(solution)/shard_map/ppermute | solution.py:527
  676.4 15.9 %collective-permute-start.20 = (bf16[4,24,2304]{2,1,0:T(8,128)(2,1)S(1)}, bf16[4,24,2304]{2,1,0:T(8,128)(2,1)S(1)}, u32[]{:S(2)}, u32[]{:S(2)}) collective-permute-start(bf16[4,24,2304]{2,1,0:T(8,128)(2,1)S(1)} %bitcast.252), channel_id=1, source_target_pairs={{0,8},{1,9},{2,10},{3,11},{4,12},{5,13},{6,14},{7,15},{8,0},{9,1},... | collective-permute-start | bytes 1327112 | tf_op jit(solution)/shard_map/ppermute | solution.py:527
  679.6 12.8 %collective-permute-start.16 = (bf16[2,24,2304]{2,1,0:T(8,128)(2,1)S(1)}, bf16[2,24,2304]{2,1,0:T(8,128)(2,1)S(1)}, u32[]{:S(2)}, u32[]{:S(2)}) collective-permute-start(bf16[2,24,2304]{2,1,0:T(8,128)(2,1)S(1)} %get-tuple-element.195), channel_id=1, source_target_pairs={{0,16},{1,17},{2,18},{3,19},{4,20},{5,21},{6,22},{7,23},{8,24},{9,... | collective-permute-start | bytes 663560 | tf_op jit(solution)/shard_map/ppermute | solution.py:527
  692.4 10.9 %collective-permute-start.21 = (bf16[2,24,2304]{2,1,0:T(8,128)(2,1)S(1)}, bf16[2,24,2304]{2,1,0:T(8,128)(2,1)S(1)}, u32[]{:S(2)}, u32[]{:S(2)}) collective-permute-start(bf16[2,24,2304]{2,1,0:T(8,128)(2,1)S(1)} %get-tuple-element.197), channel_id=1, source_target_pairs={{0,16},{1,17},{2,18},{3,19},{4,20},{5,21},{6,22},{7,23},{8,24},{9,... | collective-permute-start | bytes 663560 | tf_op jit(solution)/shard_map/ppermute | solution.py:527
  692.5 11.9 %collective-permute-start.17 = (bf16[1,24,2304]{2,1,0:T(8,128)(2,1)S(1)}, bf16[1,24,2304]{2,1,0:T(8,128)(2,1)S(1)}, u32[]{:S(2)}, u32[]{:S(2)}) collective-permute-start(bf16[1,24,2304]{2,1,0:T(8,128)(2,1)S(1)} %fusion.20), channel_id=1, source_target_pairs={{0,2},{1,3},{2,0},{3,1},{4,6},{5,7},{6,4},{7,5},{8,10},{9,11},{10,... | collective-permute-start | bytes 331784 | tf_op jit(solution)/shard_map/ppermute | solution.py:527
  (38 other events, 349.6 us)

commit v2 on v1

--- a/solution.py
+++ b/solution.py
@@ -24,8 +24,8 @@
     return pltpu.CompilerParams(vmem_limit_bytes=mib << 20)
 
 
-def row(index):
-    return pl.BlockSpec((1, index[1]), lambda *_: (index[0], 0))
+def cost(products, nbytes=0):
+    return pl.CostEstimate(flops=int(2 * products), bytes_accessed=int(nbytes), transcendentals=0)
 
 
 def normalise(x):
@@ -57,6 +57,16 @@
     half = poly * u
     cdf = jnp.where(x >= 0, 1.0 - half, half)
     return x * cdf, cdf + x * (u * 0.3989422804014327)
+
+
+def kernel_call(kernel, ins, in_specs, after=(), **kwargs):
+    n = len(ins)
+    extra = [pl.BlockSpec(memory_space=pl.ANY)] * len(after)
+
+    def body(*refs):
+        kernel(*refs[:n], *refs[n + len(after) :])
+
+    return pl.pallas_call(body, in_specs=list(in_specs) + extra, **kwargs)(*ins, *after)
 
 
 def qkv_tile(x, gain, bias, weight, row_bias, normed_ref, q_ref, kv_ref):
@@ -102,6 +112,7 @@
             jax.ShapeDtypeStruct((2, t, d), BF),
         ],
         compiler_params=params(56),
+        cost_estimate=cost(4.6e9),
         name="norm_qkv",
     )(x, gain, bias, weight, row_bias)
 
@@ -166,14 +177,190 @@
         out_specs=[one, pl.BlockSpec((1, 8, t), lambda h: (h, 0, 0))],
         out_shape=[jax.ShapeDtypeStruct((t, d), BF), jax.ShapeDtypeStruct((pairs, 8, t), F32)],
         compiler_params=params(56),
+        cost_estimate=cost(16e9),
         name="attend",
     )(q, kv, kvo)
 
 
-def attend_back_kernel(q, kv, kvo, up, out, lse, dq, dkv, dkvo, *, chunk):
+class Place:
+    def __init__(self, count):
+        self.count = count
+        self.bits = count.bit_length() - 1
+        self.dp, self.seq = lax.axis_index("dp"), lax.axis_index("seq")
+
+    def bit(self, b):
+        return (self.seq // (1 << b)) % 2 if b < 2 else (self.dp // (1 << (b - 2))) % 2
+
+    def partner(self, b):
+        step = 1 - 2 * self.bit(b)
+        if b < 2:
+            return {"dp": self.dp, "seq": self.seq + step * (1 << b)}
+        return {"dp": self.dp + step * (1 << (b - 2)), "seq": self.seq}
+
+    def greet(self):
+        barrier = pltpu.get_barrier_semaphore()
+        for b in range(self.bits):
+            pl.semaphore_signal(barrier, inc=1, device_id=self.partner(b), device_id_type=pl.DeviceIdType.MESH)
+        pl.semaphore_wait(barrier, self.bits)
+
+
+class Job:
+    def __init__(self, keep, send, count, orders):
+        self.lead = count.bit_length() - 2
+        self.keep = keep.reshape((2,) * self.lead + keep.shape[1:])
+        self.send = send.reshape((2,) * self.lead + send.shape[1:])
+        self.rows, self.cols = keep.shape[1:]
+        self.orders = orders
+        self.wide = self.cols // len(orders)
+        self.dtype = keep.dtype
+
+    def scratch(self):
+        out = []
+        for _ in self.orders:
+            block = (self.rows, self.wide)
+            out.append(pltpu.VMEM((2,) * self.lead + block, self.dtype))
+            for left in range(self.lead, -1, -1):
+                out.append(pltpu.VMEM((2,) * left + block, self.dtype))
+        return out
+
+    def out_shape(self):
+        return jax.ShapeDtypeStruct((self.rows, self.cols), F32)
+
+
+class Part:
+    def __init__(self, place, job, at, keep, send, out, scratch, sems, first_sem):
+        self.place, self.job, self.keep, self.send, self.out = place, job, keep, send, out
+        self.order = job.orders[at]
+        self.cols = slice(at * job.wide, (at + 1) * job.wide)
+        self.total, self.got = scratch[0], scratch[1:]
+        self.sems, self.first = sems, first_sem
+
+    def own(self):
+        return pltpu.make_async_copy(
+            self.keep.at[(slice(None),) * (self.job.lead + 1) + (self.cols,)], self.total, self.sems.at[0, self.first]
+        )
+
+    def index(self, stage, away):
+        out = []
+        for b in range(self.job.lead, 0, -1):
+            at = self.order.index(b) + 1
+            if at < stage or (at == stage and not away):
+                out.append(self.place.bit(b))
+            elif at == stage:
+                out.append(1 - self.place.bit(b))
+            else:
+                out.append(slice(None))
+        return tuple(out)
+
+    def copy(self, stage):
+        if stage == 0:
+            bit, src = 0, self.send.at[(slice(None),) * (self.job.lead + 1) + (self.cols,)]
+        else:
+            bit, src = self.order[stage - 1], self.total.at[self.index(stage, True)]
+        return pltpu.make_async_remote_copy(
+            src_ref=src,
+            dst_ref=self.got[stage],
+            send_sem=self.sems.at[1, self.first + stage],
+            recv_sem=self.sems.at[2, self.first + stage],
+            device_id=self.place.partner(bit),
+            device_id_type=pl.DeviceIdType.MESH,
+        )
+
+    def begin(self, stage):
+        if stage == 0:
+            self.own().start()
+        self.copy(stage).start()
+
+    def end(self, stage):
+        if stage == 0:
+            self.own().wait()
+        self.copy(stage).wait()
+        index = self.index(stage, False)
+        if stage == len(self.order):
+            self.out[:, self.cols] = self.total[index].astype(F32) + self.got[stage][...].astype(F32)
+        elif stage == 0:
+            self.total[...] = self.total[...] + self.got[0][...]
+        else:
+            self.total[index] = self.total[index] + self.got[stage][...]
+
+
+class Sums:
+    def __init__(self, jobs, count):
+        self.jobs, self.count = jobs, count
+        self.stages = count.bit_length() - 1
+
+    def inputs(self):
+        return [x for job in self.jobs for x in (job.keep, job.send)]
+
+    def n_parts(self):
+        return sum(len(job.orders) for job in self.jobs)
+
+    def in_specs(self):
+        return [pl.BlockSpec(memory_space=pl.ANY)] * (2 * len(self.jobs))
+
+    def out_shapes(self):
+        return [job.out_shape() for job in self.jobs]
+
+    def out_specs(self):
+        return [pl.BlockSpec((job.rows, job.cols), lambda *_: (0, 0)) for job in self.jobs]
+
+    def scratch(self):
+        out = [x for job in self.jobs for x in job.scratch()]
+        return out + [pltpu.SemaphoreType.DMA((3, self.n_parts() * self.stages))]
+
+    def parts(self, place, ins, outs, scratch):
+        scratch = list(scratch)
+        sems = scratch.pop()
+        found = []
+        for i, job in enumerate(self.jobs):
+            for at in range(len(job.orders)):
+                mine, scratch = scratch[: job.lead + 2], scratch[job.lead + 2 :]
+                found.append(
+                    Part(place, job, at, ins[2 * i], ins[2 * i + 1], outs[i], mine, sems, len(found) * self.stages)
+                )
+        return found
+
+    def advance(self, parts, stage):
+        for part in parts:
+            if stage > 0:
+                part.end(stage - 1)
+            if stage < self.stages:
+                part.begin(stage)
+
+
+def attend_back_kernel(*refs, chunk, sums, slots):
+    n_in, n_out = 6 + 2 * len(sums.jobs), 3 + len(sums.jobs)
+    q, kv, kvo, up, out, lse = refs[:6]
+    dq, dkv, dkvi = refs[n_in : n_in + 3]
+    outbox, box_sems = refs[n_in + n_out : n_in + n_out + 2]
+    place = Place(sums.count)
+    parts = sums.parts(place, refs[6:n_in], refs[n_in + 3 : n_in + n_out], refs[n_in + n_out + 2 :])
     t = q.shape[0]
     scale = HEAD**-0.5
     c = LOG2E * scale
+    pair, pairs = pl.program_id(0), len(slots) - 1
+
+    def parcel(at):
+        return pltpu.make_async_remote_copy(
+            src_ref=outbox.at[at % 2],
+            dst_ref=dkvi.at[at],
+            send_sem=box_sems.at[0, at],
+            recv_sem=box_sems.at[1, at],
+            device_id=place.partner(0),
+            device_id_type=pl.DeviceIdType.MESH,
+        )
+
+    pl.when(pair == 0)(place.greet)
+    for at in range(pairs):
+
+        @pl.when(pair == at)
+        def _(at=at):
+            for stage in slots[at]:
+                sums.advance(parts, stage)
+            if at >= 2:
+                parcel(at - 2).wait_send()
+
+    box = outbox.at[lax.rem(pair, 2)]
     for head in range(2):
         ls = slice(HEAD * head, HEAD * head + HEAD)
         qh = q[:, ls]
@@ -184,7 +371,7 @@
         inner = jnp.sum(uh.astype(F32) * out[:, ls].astype(F32), axis=1, keepdims=True)
         blocks = [
             (src, dst, slice(i * chunk, (i + 1) * chunk))
-            for src, dst in ((kvo, dkvo), (kv, dkv))
+            for src, dst in ((kvo, box), (kv, dkv))
             for i in range(t // chunk)
         ]
 
@@ -206,25 +393,72 @@
             total = part if total is None else total + part
         dq[:, ls] = (total * scale).astype(BF)
 
-
-def attend_back_call(q, kv, kvo, up, out, lse):
+    for at in range(pairs):
+
+        @pl.when(pair == at)
+        def _(at=at):
+            parcel(at).start()
+            if at == pairs - 1:
+                for stage in slots[pairs]:
+                    sums.advance(parts, stage)
+                for last in range(max(0, pairs - 2), pairs):
+                    parcel(last).wait_send()
+                for each in range(pairs):
+                    parcel(each).wait_recv()
+
+
+def attend_back_call(q, kv, kvo, up, out, lse, sums, collective_id):
     t, d = q.shape
     pairs = d // 128
     both = pl.BlockSpec((2, t, 128), lambda h: (0, 0, h))
     one = pl.BlockSpec((t, 128), lambda h: (0, h))
+    slots = [[] for _ in range(pairs + 1)]
+    starts = [0, 1, 3, 4, 5]
+    for stage in range(sums.stages + 1):
+        slots[starts[stage] if stage < min(len(starts), sums.stages) else pairs].append(stage)
     return pl.pallas_call(
-        functools.partial(attend_back_kernel, chunk=min(256, t)),
+        functools.partial(attend_back_kernel, chunk=min(256, t), sums=sums, slots=slots),
         grid=(pairs,),
-        in_specs=[one, both, both, one, one, pl.BlockSpec((1, 8, t), lambda h: (h, 0, 0))],
-        out_specs=[one, both, both],
+        in_specs=[one, both, both, one, one, pl.BlockSpec((1, 8, t), lambda h: (h, 0, 0))] + sums.in_specs(),
+        out_specs=[one, both, pl.BlockSpec(memory_space=pl.ANY)] + sums.out_specs(),
         out_shape=[
             jax.ShapeDtypeStruct((t, d), BF),
             jax.ShapeDtypeStruct((2, t, d), BF),
-            jax.ShapeDtypeStruct((2, t, d), BF),
-        ],
-        compiler_params=params(56),
+            jax.ShapeDtypeStruct((pairs, 2, t, 128), BF),
+        ]
+        + sums.out_shapes(),
+        scratch_shapes=[pltpu.VMEM((2, 2, t, 128), BF), pltpu.SemaphoreType.DMA((2, pairs))] + sums.scratch(),
+        compiler_params=pltpu.CompilerParams(
+            vmem_limit_bytes=60 << 20, collective_id=collective_id, has_side_effects=True
+        ),
+        cost_estimate=cost(37e9),
         name="attend_back",
-    )(q, kv, kvo, up, out, lse)
+    )(q, kv, kvo, up, out, lse, *sums.inputs())
+
+
+def sums_kernel(*refs, sums):
+    n = len(sums.jobs)
+    place = Place(sums.count)
+    parts = sums.parts(place, refs[: 2 * n], refs[2 * n : 3 * n], refs[3 * n :])
+    place.greet()
+    for stage in range(sums.stages + 1):
+        sums.advance(parts, stage)
+
+
+def sums_call(sums, collective_id):
+    return pl.pallas_call(
+        functools.partial(sums_kernel, sums=sums),
+        grid=(1,),
+        in_specs=sums.in_specs(),
+        out_specs=sums.out_specs(),
+        out_shape=sums.out_shapes(),
+        scratch_shapes=sums.scratch(),
+        compiler_params=pltpu.CompilerParams(
+            vmem_limit_bytes=60 << 20, collective_id=collective_id, has_side_effects=True
+        ),
+        cost_estimate=cost(15e9),
+        name="sums",
+    )(*sums.inputs())
 
 
 def forward_kernel(
@@ -303,6 +537,7 @@
             pltpu.SemaphoreType.DMA((3,)),
         ],
         compiler_params=params(58),
+        cost_estimate=cost(15e9),
         name="feed_forward",
     )(att, x, wo, wu, wd, bo, g2, b2, bu, bd)
 
@@ -312,7 +547,7 @@
 
 
 def backward_kernel(
-    g, slope, middle, wo_h, wu_h, wd_h, g2, dz_o, dh_o, dm_o, dy_o, da_o, sums, sums_ff, wo, wu, wd, sems, *, layer, cut
+    ga, gb, slope, middle, wo_h, wu_h, wd_h, g2, dz_o, dh_o, dm_o, dy_o, da_o, sums, sums_ff, wo, wu, wd, sems, *, layer, cut
 ):
     first = pl.program_id(0) == 0
     copies = [
@@ -329,7 +564,8 @@
         copies[0].wait()
         copies[1].wait()
 
-    dz = g[...].astype(BF)
+    g = jnp.where(first, ga[...], gb[...])
+    dz = g.astype(BF)
     dz_o[...] = dz
     sums[0:1, :] += column_sum(dz.astype(F32))
     ff = wu.shape[1]
@@ -353,7 +589,7 @@
     unit, inverse = normalise(middle[...])
     sums[1:2, :] += column_sum(total * unit)
     sums[2:3, :] += column_sum(total)
-    dm = g[...].astype(F32) + norm_back(total, g2[...], unit, inverse)
+    dm = g.astype(F32) + norm_back(total, g2[...], unit, inverse)
     dm_o[...] = dm
     dy = dm.astype(BF)
     dy_o[...] = dy
@@ -366,17 +602,24 @@
     da_o[...] = dot(dy, wo[...], NT).astype(BF)
 
 
-def backward_call(g, slope, middle, layer, wo, wu, wd, g2, tile):
+def backward_call(g, slope, middle, layer, wo, wu, wd, g2, tile, after):
     t, d = middle.shape
     ff = wu.shape[2]
     tok = pl.BlockSpec((tile, d), lambda i: (i, 0))
     wide = pl.BlockSpec((tile, ff), lambda i: (i, 0))
     vec = pl.BlockSpec((None, 1, d), lambda i: (layer, 0, 0))
     hbm = pl.BlockSpec(memory_space=pl.ANY)
-    return pl.pallas_call(
+    if isinstance(g, tuple):
+        pieces = [pl.BlockSpec((tile, d), lambda i: (0, 0))] * 2
+    else:
+        g = (g, g)
+        pieces = [pl.BlockSpec((tile, d), lambda i: (0, 0)), pl.BlockSpec((tile, d), lambda i: (1, 0))]
+    return kernel_call(
         functools.partial(backward_kernel, layer=layer, cut=512),
+        (*g, slope, middle, wo, wu, wd, g2),
+        [*pieces, wide, tok, hbm, hbm, hbm, vec],
+        after,
         grid=(t // tile,),
-        in_specs=[tok, wide, tok, hbm, hbm, hbm, vec],
         out_specs=[
             tok,
             wide,
@@ -402,12 +645,13 @@
             pltpu.SemaphoreType.DMA((3,)),
         ],
         compiler_params=params(58),
+        cost_estimate=cost(13e9),
         name="feed_forward_back",
-    )(g, slope, middle, wo, wu, wd, g2)
-
-
-def joined_back_kernel(dq, dkv, dkv_in, x, dm, weight, gain, df_o, g_o, sums):
-    d = dq.shape[-1]
+    )
+
+
+def joined_back_kernel(dq, dkv, dkvi, x, dm, weight, gain, df_o, g_o, sums):
+    d = x.shape[-1]
 
     @pl.when(pl.program_id(0) == 0)
     def _():
@@ -415,7 +659,8 @@
 
     parts = [dq[...]]
     for i in range(2):
-        parts.append((dkv[i].astype(F32) + dkv_in[i].astype(F32)).astype(BF))
+        got = jnp.concatenate([dkvi[h, i] for h in range(d // 128)], axis=1)
+        parts.append((dkv[i].astype(F32) + got.astype(F32)).astype(BF))
     total = None
     for i, part in enumerate(parts):
         cols = slice(i * d, (i + 1) * d)
@@ -430,22 +675,21 @@
     g_o[...] = dm[...] + norm_back(total, gain[...], unit, inverse)
 
 
-def joined_back_call(dq, dkv, dkv_in, x, dm, layer, weight, gain, tile):
-    t, d = dq.shape
+def joined_back_call(dq, dkv, dkvi, x, dm, layer, weight, gain, tile):
+    t, d = x.shape
     tok = pl.BlockSpec((tile, d), lambda i: (i, 0))
-    both = pl.BlockSpec((2, tile, d), lambda i: (0, i, 0))
     return pl.pallas_call(
         joined_back_kernel,
-        grid=(t // tile,),
         in_specs=[
             tok,
-            both,
-            both,
+            pl.BlockSpec((2, tile, d), lambda i: (0, i, 0)),
+            pl.BlockSpec((d // 128, 2, tile, 128), lambda i: (0, 0, i, 0)),
             tok,
             tok,
             pl.BlockSpec((None, d, 3 * d), lambda i: (layer, 0, 0)),
             pl.BlockSpec((None, 1, d), lambda i: (layer, 0, 0)),
         ],
+        grid=(t // tile,),
         out_specs=[
             pl.BlockSpec((tile, 3 * d), lambda i: (i, 0)),
             tok,
@@ -457,20 +701,14 @@
             jax.ShapeDtypeStruct((8, d), F32),
         ],
         compiler_params=params(56),
+        cost_estimate=cost(6e9),
         name="joined_back",
-    )(dq, dkv, dkv_in, x, dm, weight, gain)
-
-
-def weight_grad_kernel(core, a, b, keep, send, turned, *, rows, fixed_a):
-    def turn():
-        turned[...] = a[...].astype(F32).T.astype(BF)
-
-    if fixed_a:
-        pl.when(pl.program_id(0) == 0)(turn)
-    else:
-        turn()
-    out = dot(turned[...], b[...], NN)
-    n, cols = out.shape
+    )(dq, dkv, dkvi, x, dm, weight, gain)
+
+
+def weight_grad_kernel(core, a, b, keep, send, *, rows):
+    out = lax.dot_general(a[...], b[...], (((0,), (0,)), ((), ())), preferred_element_type=F32)
+    n, _ = out.shape
     even = jnp.concatenate([out[i : i + rows] for i in range(0, n, 2 * rows)], axis=0).astype(BF)
     odd = jnp.concatenate([out[i + rows : i + 2 * rows] for i in range(0, n, 2 * rows)], axis=0).astype(BF)
 
@@ -485,76 +723,39 @@
         send[...] = even
 
 
-def weight_grad_call(core, a, b, chunks, block):
+def weight_grad_call(core, a, b, chunks, block, after=()):
     t, n = a.shape
     cols = b.shape[1]
     fixed_a = n == block
     steps = cols // block if fixed_a else n // block
-    half = block // 2
     if fixed_a:
         a_at, b_at, o_at = (lambda i: (0, 0)), (lambda i: (0, i)), (lambda i: (0, i))
     else:
         a_at, b_at, o_at = (lambda i: (0, i)), (lambda i: (0, 0)), (lambda i: (i, 0))
     shape = jax.ShapeDtypeStruct((n // 2, cols), BF)
-    keep, send = pl.pallas_call(
-        functools.partial(weight_grad_kernel, rows=n // chunks, fixed_a=fixed_a),
-        grid=(steps,),
-        in_specs=[
+    keep, send = kernel_call(
+        functools.partial(weight_grad_kernel, rows=n // chunks),
+        (core, a, b),
+        [
             pl.BlockSpec(memory_space=pltpu.SMEM),
             pl.BlockSpec((t, block), a_at),
             pl.BlockSpec((t, block), b_at),
         ],
-        out_specs=[pl.BlockSpec((half, block), o_at)] * 2,
+        after,
+        grid=(steps,),
+        out_specs=[pl.BlockSpec((block // 2, block), o_at)] * 2,
         out_shape=[shape, shape],
-        scratch_shapes=[pltpu.VMEM((block, t), BF)],
         compiler_params=params(56),
+        cost_estimate=cost(t * n * cols * 1.7),
         name="weight_grad",
-    )(core, a, b)
+    )
     split = (chunks // 2, n // chunks, cols)
     return keep.reshape(split), send.reshape(split)
 
 
-def flip(device_count, bit):
-    return [(i, i ^ (1 << bit)) for i in range(device_count)]
-
-
-class Reducer:
-    def __init__(self, device_count, index):
-        self.count, self.index = device_count, index
-        self.bits = device_count.bit_length() - 1
-
-    def swap(self, array, bit):
-        return lax.ppermute(array, ("dp", "seq"), flip(self.count, bit))
-
-    def begin(self, keep, send):
-        return [keep, self.swap(send, 0)], list(range(self.bits - 1, 0, -1))
-
-    def half(self, terms, bits, bit, which):
-        at = bits.index(bit)
-        out = []
-        for term in terms:
-            n = term.shape[0]
-            lo = 1 << (len(bits) - 1 - at)
-            view = term.reshape(n // (2 * lo), 2, lo, *term.shape[1:])
-            out.append(lax.dynamic_index_in_dim(view, which, 1, keepdims=False).reshape(n // 2, *term.shape[1:]))
-        return out
-
-    def run(self, terms, bits, order, dtype):
-        for bit in order:
-            mine = (self.index >> bit) & 1
-            total = sum(t.astype(F32) for t in self.half(terms, bits, bit, 1 - mine)).astype(dtype)
-            kept = self.half(terms, bits, bit, mine)
-            terms = [sum(t.astype(F32) for t in kept).astype(dtype), self.swap(total, bit)]
-            bits = [b for b in bits if b != bit]
-        return sum(t.astype(F32) for t in terms)[0]
-
-    def small(self, rows):
-        flat = jnp.concatenate([r.reshape(self.count, -1) for r in rows], axis=1)[:, None, :]
-        width = flat.shape[2]
-        pad = -width % 128
-        flat = jnp.pad(flat, ((0, 0), (0, 0), (0, pad)))
-        bits = list(range(self.bits - 1, -1, -1))
-        return self.run([flat], bits, list(range(self.bits)), F32)[0, :width]
+def cut_rows(rows, count):
+    flat = jnp.concatenate([r.reshape(count, -1) for r in rows], axis=1)
+    return jnp.pad(flat, ((0, 0), (0, -flat.shape[1] % 1024)))
 
 
 def on_device(
@@ -584,7 +785,6 @@
     across = [(0, 2), (1, 3), (2, 0), (3, 1)]
     beside = [(0, 1), (1, 0), (2, 3), (3, 2)]
     tile = genes
-    reducer = Reducer(device_count, index)
 
     def rows(v):
         return v[:, None, :]
@@ -592,7 +792,7 @@
     def trade(pair):
         mine = lax.dynamic_index_in_dim(pair, chip, 0, keepdims=False)
         other = lax.dynamic_index_in_dim(pair, 1 - chip, 0, keepdims=False)
-        return jnp.concatenate([mine, lax.ppermute(other, "seq", across)], axis=0)
+        return mine, lax.ppermute(other, "seq", across)
 
     def trade_back(held):
         own = held[:genes]
@@ -608,7 +808,7 @@
         )
     )
 
-    x = trade(cell_tokens)
+    x = jnp.concatenate(trade(cell_tokens), axis=0)
     seeded = cotangent * gene_mask.astype(BF)[:, :, None]
     g = trade(seeded)
 
@@ -627,25 +827,29 @@
     chunks = device_count
     grads = [None] * layers
     vectors = [None] * layers
-    dp_bits = list(range(2, reducer.bits))
+    high = list(range(device_count.bit_length() - 1, 1, -1))[1:]
+    dp_bits = high[::-1]
+    orders = (
+        [1] + dp_bits,
+        dp_bits[:1] + dp_bits[1:-1] + [1] + dp_bits[-1:],
+        dp_bits[1:-1] + [1] + dp_bits[:1] + dp_bits[-1:],
+    )
+    waiting = []
     for layer in reversed(range(layers)):
         x, normed, q, kv, kvo, att, lse, middle, n2, act, slope = saved[layer]
         dz, dh, dm, dy, da, sums, sums_ff = backward_call(
-            g, slope, middle, layer, output_weight, up_weight, down_weight, g2, tile
+            g, slope, middle, layer, output_weight, up_weight, down_weight, g2, tile, []
         )
-        w_down = reducer.begin(*weight_grad_call(core_ref, act, dz, chunks, d))
-        w_up = reducer.begin(*weight_grad_call(core_ref, n2, dh, chunks, d))
-        w_out = reducer.begin(*weight_grad_call(core_ref, att, dy, chunks, d))
-        dq, dkv, dkvo = attend_back_call(q, kv, kvo, da, att, lse)
-        dkv_in = lax.ppermute(dkvo, "seq", beside)
-        df, g, sums_in = joined_back_call(dq, dkv, dkv_in, x, dm, layer, joined_weight, g1, tile)
-        w_joined = reducer.begin(*weight_grad_call(core_ref, normed, df, chunks, d))
-        grads[layer] = [
-            reducer.run(*w_joined, dp_bits + [1], BF),
-            reducer.run(*w_out, dp_bits + [1], BF),
-            reducer.run(*w_up, [1] + dp_bits, BF),
-            reducer.run(*w_down, dp_bits + [1], BF),
+        jobs = waiting + [
+            Job(*weight_grad_call(core_ref, a, b, chunks, d), device_count, orders)
+            for a, b in ((att, dy), (n2, dh), (act, dz))
         ]
+        dq, dkv, dkvi, *done = attend_back_call(q, kv, kvo, da, att, lse, Sums(jobs, device_count), layer)
+        if waiting:
+            grads[layer + 1].append(done.pop(0))
+        grads[layer] = done
+        df, g, sums_in = joined_back_call(dq, dkv, dkvi, x, dm, layer, joined_weight, g1, tile)
+        waiting = [Job(*weight_grad_call(core_ref, normed, df, chunks, d), device_count, orders)]
         vectors[layer] = [
             sums_in[0],
             sums_in[1],
@@ -663,7 +867,13 @@
     plain = [0, 1, 4, 5, 6, 8]
     rows_out = [vectors[l][i] for l in range(layers) for i in plain]
     rows_out += qv + [v[7] for v in vectors]
-    summed = reducer.small(rows_out)
+    flat = cut_rows(rows_out, device_count).reshape(device_count // 2, 2, -1, 128)
+    own = lax.dynamic_index_in_dim(flat, core, 1, keepdims=False)
+    other = lax.dynamic_index_in_dim(flat, 1 - core, 1, keepdims=False)
+    waiting.append(Job(own, other, device_count, orders[:1]))
+    last, summed = sums_call(Sums(waiting, device_count), layers)
+    grads[0].append(last)
+    summed = summed.reshape(-1)
     piece = d // device_count
     at = 0
     small = {}
@@ -687,15 +897,15 @@
         input_gradient,
         vec(0),
         vec(1),
+        mat(3),
+        vec("qv"),
         mat(0),
-        vec("qv"),
-        mat(1),
         vec(4),
         vec(5),
         vec(6),
+        mat(1),
+        vec("up"),
         mat(2),
-        vec("up"),
-        mat(3),
         vec(8),
     )
 

time: 719 us -> 549 us (0.76)
  waiting for transfers between devices: 194 us -> 43.5 us
  Pallas kernels: 396 us -> 457 us
  starting transfers between devices: 49 us -> 6.66 us
  other arithmetic: 38.9 us -> 13.2 us
  local copies, waits for them, and re-layouts: 30 us -> 18.2 us
    ppermute x49 -> x2, waiting for transfers between devices: 191 us -> 15.7 us  [trade(): return (mine, lax.ppermute(other, 'seq', across))]
    pallas_call x14 -> x15, Pallas kernels: 264 us -> 325 us  [the longest x2 165 us: attend_back_call(): pl.pallas_call(functools.partial(attend_back_kernel, chunk=min(256, t), s...]
    ppermute x49 -> x2, starting transfers between devices: 46 us -> 4.76 us  [trade(): return (mine, lax.ppermute(other, 'seq', across))]
    ppermute x2, waiting for transfers between devices: 0.01 us -> 22.1 us  [trade_back(): got = lax.ppermute(held[genes:].astype(BF), 'seq', across).astype(F32)]
    convert_element_type x29 -> x0, other arithmetic: 21.6 us -> none  [the longest x19 21.2 us: run(): sum((t.astype(F32) for t in kept)).astype(dtype)]
  transfers between devices with their start and end apart: 53 -> 6, of which waited for: 23 -> 5; matrix products, arithmetic and copies ran while one was open for 9% -> 3% of each run, Pallas kernels for 25% -> 11%
where the time goes in v2:
time: 549 us; the launch traced here: 540 us
  Pallas kernels  457 us (83%)
  waiting for transfers between devices  43.5 us (8%)
  local copies, waits for them, and re-layouts  18.2 us (3%)
  other arithmetic  13.2 us (2%)
  starting transfers between devices  6.66 us (1%)
    pallas_call x2, Pallas kernels, attend_back_call(): pl.pallas_call(functools.partial(attend_back_kernel, chunk=min(256, t), s...  165 us
    pallas_call x10, Pallas kernels, kernel_call(): pl.pallas_call(body, in_specs=list(in_specs) + extra, **kwargs)  110 us
    pallas_call x2, Pallas kernels, attend_call(): pl.pallas_call(functools.partial(attend_kernel, chunk=min(256, t)), grid=...  59.1 us
    pallas_call x2, Pallas kernels, forward_call(): pl.pallas_call(functools.partial(forward_kernel, layer=layer, cut=512), g...  56 us
    pallas_call x1, Pallas kernels, sums_call(): pl.pallas_call(functools.partial(sums_kernel, sums=sums), grid=(1,), in_s...  27.6 us
    ppermute x2, waiting for transfers between devices, trade_back(): got = lax.ppermute(held[genes:].astype(BF), 'seq', across).astype(F32)  22.1 us
    pallas_call x2, Pallas kernels, joined_back_call(): pl.pallas_call(joined_back_kernel, in_specs=[tok, pl.BlockSpec((2, tile,...  21.5 us
    pallas_call x2, Pallas kernels, first_call(): pl.pallas_call(first_kernel, grid=(t // tile,), in_specs=[pl.BlockSpec((t...  17.2 us
  transfers between devices with their start and end apart: 6, of which 5 were waited for; matrix products, arithmetic and copies ran while one was open for 3% of the time, Pallas kernels for 11%

profile of v2, /device:TPU:0, one launch (start us, length us, event | category | flops | bytes accessed | tf_op | source)
XLA Modules:
  0.0 539.9 jit_solution(8522660981432471524)
XLA Ops:
  0.7 1.5 dynamic-slice_bitcast_fusion.3
  2.2 3.0 collective-permute-start
  7.0 15.7 %collective-permute-done = bf16[512,768]{1,0:T(8,128)(2,1)S(1)} collective-permute-done((bf16[512,768]{1,0:T(8,128)(2,1)S(1)}, bf16[512,768]{1,0:T(8,128)(2,1)S(1)}, u32[]{:S(2)}, u32[]{:S(2)}) %collective-permute-start) | collective-permute-done | bytes 786464 | tf_op jit(solution)/shard_map/ppermute | solution.py:795
  22.7 1.2 pad_maximum_fusion.x
  24.0 8.3 %norm_qkv.2 = (bf16[1024,768]{1,0:T(8,128)(2,1)}, bf16[1024,768]{1,0:T(8,128)(2,1)}, bf16[2,1024,768]{2,1,0:T(8,128)(2,1)}) custom-call(bf16[1024,768]{1,0:T(8,128)(2,1)} %pad_maximum_fusion.x, f32[2,1,768]{2,1,0:T(1,128)} %broadcast_in_dim.28.gain, f32[2,1,768]{2,1,0:T(1,128)} %broadcast_in_dim.29.bias, bf16[2,768,2304]{2,1,0:T(8,128)(2,1)} %weight.7, ...), custom_call_target="tpu_custom_call" | custom-call | flops 9200000000 | tf_op jit(solution)/shard_map/norm_qkv/pallas_call | solution.py:94
  35.3 2.8 collective-permute-done.1.kvo.refs_2_
  38.1 1.7 copy-done.23
  39.8 29.5 %attend.2 = (bf16[1024,768]{1,0:T(8,128)(2,1)}, f32[6,8,1024]{2,1,0:T(8,128)}) custom-call(bf16[1024,768]{1,0:T(8,128)(2,1)} %get-tuple-element.85.q.refs_0_, bf16[2,1024,768]{2,1,0:T(8,128)(2,1)} %get-tuple-element.86.kv.refs_1_, bf16[2,1024,768]{2,1,0:T(8,128)(2,1)} %copy-done.23), custom_call_target="tpu_custom_call" | custom-call | flops 32000000000 | tf_op jit(solution)/shard_map/attend/pallas_call | solution.py:173
  69.3 27.9 %feed_forward.2 = (f32[1024,768]{1,0:T(8,128)}, bf16[1024,768]{1,0:T(8,128)(2,1)}, bf16[1024,3072]{1,0:T(8,128)(2,1)}, bf16[1024,3072]{1,0:T(8,128)(2,1)}, f32[1024,768]{1,0:T(8,128)}) custom-call(bf16[1024,768]{1,0:T(8,128)(2,1)} %get-tuple-element.87.att.refs_1_.refs_4_, bf16[1024,768]{1,0:T(8,128)(2,1)} %pad_maximum_fusion.x, ...), custom_call_target="tpu_custom_call" | custom-call | flops 30000001024 | tf_op jit(solution)/shard_map/feed_forward/pallas_call | solution.py:521
  97.2 8.9 %norm_qkv.3 = (bf16[1024,768]{1,0:T(8,128)(2,1)}, bf16[1024,768]{1,0:T(8,128)(2,1)}, bf16[2,1024,768]{2,1,0:T(8,128)(2,1)}) custom-call(f32[1024,768]{1,0:T(8,128)} %get-tuple-element.88.x, f32[2,1,768]{2,1,0:T(1,128)} %broadcast_in_dim.28.gain, f32[2,1,768]{2,1,0:T(1,128)} %broadcast_in_dim.29.bias, bf16[2,768,2304]{2,1,0:T(8,128)(2,1)} %weight.7, ...), custom_call_target="tpu_custom_call" | custom-call | flops 9200000000 | tf_op jit(solution)/shard_map/norm_qkv/pallas_call | solution.py:94
  106.5 1.0 dynamic-slice_bitcast_fusion
  107.6 1.8 collective-permute-start.4
  109.3 2.8 collective-permute-done.2.kvo.refs_2_
  112.2 29.5 %attend.3 = (bf16[1024,768]{1,0:T(8,128)(2,1)}, f32[6,8,1024]{2,1,0:T(8,128)}) custom-call(bf16[1024,768]{1,0:T(8,128)(2,1)} %get-tuple-element.89.q.refs_0_, bf16[2,1024,768]{2,1,0:T(8,128)(2,1)} %get-tuple-element.90.kv.refs_1_, bf16[2,1024,768]{2,1,0:T(8,128)(2,1)} %collective-permute-done.2.kvo.refs_2_), custom_call_target="tpu_custom_call" | custom-call | flops 32000000000 | tf_op jit(solution)/shard_map/attend/pallas_call | solution.py:173
  141.7 28.1 %feed_forward.3 = (f32[1024,768]{1,0:T(8,128)}, bf16[1024,768]{1,0:T(8,128)(2,1)}, bf16[1024,3072]{1,0:T(8,128)(2,1)}, bf16[1024,3072]{1,0:T(8,128)(2,1)}, f32[1024,768]{1,0:T(8,128)}) custom-call(bf16[1024,768]{1,0:T(8,128)(2,1)} %get-tuple-element.91.att.refs_1_.refs_4_, f32[1024,768]{1,0:T(8,128)} %get-tuple-element.88.x, bf16[2,768,768]{2,1,0:T(8,128)(2,1)} %refs_4_.3, ...), custom_call_target="tpu_custom_call" | custom-call | flops 30000001024 | tf_op jit(solution)/shard_map/feed_forward/pallas_call | solution.py:521
  169.8 0.9 copy-done.24
  170.7 23.5 %feed_forward_back.2 = (bf16[1024,768]{1,0:T(8,128)(2,1)}, bf16[1024,3072]{1,0:T(8,128)(2,1)}, f32[1024,768]{1,0:T(8,128)}, bf16[1024,768]{1,0:T(8,128)(2,1)}, b...) custom-call(bf16[512,768]{1,0:T(8,128)(2,1)} %get-tuple-element.173.refs_0_, ...), custom_call_target="tpu_custom_call" | custom-call | flops 25999998976 | tf_op jit(solution)/shard_map/feed_forward_back/pallas_call | solution.py:69
  194.2 4.4 weight_grad.8
  198.7 9.5 %weight_grad.10 = (bf16[1536,768]{1,0:T(8,128)(2,1)}, bf16[1536,768]{1,0:T(8,128)(2,1)}) custom-call(s32[1]{0:T(128)} %bitcast.7.refs_0_, bf16[1024,3072]{1,0:T(8,128)(2,1)} %get-tuple-element.104.refs_1_, bf16[1024,768]{1,0:T(8,128)(2,1)} %get-tuple-element.105.refs_2_), custom_call_target="tpu_custom_call" | custom-call | flops 8214125056 | tf_op jit(solution)/shard_map/weight_grad/pallas_call | solution.py:69
  208.1 9.7 %weight_grad.9 = (bf16[384,3072]{1,0:T(8,128)(2,1)}, bf16[384,3072]{1,0:T(8,128)(2,1)}) custom-call(s32[1]{0:T(128)} %bitcast.7.refs_0_, bf16[1024,768]{1,0:T(8,128)(2,1)} %get-tuple-element.100.refs_1_, bf16[1024,3072]{1,0:T(8,128)(2,1)} %get-tuple-element.101.refs_2_), custom_call_target="tpu_custom_call" | custom-call | flops 8214125056 | tf_op jit(solution)/shard_map/weight_grad/pallas_call | solution.py:69
  217.9 77.4 %attend_back.2 = (bf16[1024,768]{1,0:T(8,128)(2,1)}, bf16[2,1024,768]{2,1,0:T(8,128)(2,1)}, bf16[6,2,1024,128]{3,2,1,0:T(8,128)(2,1)}, f32[24,768]{1,0:T(8,128)}, f32[24,3072]{1,0:T(8,128)}, /*index=5*/f32[96,768]{1,0:T(8,128)}) custom-call(bf16[1024,768]{1,0:T(8,128)(2,1)} %get-tuple-element.89.q.refs_0_, ...), custom_call_target="tpu_custom_call" | custom-call | flops 73999998976 | tf_op jit(solution)/shard_map/attend_back/pallas_call | solution.py:419
  295.3 10.9 %joined_back.2 = (bf16[1024,2304]{1,0:T(8,128)(2,1)}, f32[1024,768]{1,0:T(8,128)}, f32[8,768]{1,0:T(8,128)}) custom-call(bf16[1024,768]{1,0:T(8,128)(2,1)} %get-tuple-element.108.dq, bf16[2,1024,768]{2,1,0:T(8,128)(2,1)} %get-tuple-element.109.dkv, bf16[6,2,1024,128]{3,2,1,0:T(8,128)(2,1)} %get-tuple-element.110.dkvi, f32[1024,768]{1,0:T(8,128)} %get-tuple-element.88.x, ...), custom_call_target="tpu_custom_call" | custom-call | flops 12000000000 | tf_op jit(solution)/shard_map/joined_back/pallas_call | solution.py:681
  306.2 23.8 %feed_forward_back.3 = (bf16[1024,768]{1,0:T(8,128)(2,1)}, bf16[1024,3072]{1,0:T(8,128)(2,1)}, f32[1024,768]{1,0:T(8,128)}, bf16[1024,768]{1,0:T(8,128)(2,1)}, b...) custom-call(f32[1024,768]{1,0:T(8,128)} %get-tuple-element.112.refs_0_.refs_1_, ...), custom_call_target="tpu_custom_call" | custom-call | flops 25999998976 | tf_op jit(solution)/shard_map/feed_forward_back/pallas_call | solution.py:69
  330.0 1.0 slice_reduce_fusion
  331.1 4.4 weight_grad.12
  335.6 9.5 %weight_grad.14 = (bf16[1536,768]{1,0:T(8,128)(2,1)}, bf16[1536,768]{1,0:T(8,128)(2,1)}) custom-call(s32[1]{0:T(128)} %bitcast.7.refs_0_, bf16[1024,3072]{1,0:T(8,128)(2,1)} %get-tuple-element.128.refs_1_, bf16[1024,768]{1,0:T(8,128)(2,1)} %get-tuple-element.129.refs_2_), custom_call_target="tpu_custom_call" | custom-call | flops 8214125056 | tf_op jit(solution)/shard_map/weight_grad/pallas_call | solution.py:69
  345.1 9.6 %weight_grad.13 = (bf16[384,3072]{1,0:T(8,128)(2,1)}, bf16[384,3072]{1,0:T(8,128)(2,1)}) custom-call(s32[1]{0:T(128)} %bitcast.7.refs_0_, bf16[1024,768]{1,0:T(8,128)(2,1)} %get-tuple-element.124.refs_1_, bf16[1024,3072]{1,0:T(8,128)(2,1)} %get-tuple-element.125.refs_2_), custom_call_target="tpu_custom_call" | custom-call | flops 8214125056 | tf_op jit(solution)/shard_map/weight_grad/pallas_call | solution.py:69
  354.7 7.9 %weight_grad.11 = (bf16[384,2304]{1,0:T(8,128)(2,1)}, bf16[384,2304]{1,0:T(8,128)(2,1)}) custom-call(s32[1]{0:T(128)} %bitcast.7.refs_0_, bf16[1024,768]{1,0:T(8,128)(2,1)} %get-tuple-element.117.refs_1_, bf16[1024,2304]{1,0:T(8,128)(2,1)} %get-tuple-element.118.refs_2_), custom_call_target="tpu_custom_call" | custom-call | flops 6160593920 | tf_op jit(solution)/shard_map/weight_grad/pallas_call | solution.py:69
  362.6 87.8 %attend_back.3 = (bf16[1024,768]{1,0:T(8,128)(2,1)}, bf16[2,1024,768]{2,1,0:T(8,128)(2,1)}, bf16[6,2,1024,128]{3,2,1,0:T(8,128)(2,1)}, f32[24,2304]{1,0:T(8,128)...) custom-call(bf16[1024,768]{1,0:T(8,128)(2,1)} %get-tuple-element.85.q.refs_0_, ...), custom_call_target="tpu_custom_call" | custom-call | flops 73999998976 | tf_op jit(solution)/shard_map/attend_back/pallas_call | solution.py:419
  450.4 10.6 %joined_back.3 = (bf16[1024,2304]{1,0:T(8,128)(2,1)}, f32[1024,768]{1,0:T(8,128)}, f32[8,768]{1,0:T(8,128)}) custom-call(bf16[1024,768]{1,0:T(8,128)(2,1)} %get-tuple-element.132.dq, bf16[2,1024,768]{2,1,0:T(8,128)(2,1)} %get-tuple-element.133.dkv, bf16[6,2,1024,128]{3,2,1,0:T(8,128)(2,1)} %get-tuple-element.134.dkvi, bf16[1024,768]{1,0:T(8,128)(2,1)} %pad_maximum_fusion.x, ...), custom_call_target="tpu_custom_call" | custom-call | flops 12000000000 | tf_op jit(solution)/shard_map/joined_back/pallas_call | solution.py:681
  461.0 0.9 slice_reduce_fusion.5
  463.6 7.9 %weight_grad.15 = (bf16[384,2304]{1,0:T(8,128)(2,1)}, bf16[384,2304]{1,0:T(8,128)(2,1)}) custom-call(s32[1]{0:T(128)} %bitcast.7.refs_0_, bf16[1024,768]{1,0:T(8,128)(2,1)} %get-tuple-element.137.refs_1_, bf16[1024,2304]{1,0:T(8,128)(2,1)} %get-tuple-element.138.refs_2_), custom_call_target="tpu_custom_call" | custom-call | flops 6160593920 | tf_op jit(solution)/shard_map/weight_grad/pallas_call | solution.py:69
  471.6 0.7 constant_dynamic-slice_fusion
  472.2 27.6 %sums.1 = (f32[24,2304]{1,0:T(8,128)}, f32[8,128]{1,0:T(8,128)}) custom-call(bf16[2,2,2,2,24,2304]{5,4,3,2,1,0:T(8,128)(2,1)} %bitcast.106, bf16[2,2,2,2,24,2304]{5,4,3,2,1,0:T(8,128)(2,1)} %bitcast.107, f32[2,2,2,2,8,128]{5,4,3,2,1,0:T(8,128)} %bitcast.92, f32[2,2,2,2,8,128]{5,4,3,2,1,0:T(8,128)} %bitcast.91), custom_call_target="tpu_custom_call" | custom-call | flops 30000001024 | tf_op jit(solution)/shard_map/sums/pallas_call | solution.py:449
  499.8 1.2 slice_bitcast_fusion.3
  501.0 0.8 slice_bitcast_fusion.5
  501.8 0.8 slice_bitcast_fusion.13
  502.9 0.8 collective-permute-start.5
  503.8 0.8 copy-done
  504.6 0.8 collective-permute-start.3
  506.1 0.9 pad_maximum_fusion.2
  507.5 0.9 pad_maximum_fusion.1
  510.1 0.7 pad_maximum_fusion.4
  511.9 0.8 pad_maximum_fusion.3
  513.4 10.1 %collective-permute-done.5 = bf16[512,768]{1,0:T(8,128)(2,1)S(1)} collective-permute-done((bf16[512,768]{1,0:T(8,128)(2,1)S(1)}, bf16[512,768]{1,0:T(8,128)(2,1)S(1)}, u32[]{:S(2)}, u32[]{:S(2)}) %collective-permute-start.5) | collective-permute-done | bytes 786464 | tf_op jit(solution)/shard_map/ppermute | solution.py:799
  523.6 1.9 maximum_select_fusion.1
  525.5 12.0 %collective-permute-done.3 = bf16[512,768]{1,0:T(8,128)(2,1)S(1)} collective-permute-done((bf16[512,768]{1,0:T(8,128)(2,1)S(1)}, bf16[512,768]{1,0:T(8,128)(2,1)S(1)}, u32[]{:S(2)}, u32[]{:S(2)}) %collective-permute-start.3) | collective-permute-done | bytes 786464 | tf_op jit(solution)/shard_map/ppermute | solution.py:799
  537.6 1.9 maximum_select_fusion
  (103 shorter events, 12.2 us)
Async XLA Ops:
  0.6 4.6 copy-start.12
  0.7 5.2 copy-start.16
  0.7 5.8 %copy-start.17 = (f32[2,768]{1,0:T(2,128)S(1)}, f32[2,768]{1,0:T(2,128)}, u32[]{:S(2)}) copy-start(f32[2,768]{1,0:T(2,128)} %param.17) | copy-start | bytes 18436
  2.2 20.5 %collective-permute-start = (bf16[512,768]{1,0:T(8,128)(2,1)S(1)}, bf16[512,768]{1,0:T(8,128)(2,1)S(1)}, u32[]{:S(2)}, u32[]{:S(2)}) collective-permute-start(bf16[512,768]{1,0:T(8,128)(2,1)S(1)} %get-tuple-element.175), channel_id=1, source_target_pairs={{0,2},{1,3},{2,0},{3,1},{4,6},{5,7},{6,4},{7,5},{8,10},{9,11},{10,... | collective-permute-start | bytes 2359304 | tf_op jit(solution)/shard_map/ppermute | solution.py:795
  24.0 8.3 %copy-start.18 = (f32[2,768]{1,0:T(2,128)S(1)}, f32[2,768]{1,0:T(2,128)}, u32[]{:S(2)}) copy-start(f32[2,768]{1,0:T(2,128)} %param.22) | copy-start | bytes 18436
  24.0 8.9 %copy-start.11 = (f32[2,3072]{1,0:T(2,128)S(1)}, f32[2,3072]{1,0:T(2,128)}, u32[]{:S(2)}) copy-start(f32[2,3072]{1,0:T(2,128)} %param.25) | copy-start | bytes 73732
  24.0 9.5 %copy-start.19 = (f32[2,768]{1,0:T(2,128)S(1)}, f32[2,768]{1,0:T(2,128)}, u32[]{:S(2)}) copy-start(f32[2,768]{1,0:T(2,128)} %param.21) | copy-start | bytes 18436
  24.0 10.1 %copy-start.20 = (f32[2,768]{1,0:T(2,128)S(1)}, f32[2,768]{1,0:T(2,128)}, u32[]{:S(2)}) copy-start(f32[2,768]{1,0:T(2,128)} %param.23) | copy-start | bytes 18436
  24.0 10.7 %copy-start.21 = (f32[2,768]{1,0:T(2,128)S(1)}, f32[2,768]{1,0:T(2,128)}, u32[]{:S(2)}) copy-start(f32[2,768]{1,0:T(2,128)} %param.27) | copy-start | bytes 18436
  32.2 5.9 %collective-permute-start.1 = (bf16[2,1024,768]{2,1,0:T(8,128)(2,1)}, bf16[2,1024,768]{2,1,0:T(8,128)(2,1)S(1)}, u32[]{:S(2)}, u32[]{:S(2)}) collective-permute-start(bf16[2,1024,768]{2,1,0:T(8,128)(2,1)} %get-tuple-element.86.kv.refs_1_), channel_id=1, source_target_pairs={{0,1},{1,0},{2,3},{3,2},{4,5},{5,4},{6,7},{7,6},{8,9},{9,8},{10,11... | collective-permute-start | bytes 9437192 | tf_op jit(solution)/shard_map/ppermute | solution.py:818
  38.1 1.7 copy-start.23
  97.2 9.1 %copy-start.22 = (s32[2,512]{1,0:T(2,128)S(1)}, s32[2,512]{1,0:T(2,128)}, u32[]{:S(2)}) copy-start(s32[2,512]{1,0:T(2,128)} %param.29) | copy-start | bytes 12292
  97.2 9.1 %copy-start.2 = (bf16[2,512,768]{2,1,0:T(8,128)(2,1)S(1)}, bf16[2,512,768]{2,1,0:T(8,128)(2,1)}, u32[]{:S(2)}) copy-start(bf16[2,512,768]{2,1,0:T(8,128)(2,1)} %param.28) | copy-start | bytes 4718596
  106.1 6.1 %collective-permute-start.2 = (bf16[2,1024,768]{2,1,0:T(8,128)(2,1)}, bf16[2,1024,768]{2,1,0:T(8,128)(2,1)}, u32[]{:S(2)}, u32[]{:S(2)}) collective-permute-start(bf16[2,1024,768]{2,1,0:T(8,128)(2,1)} %get-tuple-element.90.kv.refs_1_), channel_id=1, source_target_pairs={{0,1},{1,0},{2,3},{3,2},{4,5},{5,4},{6,7},{7,6},{8,9},{9,8},{10,11... | collective-permute-start | bytes 9437192 | tf_op jit(solution)/shard_map/ppermute | solution.py:818
  107.6 62.3 %collective-permute-start.4 = (bf16[512,768]{1,0:T(8,128)(2,1)S(1)}, bf16[512,768]{1,0:T(8,128)(2,1)S(1)}, u32[]{:S(2)}, u32[]{:S(2)}) collective-permute-start(bf16[512,768]{1,0:T(8,128)(2,1)S(1)} %get-tuple-element.172), channel_id=1, source_target_pairs={{0,2},{1,3},{2,0},{3,1},{4,6},{5,7},{6,4},{7,5},{8,10},{9,11},{10,... | collective-permute-start | bytes 2359304 | tf_op jit(solution)/shard_map/ppermute | solution.py:795
  169.8 0.9 copy-start.24
  450.4 11.7 %copy-start.15 = (f32[8,768]{1,0:T(8,128)S(1)}, f32[8,768]{1,0:T(8,128)}, u32[]{:S(2)}) copy-start(f32[8,768]{1,0:T(8,128)} %get-tuple-element.143) | copy-start | bytes 73732
  450.4 12.0 %copy-start.14 = (f32[8,768]{1,0:T(8,128)S(1)}, f32[8,768]{1,0:T(8,128)}, u32[]{:S(2)}) copy-start(f32[8,768]{1,0:T(8,128)} %get-tuple-element.142) | copy-start | bytes 73732
  450.4 12.6 %copy-start.13 = (f32[8,768]{1,0:T(8,128)S(1)}, f32[8,768]{1,0:T(8,128)}, u32[]{:S(2)}) copy-start(f32[8,768]{1,0:T(8,128)} %get-tuple-element.144) | copy-start | bytes 73732
  472.2 30.4 %copy-start.1 = (f32[1024,768]{1,0:T(8,128)S(1)}, f32[1024,768]{1,0:T(8,128)}, u32[]{:S(2)}) copy-start(f32[1024,768]{1,0:T(8,128)} %get-tuple-element.136) | copy-start | bytes 9437188
  502.7 1.9 copy-start
  502.7 3.3 copy-start.4
  502.8 3.3 copy-start.6
  502.8 4.7 copy-start.3
  502.8 4.7 copy-start.5
  502.9 7.2 %copy-start.9 = (f32[24,768]{1,0:T(8,128)S(1)}, f32[24,768]{1,0:T(8,128)}, u32[]{:S(2)}) copy-start(f32[24,768]{1,0:T(8,128)} %get-tuple-element.151) | copy-start | bytes 221188
  502.9 7.1 %copy-start.10 = (f32[24,768]{1,0:T(8,128)S(1)}, f32[24,768]{1,0:T(8,128)}, u32[]{:S(2)}) copy-start(f32[24,768]{1,0:T(8,128)} %get-tuple-element.150) | copy-start | bytes 221188
  502.9 9.0 %copy-start.7 = (f32[24,2304]{1,0:T(8,128)S(1)}, f32[24,2304]{1,0:T(8,128)}, u32[]{:S(2)}) copy-start(f32[24,2304]{1,0:T(8,128)} %get-tuple-element.149) | copy-start | bytes 663556
  502.9 8.9 %copy-start.8 = (f32[24,2304]{1,0:T(8,128)S(1)}, f32[24,2304]{1,0:T(8,128)}, u32[]{:S(2)}) copy-start(f32[24,2304]{1,0:T(8,128)} %get-tuple-element.148) | copy-start | bytes 663556
  502.9 20.5 %collective-permute-start.5 = (bf16[512,768]{1,0:T(8,128)(2,1)S(1)}, bf16[512,768]{1,0:T(8,128)(2,1)S(1)}, u32[]{:S(2)}, u32[]{:S(2)}) collective-permute-start(bf16[512,768]{1,0:T(8,128)(2,1)S(1)} %slice.202), channel_id=1, source_target_pairs={{0,2},{1,3},{2,0},{3,1},{4,6},{5,7},{6,4},{7,5},{8,10},{9,11},{10,... | collective-permute-start | bytes 2359304 | tf_op jit(solution)/shard_map/ppermute | solution.py:799
  504.6 32.8 %collective-permute-start.3 = (bf16[512,768]{1,0:T(8,128)(2,1)S(1)}, bf16[512,768]{1,0:T(8,128)(2,1)S(1)}, u32[]{:S(2)}, u32[]{:S(2)}) collective-permute-start(bf16[512,768]{1,0:T(8,128)(2,1)S(1)} %slice.203), channel_id=1, source_target_pairs={{0,2},{1,3},{2,0},{3,1},{4,6},{5,7},{6,4},{7,5},{8,10},{9,11},{10,... | collective-permute-start | bytes 2359304 | tf_op jit(solution)/shard_map/ppermute | solution.py:799

commit v3 on v2

v3 whole, which is shorter than its diff:
```python
import functools

import jax
import jax.numpy as jnp
from jax import lax
from jax.experimental import pallas as pl
from jax.experimental.pallas import tpu as pltpu
from jax.sharding import PartitionSpec as P

HEAD = 64
LOG2E = 1.4426950408889634
BF = jnp.bfloat16
F32 = jnp.float32
NN = ((1,), (0,))
NT = ((1,), (1,))
SAFE = 80.0
BLOCK = 256
SLOTS = (0, 2, 6, 8, 10)


class _Names:
    def __getattr__(self, word):
        return word


N = _Names()


def tag(word, *numbers):
    return N._.join([word, *map(str, numbers)])


def dot(a, b, dims):
    return lax.dot_general(a, b, (dims, ((), ())), preferred_element_type=F32)


def params(mib):
    return pltpu.CompilerParams(vmem_limit_bytes=mib << 20)


def cost(products, nbytes=0):
    return pl.CostEstimate(flops=int(2 * products), bytes_accessed=int(nbytes), transcendentals=0)


def normalise(x):
    n = x.shape[-1]
    centred = x - jnp.sum(x, axis=-1, keepdims=True) * (1.0 / n)
    inverse = lax.rsqrt(jnp.sum(centred * centred, axis=-1, keepdims=True) * (1.0 / n) + 1e-05)
    return centred * inverse, inverse


def norm_back(upstream, gain, unit, inverse):
    n = unit.shape[-1]
    e = upstream * gain
    mean_e = jnp.sum(e, axis=-1, keepdims=True) * (1.0 / n)
    mean_eu = jnp.sum(e * unit, axis=-1, keepdims=True) * (1.0 / n)
    return inverse * (e - mean_e - unit * mean_eu)


def column_sum(x):
    return jnp.sum(x, axis=0, keepdims=True)


def gelu_pair(x):
    cdf = 0.5 + 0.5 * lax.erf(x * 0.7071067811865476)
    slope = jnp.exp2(x * x * (-0.5 * LOG2E)) * 0.3989422804014327
    return x * cdf, cdf + x * slope


def kernel_call(kernel, ins, in_specs, after=(), **kwargs):
    n = len(ins)
    extra = [pl.BlockSpec(memory_space=pl.ANY)] * len(after)

    def body(*refs):
        kernel(*refs[:n], *refs[n + len(after) :])

    return pl.pallas_call(body, in_specs=list(in_specs) + extra, **kwargs)(*ins, *after)


def qkv_kernel(*refs, names, layer, block, count, trading):
    r = dict(zip(names, refs))
    t, d = r[N.x_v].shape
    spans = [slice(i, i + block) for i in range(0, t, block)]
    half = len(spans) // 2
    place = Place(count)
    row = slice(layer, layer + 1)
    copies = Copies(r[N.sems])
    for k in range(3):
        cols = slice(k * d, (k + 1) * d)
        copies.add((N.weight, k), r[N.weight].at[layer, :, cols], r[N.weight_v].at[k])
    chip = place.bit(1)
    for i, at in enumerate(spans):
        if not trading:
            copies.add((N.x, i), r[N.x].at[at], r[N.x_v].at[at])
        elif i < half:
            copies.add((N.x, i), r[N.x].at[chip, at], r[N.x_v].at[at])
        if trading:
            copies.add((N.held, i), r[N.x_v].at[at], r[N.held].at[at])
        copies.add((N.normed, i), r[N.normed_v].at[at], r[N.normed].at[at])
        copies.add((N.q, i), r[N.q_v].at[at], r[N.q].at[at])
        copies.add((N.kv, i), r[N.kv_v].at[:, at], r[N.kv].at[:, at])

    def remote(src, dst, i, bit):
        return pltpu.make_async_remote_copy(
            src_ref=src,
            dst_ref=dst,
            send_sem=r[N.far_sems].at[0, i],
            recv_sem=r[N.far_sems].at[1, i],
            device_id=place.partner(bit),
            device_id_type=pl.DeviceIdType.MESH,
        )

    if trading:
        for i, cell in enumerate((chip, 1 - chip)):
            copies.add((N.seed, i), r[N.cotangent].at[cell], r[N.seed_v].at[i])
            copies.add((N.seeded, i), r[N.seed_v].at[i], r[N.seed_own if i == 0 else N.seed_send])

    def parcel(i):
        return remote(r[N.kv_v].at[:, spans[i]], r[N.kvo].at[:, spans[i]], i, 0)

    def trade():
        return remote(r[N.x].at[1 - chip], r[N.x_v].at[t // 2 :], len(spans), 1)

    for i in range(half if trading else len(spans)):
        copies.start(N.x, i)
        if i == 0:
            for k in (1, 2, 0):
                copies.start(N.weight, k)
    place.greet(2)
    if trading:
        trade().start()
        for i in range(2):
            copies.start(N.seed, i)
    waited = set()

    def weight(k):
        if k not in waited:
            copies.wait(N.weight, k)
            waited.add(k)
        return r[N.weight_v][k]

    for group in (range(half), range(half, len(spans))):
        if trading and group.start:
            masks = jnp.broadcast_to(r[N.mask][...].astype(F32)[:, None, :], (2, 8, t // 2))
            for i in range(2):
                mask = jnp.where(chip == i, masks[0], masks[1])
                copies.wait(N.seed, i)
                r[N.seed_v][i] = r[N.seed_v][i] * mask.T[:, :1].astype(BF)
                copies.start(N.seeded, i)
            trade().wait()
        for i in group:
            at = spans[i]
            if not trading or i < half:
                copies.wait(N.x, i)
            if trading:
                copies.start(N.held, i)
            unit, _ = normalise(r[N.x_v][at].astype(F32))
            normed = (unit * r[N.gain][row, :] + r[N.bias][row, :]).astype(BF)
            r[N.normed_v][at] = normed
            copies.start(N.normed, i)
            r[N.kv_v][0, at] = dot(normed, weight(1), NN).astype(BF)
            r[N.kv_v][1, at] = (dot(normed, weight(2), NN) + r[N.qv_bias][row, d:]).astype(BF)
            parcel(i).start()
            copies.start(N.kv, i)
        if trading or group.start:
            for i in group if trading else range(len(spans)):
                at = spans[i]
                r[N.q_v][at] = (dot(r[N.normed_v][at], weight(0), NN) + r[N.qv_bias][row, :d]).astype(BF)
                copies.start(N.q, i)
    if trading:
        for i in range(2):
            copies.wait(N.seeded, i)
    for i in range(len(spans)):
        for name in (N.held, N.normed, N.q, N.kv) if trading else (N.normed, N.q, N.kv):
            copies.wait(name, i)
        parcel(i).wait()


def qkv_call(x, layer, devices, gain, bias, weight, qv_bias, collective_id, seeds=()):
    trading = x.ndim == 3
    d = x.shape[-1]
    t = x.size // d
    block = min(BLOCK, t // 2)
    blocks = t // block
    ins, outs, scratch = Names(), Names(), Names()
    hbm = pl.BlockSpec(memory_space=pl.ANY)
    ins.add(N.x, hbm)
    ins.add(N.weight, hbm)
    for name in (N.gain, N.bias, N.qv_bias):
        ins.add(name, pl.BlockSpec(memory_space=pltpu.VMEM))
    if trading:
        ins.add(N.cotangent, hbm)
        ins.add(N.mask, pl.BlockSpec(memory_space=pltpu.VMEM))
        outs.add(N.held, hbm, ((t, d), x.dtype))
        for name in (N.seed_own, N.seed_send):
            outs.add(name, hbm, ((t // 2, d), BF))
        scratch.add(N.seed_v, pltpu.VMEM((2, t // 2, d), BF))
    outs.add(N.normed, hbm, ((t, d), BF))
    outs.add(N.q, hbm, ((t, d), BF))
    outs.add(N.kv, hbm, ((2, t, d), BF))
    outs.add(N.kvo, hbm, ((2, t, d), BF))
    scratch.add(N.x_v, pltpu.VMEM((t, d), x.dtype))
    scratch.add(N.normed_v, pltpu.VMEM((t, d), BF))
    scratch.add(N.q_v, pltpu.VMEM((t, d), BF))
    scratch.add(N.kv_v, pltpu.VMEM((2, t, d), BF))
    scratch.add(N.weight_v, pltpu.VMEM((3, d, d), BF))
    scratch.add(N.sems, pltpu.SemaphoreType.DMA((7 + 5 * blocks,)))
    scratch.add(N.far_sems, pltpu.SemaphoreType.DMA((2, blocks + 1)))
    found = pl.pallas_call(
        functools.partial(
            qkv_kernel,
            names=ins.names + outs.names + scratch.names,
            layer=layer,
            block=block,
            count=devices,
            trading=trading,
        ),
        grid=(1,),
        in_specs=ins.specs,
        out_specs=outs.specs,
        out_shape=[jax.ShapeDtypeStruct(*shape) for shape in outs.shapes],
        scratch_shapes=scratch.specs,
        compiler_params=pltpu.CompilerParams(
            vmem_limit_bytes=62 << 20, collective_id=collective_id, has_side_effects=True
        ),
        cost_estimate=cost(12e9 if trading else 5e9),
        name=N.norm_qkv,
    )(x, weight, gain, bias, qv_bias, *seeds)
    return dict(zip(outs.names, found))


def attend_kernel(q, kv, kvo, out, lse, *, chunk):
    t = q.shape[0]
    c = LOG2E * HEAD**-0.5
    lane = lax.broadcasted_iota(jnp.int32, (128, 128), 0) // HEAD
    pick = (lane == lax.broadcasted_iota(jnp.int32, (128, 128), 1)).astype(BF)

    def squares(x):
        x = x.astype(F32)
        return jnp.max(dot((x * x).astype(BF), pick, NN), axis=0, keepdims=True)

    bound = squares(q[...]) * jnp.maximum(squares(kv[0]), squares(kvo[0]))
    fast = jnp.max(bound) * (c * c * 1.05) < SAFE * SAFE

    def run(stable):
        for head in range(2):
            ls = slice(HEAD * head, HEAD * head + HEAD)
            values = []
            for ref in (kv, kvo):
                v = ref[1, :, ls].astype(F32).T.astype(BF)
                values.append(jnp.concatenate([v, jnp.ones((16, t), BF)], axis=0))

            def score(j):
                block = q[j * chunk : (j + 1) * chunk, ls]
                return [dot(ref[0, :, ls], block, NT) for ref in (kv, kvo)]

            ahead = score(0)
            for j in range(t // chunk):
                s = ahead
                if j + 1 < t // chunk:
                    ahead = score(j + 1)
                if stable:
                    shift = c * jnp.maximum(
                        jnp.max(s[0], axis=0, keepdims=True), jnp.max(s[1], axis=0, keepdims=True)
                    )
                    p = [jnp.exp2(x * c - shift).astype(BF) for x in s]
                else:
                    shift = 0.0
                    p = [jnp.exp2(x * c).astype(BF) for x in s]
                total = dot(values[0], p[0], NN) + dot(values[1], p[1], NN)
                level = total[HEAD : HEAD + 1]
                cols = slice(j * chunk, (j + 1) * chunk)
                out[cols, ls] = (total[:HEAD] / level).T.astype(BF)
                lse[0, head : head + 1, cols] = shift + jnp.log2(level)

    pl.when(fast)(lambda: run(False))
    pl.when(jnp.logical_not(fast))(lambda: run(True))


def attend_call(q, kv, kvo):
    t, d = q.shape
    pairs = d // 128
    both = pl.BlockSpec((2, t, 128), lambda h: (0, 0, h))
    one = pl.BlockSpec((t, 128), lambda h: (0, h))
    return pl.pallas_call(
        functools.partial(attend_kernel, chunk=min(256, t)),
        grid=(pairs,),
        in_specs=[one, both, both],
        out_specs=[one, pl.BlockSpec((1, 8, t), lambda h: (h, 0, 0))],
        out_shape=[jax.ShapeDtypeStruct((t, d), BF), jax.ShapeDtypeStruct((pairs, 8, t), F32)],
        compiler_params=params(62),
        cost_estimate=cost(16e9),
        name=N.attend,
    )(q, kv, kvo)


class Place:
    def __init__(self, count):
        self.count = count
        self.bits = count.bit_length() - 1
        self.dp, self.seq = lax.axis_index(N.dp), lax.axis_index(N.seq)

    def bit(self, b):
        return (self.seq // (1 << b)) % 2 if b < 2 else (self.dp // (1 << (b - 2))) % 2

    def partner(self, b):
        step = 1 - 2 * self.bit(b)
        if b < 2:
            return {N.dp: self.dp, N.seq: self.seq + step * (1 << b)}
        return {N.dp: self.dp + step * (1 << (b - 2)), N.seq: self.seq}

    def greet(self, bits=None):
        bits = self.bits if bits is None else bits
        barrier = pltpu.get_barrier_semaphore()
        for b in range(bits):
            pl.semaphore_signal(barrier, inc=1, device_id=self.partner(b), device_id_type=pl.DeviceIdType.MESH)
        pl.semaphore_wait(barrier, bits)


class Job:
    def __init__(self, keep, send, count, orders, shape=None):
        self.lead = count.bit_length() - 2
        self.made = keep is None
        if not self.made:
            self.keep = keep.reshape((2,) * self.lead + keep.shape[1:])
            self.send = send.reshape((2,) * self.lead + send.shape[1:])
        self.rows, self.cols = shape or keep.shape[1:]
        self.orders = orders
        self.wide = self.cols // len(orders)
        self.dtype = BF

    def scratch(self):
        out = []
        for _ in self.orders:
            block = (self.rows, self.wide)
            out.append(pltpu.VMEM((2,) * self.lead + block, self.dtype))
            if self.made:
                out.append(pltpu.VMEM((2,) * self.lead + block, self.dtype))
            for left in range(self.lead, -1, -1):
                out.append(pltpu.VMEM((2,) * left + block, self.dtype))
        return out

    def out_shape(self):
        return jax.ShapeDtypeStruct((self.rows, self.cols), F32)


class Part:
    def __init__(self, place, job, at, keep, send, out, scratch, sems, first_sem):
        self.place, self.job, self.keep, self.send, self.out = place, job, keep, send, out
        self.order = job.orders[at]
        self.cols = slice(at * job.wide, (at + 1) * job.wide)
        self.total, self.got = scratch[0], scratch[1:]
        self.sems, self.first = sems, first_sem

    def fill(self, out, rows):
        lead = self.job.lead
        for core in range(2):

            @pl.when(self.place.bit(0) == core)
            def _(core=core):
                for at in range(2 << lead):
                    index = tuple((at >> (b + 1)) & 1 for b in reversed(range(lead)))
                    into = self.total if at % 2 == core else self.send
                    into[index] = out[at * rows : (at + 1) * rows].astype(BF)

    def own(self):
        return pltpu.make_async_copy(
            self.keep.at[(slice(None),) * (self.job.lead + 1) + (self.cols,)], self.total, self.sems.at[0, self.first]
        )

    def index(self, stage, away):
        out = []
        for b in range(self.job.lead, 0, -1):
            at = self.order.index(b) + 1
            if at < stage or (at == stage and not away):
                out.append(self.place.bit(b))
            elif at == stage:
                out.append(1 - self.place.bit(b))
            else:
                out.append(slice(None))
        return tuple(out)

    def copy(self, stage):
        if stage == 0 and self.keep is None:
            bit, src = 0, self.send
        elif stage == 0:
            bit, src = 0, self.send.at[(slice(None),) * (self.job.lead + 1) + (self.cols,)]
        else:
            bit, src = self.order[stage - 1], self.total.at[self.index(stage, True)]
        return pltpu.make_async_remote_copy(
            src_ref=src,
            dst_ref=self.got[stage],
            send_sem=self.sems.at[1, self.first + stage],
            recv_sem=self.sems.at[2, self.first + stage],
            device_id=self.place.partner(bit),
            device_id_type=pl.DeviceIdType.MESH,
        )

    def begin(self, stage):
        if stage == 0 and self.keep is not None:
            self.own().start()
        self.copy(stage).start()

    def end(self, stage):
        if stage == 0 and self.keep is not None:
            self.own().wait()
        self.copy(stage).wait()
        index = self.index(stage, False)
        if stage == len(self.order):
            self.out[:, self.cols] = self.total[index].astype(F32) + self.got[stage][...].astype(F32)
        elif stage == 0:
            self.total[...] = self.total[...] + self.got[0][...]
        else:
            self.total[index] = self.total[index] + self.got[stage][...]


class Trade:
    def __init__(self, place, src, dst, sems):
        self.ends = dict(src_ref=src, dst_ref=dst, send_sem=sems.at[0], recv_sem=sems.at[1])
        self.place = place

    def copy(self):
        return pltpu.make_async_remote_copy(
            **self.ends, device_id=self.place.partner(1), device_id_type=pl.DeviceIdType.MESH
        )


class Sums:
    def __init__(self, jobs, count, trade=None, trade_at=0):
        self.jobs, self.count, self.trade, self.trade_at = jobs, count, trade, trade_at
        self.stages = count.bit_length() - 1

    def n_ins(self):
        return 2 * sum(not job.made for job in self.jobs) + (self.trade is not None)

    def n_outs(self):
        return len(self.jobs) + (self.trade is not None)

    def inputs(self):
        return [x for job in self.jobs if not job.made for x in (job.keep, job.send)] + ([] if self.trade is None else [self.trade])

    def n_parts(self):
        return sum(len(job.orders) for job in self.jobs)

    def in_specs(self):
        return [pl.BlockSpec(memory_space=pl.ANY)] * self.n_ins()

    def out_shapes(self):
        out = [job.out_shape() for job in self.jobs]
        return out if self.trade is None else out + [jax.ShapeDtypeStruct(self.trade.shape, self.trade.dtype)]

    def out_specs(self):
        out = [pl.BlockSpec((job.rows, job.cols), lambda *_: (0, 0), pipeline_mode=pl.Buffered(1)) for job in self.jobs]
        return out if self.trade is None else out + [pl.BlockSpec(memory_space=pl.ANY)]

    def scratch(self):
        out = [x for job in self.jobs for x in job.scratch()]
        return out + [pltpu.SemaphoreType.DMA((3, self.n_parts() * self.stages)), pltpu.SemaphoreType.DMA((2,))]

    def parts(self, place, ins, outs, scratch):
        scratch = list(scratch)
        trade_sems = scratch.pop()
        sems = scratch.pop()
        found = []
        self.swap = None if self.trade is None else Trade(place, ins[-1], outs[-1], trade_sems)
        for i, job in enumerate(self.jobs):
            for at in range(len(job.orders)):
                size = job.lead + 2 + job.made
                mine, scratch = scratch[:size], scratch[size:]
                if job.made:
                    keep, send = None, mine.pop(1)
                else:
                    keep, send = ins[2 * i], ins[2 * i + 1]
                found.append(Part(place, job, at, keep, send, outs[i], mine, sems, len(found) * self.stages))
        return found

    def advance(self, parts, stage):
        for part in parts:
            if stage > 0:
                part.end(stage - 1)
            if stage < self.stages:
                part.begin(stage)
        if self.swap is not None:
            if stage == self.trade_at:
                self.swap.copy().start()
            if stage == self.stages:
                self.swap.copy().wait()


def attend_back_kernel(*refs, chunk, sums, slots):
    n_in, n_out = 6 + sums.n_ins(), 3 + sums.n_outs()
    q, kv, kvo, up, out, lse = refs[:6]
    dq, dkv, dkvi = refs[n_in : n_in + 3]
    outbox, box_sems = refs[n_in + n_out : n_in + n_out + 2]
    place = Place(sums.count)
    parts = sums.parts(place, refs[6:n_in], refs[n_in + 3 : n_in + n_out], refs[n_in + n_out + 2 :])
    t = q.shape[0]
    scale = HEAD**-0.5
    c = LOG2E * scale
    pair, pairs = pl.program_id(0), len(slots) // 2

    def parcel(at):
        return pltpu.make_async_remote_copy(
            src_ref=outbox.at[at % 2],
            dst_ref=dkvi.at[at],
            send_sem=box_sems.at[0, at],
            recv_sem=box_sems.at[1, at],
            device_id=place.partner(0),
            device_id_type=pl.DeviceIdType.MESH,
        )

    def advance(at):
        for stage in slots[at]:
            sums.advance(parts, stage)

    pl.when(pair == 0)(place.greet)
    for at in range(2, pairs):
        pl.when(pair == at)(lambda at=at: parcel(at - 2).wait_send())
    box = outbox.at[lax.rem(pair, 2)]
    for head in range(2):
        for at in range(pairs):
            if slots[2 * at + head]:
                pl.when(pair == at)(functools.partial(advance, 2 * at + head))
        ls = slice(HEAD * head, HEAD * head + HEAD)
        qh = q[:, ls]
        uh = up[:, ls]
        q_t = qh.astype(F32).T.astype(BF)
        u_t = uh.astype(F32).T.astype(BF)
        level = lse[0].T[:, head : head + 1]
        inner = jnp.sum(uh.astype(F32) * out[:, ls].astype(F32), axis=1, keepdims=True)
        blocks = [
            (src, dst, slice(i * chunk, (i + 1) * chunk))
            for src, dst in ((kvo, box), (kv, dkv))
            for i in range(t // chunk)
        ]

        def products(block):
            src, _, rows = block
            return dot(qh, src[0, rows, ls], NT), dot(uh, src[1, rows, ls], NT)

        total = None
        ahead = products(blocks[0])
        for at, (src, dst, rows) in enumerate(blocks):
            s, dp = ahead
            if at + 1 < len(blocks):
                ahead = products(blocks[at + 1])
            p = jnp.exp2(s * c - level)
            ds = (p * (dp - inner)).astype(BF)
            dst[1, rows, ls] = dot(u_t, p.astype(BF), NN).T.astype(BF)
            dst[0, rows, ls] = (dot(q_t, ds, NN).T * scale).astype(BF)
            part = dot(ds, src[0, rows, ls], NN)
            total = part if total is None else total + part
        dq[:, ls] = (total * scale).astype(BF)

    for at in range(pairs):

        @pl.when(pair == at)
        def _(at=at):
            parcel(at).start()
            if at == pairs - 1:
                advance(2 * pairs)
                for last in range(max(0, pairs - 2), pairs):
                    parcel(last).wait_send()
                for each in range(pairs):
                    parcel(each).wait_recv()


def attend_back_call(q, kv, kvo, up, out, lse, sums, collective_id):
    t, d = q.shape
    pairs = d // 128
    both = pl.BlockSpec((2, t, 128), lambda h: (0, 0, h))
    one = pl.BlockSpec((t, 128), lambda h: (0, h))
    slots = [[] for _ in range(2 * pairs + 1)]
    for stage in range(sums.stages + 1):
        slots[SLOTS[stage] if stage < min(len(SLOTS), sums.stages) else 2 * pairs].append(stage)
    return pl.pallas_call(
        functools.partial(attend_back_kernel, chunk=min(256, t), sums=sums, slots=slots),
        grid=(pairs,),
        in_specs=[one, both, both, one, one, pl.BlockSpec((1, 8, t), lambda h: (h, 0, 0))] + sums.in_specs(),
        out_specs=[one, both, pl.BlockSpec(memory_space=pl.ANY)] + sums.out_specs(),
        out_shape=[
            jax.ShapeDtypeStruct((t, d), BF),
            jax.ShapeDtypeStruct((2, t, d), BF),
            jax.ShapeDtypeStruct((pairs, 2, t, 128), BF),
        ]
        + sums.out_shapes(),
        scratch_shapes=[pltpu.VMEM((2, 2, t, 128), BF), pltpu.SemaphoreType.DMA((2, pairs))] + sums.scratch(),
        compiler_params=pltpu.CompilerParams(
            vmem_limit_bytes=60 << 20, collective_id=collective_id, has_side_effects=True
        ),
        cost_estimate=cost(37e9),
        name=N.attend_back,
    )(q, kv, kvo, up, out, lse, *sums.inputs())


def split_rows(out, rows):
    n = out.shape[0]
    even = jnp.concatenate([out[i : i + rows] for i in range(0, n, 2 * rows)], axis=0).astype(BF)
    odd = jnp.concatenate([out[i + rows : i + 2 * rows] for i in range(0, n, 2 * rows)], axis=0).astype(BF)
    return even, odd


def deliver(core, out, rows, keep, send):
    even, odd = split_rows(out, rows)

    @pl.when(core == 0)
    def _():
        keep[...] = even
        send[...] = odd

    @pl.when(core == 1)
    def _():
        keep[...] = odd
        send[...] = even


def grad_dot(a, b):
    return lax.dot_general(a, b, (((0,), (0,)), ((), ())), preferred_element_type=F32)


class Names:
    def __init__(self):
        self.names, self.specs, self.shapes = [], [], []

    def add(self, name, spec, shape=None):
        self.names.append(name)
        self.specs.append(spec)
        self.shapes.append(shape)


class Copies:
    def __init__(self, sems):
        self.sems, self.made = sems, {}

    def add(self, key, src, dst):
        self.made[key] = pltpu.make_async_copy(src, dst, self.sems.at[len(self.made)])

    def start(self, *key):
        self.made[key].start()

    def wait(self, *key):
        self.made[key].wait()


def ffn_kernel(*refs, names, forward, backward, block, chunks, sums):
    r = dict(zip(names, refs))
    if sums is not None:
        place = Place(sums.count)
        parts = sums.parts(
            place, *[[ref for name, ref in r.items() if name.startswith(kind)] for kind in (N.sum_i, N.sum_o, N.sum_s)]
        )
    layer = r[N.layer]
    row = slice(layer, layer + 1)
    j = pl.program_id(0)
    t, d = r[N.att_v].shape
    cut = r[N.wu_v].shape[2]
    count = r[N.wu_v].shape[0]
    first, final = j == 0, j == count - 1
    spans = [slice(i, i + block) for i in range(0, t, block)]
    every = range(len(spans))
    copies = Copies(r[N.sems])
    copies.add((N.wo,), r[N.wo].at[layer], r[N.wo_v])
    for i, at in enumerate(spans):
        copies.add((N.att, i), r[N.att].at[at], r[N.att_v].at[at])
        if forward:
            copies.add((N.x, i), r[N.x].at[at], r[N.x_v].at[at])
            if not backward:
                copies.add((N.next, i), r[N.next_v].at[at], r[N.next].at[at])
            elif at.start < r[N.next].shape[0]:
                copies.add((N.next, i), r[N.next_v].at[at], r[N.next].at[at])
            else:
                low = slice(at.start - r[N.next].shape[0], at.stop - r[N.next].shape[0])
                copies.add((N.next, i), r[N.dz_low].at[low], r[N.next_low].at[low])
            if not backward:
                copies.add((N.middle_o, i), r[N.middle_v].at[at], r[N.middle].at[at])
                copies.add((N.n2_o, i), r[N.n2_v].at[at], r[N.n2].at[at])
        else:
            copies.add((N.middle, i), r[N.middle].at[at], r[N.middle_v].at[at])
            copies.add((N.n2, i), r[N.n2].at[at], r[N.n2_v].at[at])
            copies.add((N.g, i), r[N.g].at[at], r[N.dm_v].at[at])
        if backward:
            copies.add((N.dm, i), r[N.dm_v].at[at], r[N.dm].at[at])
            copies.add((N.da, i), r[N.da_v].at[at], r[N.da].at[at])
    if backward:
        half = r[N.dza].shape[0]
        copies.add((N.dza,), r[N.dza], r[N.dz_v].at[:half])
        if half < t:
            copies.add((N.dzb,), r[N.dzb], r[N.dz_v].at[half:])
    for c in range(count):
        cols = slice(c * cut, (c + 1) * cut)
        copies.add((N.wu, c), r[N.wu].at[layer, :, cols], r[N.wu_v].at[c])
        copies.add((N.wd, c), r[N.wd].at[layer, cols, :], r[N.wd_v].at[c])
        if not (forward and backward):
            for name in (N.act, N.slope):
                for i, at in enumerate(spans):
                    ends = r[name].at[at, cols], r[name + N._v].at[c % 2, at]
                    copies.add((name, c, i), *(ends if backward else ends[::-1]))

    def per_chunk(act):
        for c in range(count):
            pl.when(j == c)(functools.partial(act, c))

    def feed(c):
        for i in every:
            for name in (N.act, N.slope):
                copies.start(name, c, i)

    if sums is not None:
        pl.when(first)(place.greet)

    @pl.when(first)
    def _():
        if forward:
            copies.start(N.wo)
            for i in every:
                copies.start(N.att, i)
                copies.start(N.x, i)
        if backward:
            copies.start(N.dza)
            if half < t:
                copies.start(N.dzb)
        for c in range(count):
            copies.start(N.wu, c)
            copies.start(N.wd, c)
            if c == 0 and not forward:
                feed(0)
                for i in every:
                    copies.start(N.n2, i)
        if not forward:
            for i in every:
                copies.start(N.middle, i)
                copies.start(N.g, i)
                copies.start(N.att, i)
            copies.start(N.wo)
        if forward:
            copies.wait(N.wo)
            for i, at in enumerate(spans):
                copies.wait(N.att, i)
                copies.wait(N.x, i)
                middle = r[N.x_v][at].astype(F32) + (dot(r[N.att_v][at], r[N.wo_v][...], NN) + r[N.bo][row, :])
                unit, _ = normalise(middle)
                r[N.n2_v][at] = (unit * r[N.g2][row, :] + r[N.b2][row, :]).astype(BF)
                r[N.middle_v][at] = middle
                r[N.next_v][at] = middle + r[N.bd][row, :]
                if not backward:
                    copies.start(N.middle_o, i)
                    copies.start(N.n2_o, i)
        if backward:
            r[N.dn_v][...] = jnp.zeros(r[N.dn_v].shape, F32)
            r[N.sums][...] = jnp.zeros(r[N.sums].shape, F32)
            copies.wait(N.dza)
            if half < t:
                copies.wait(N.dzb)
            r[N.sums][0:1, :] = column_sum(r[N.dz_v][...].astype(F32))
            if not forward:
                for i in every:
                    copies.wait(N.n2, i)

    @per_chunk
    def _(c):
        if sums is not None:
            sums.advance(parts, c)
        copies.wait(N.wu, c)
        copies.wait(N.wd, c)
        if not forward:
            if c + 1 < count:
                feed(c + 1)
            for i in every:
                for name in (N.act, N.slope):
                    copies.wait(name, c, i)
        elif not backward and c >= 2:
            for i in every:
                for name in (N.act, N.slope):
                    copies.wait(name, c - 2, i)

    wu, wd = r[N.wu_v].at[j], r[N.wd_v].at[j]
    slot = lax.rem(j, 2)

    def lead(at):
        return (
            dot(r[N.n2_v][at], wu[...], NN) if forward else None,
            dot(r[N.dz_v][at], wd[...], NT) if backward else None,
        )

    ff_sum = 0.0
    ahead = lead(spans[0])
    for i, at in enumerate(spans):
        hidden, da = ahead
        if i + 1 < len(spans):
            ahead = lead(spans[i + 1])
        if forward:
            act, slope = gelu_pair(hidden + r[N.bu][row, :])
            act = act.astype(BF)
            r[N.act_v][slot, at] = act
            if not backward:
                r[N.slope_v][slot, at] = slope.astype(BF)
        else:
            slope = r[N.slope_v][slot, at].astype(F32)
        if backward:
            dh = (da * slope).astype(BF)
            r[N.dh_v][at] = dh
            ff_sum = ff_sum + column_sum(dh.astype(F32))
        if forward:
            r[N.next_v][at] += dot(act, wd[...], NN)
        if backward:
            r[N.dn_v][at] += dot(dh, wu[...], NT)

    if forward:

        @per_chunk
        def _(c):
            for i in every:
                if not backward:
                    copies.start(N.act, c, i)
                    copies.start(N.slope, c, i)
                if c == count - 1:
                    if backward and spans[i].start >= r[N.next].shape[0]:
                        low = slice(spans[i].start - r[N.next].shape[0], spans[i].stop - r[N.next].shape[0])
                        r[N.dz_low][low] = r[N.next_v][spans[i]].astype(BF)
                    copies.start(N.next, i)

    if backward:
        core = r[N.core][0] if sums is None else place.bit(0)
        r[N.sums_ff][0:1, :] = ff_sum
        deliver(core, grad_dot(r[N.act_v][slot], r[N.dz_v][...]), chunks[1], r[N.wd_keep], r[N.wd_send])
        deliver(core, grad_dot(r[N.n2_v][...], r[N.dh_v][...]), chunks[0], r[N.wu_keep], r[N.wu_send])

    @pl.when(final)
    def _():
        if sums is not None:
            for stage in range(count, sums.stages):
                sums.advance(parts, stage)
        if backward:
            if not forward:
                copies.wait(N.wo)
            for i, at in enumerate(spans):
                if not forward:
                    copies.wait(N.middle, i)
                    copies.wait(N.g, i)
                    copies.wait(N.att, i)
                g = r[N.dz_v][at].astype(F32) if forward else r[N.dm_v][at]
                unit, inverse = normalise(r[N.middle_v][at])
                up = r[N.dn_v][at]
                r[N.sums][1:2, :] += column_sum(up * unit)
                r[N.sums][2:3, :] += column_sum(up)
                dm = g + norm_back(up, r[N.g2][row, :], unit, inverse)
                r[N.dm_v][at] = dm
                copies.start(N.dm, i)
                dy = dm.astype(BF)
                r[N.dh_v][at] = dy
                r[N.sums][3:4, :] += column_sum(dy.astype(F32))
                r[N.da_v][at] = dot(dy, r[N.wo_v][...], NT).astype(BF)
                copies.start(N.da, i)
            deliver(core, grad_dot(r[N.att_v][...], r[N.dh_v][...]), chunks[0], r[N.wo_keep], r[N.wo_send])
        for i in every:
            if forward:
                copies.wait(N.next, i)
                if not backward:
                    copies.wait(N.middle_o, i)
                    copies.wait(N.n2_o, i)
                    for c in range(max(0, count - 2), count):
                        copies.wait(N.act, c, i)
                        copies.wait(N.slope, c, i)
            if backward:
                copies.wait(N.dm, i)
                copies.wait(N.da, i)
        if sums is not None:
            sums.advance(parts, sums.stages)


def ffn_call(layer, devices, arrays, weights, forward, backward, sums=None, collective_id=0):
    t, d = arrays[N.att].shape
    ff = weights[N.wu].shape[2]
    cut, count = d, ff // d
    block = min(BLOCK, t)
    once = pl.Buffered(1)
    ins, outs, scratch = Names(), Names(), Names()
    hbm = pl.BlockSpec(memory_space=pl.ANY)

    def whole(shape):
        return pl.BlockSpec(shape, lambda j: (0,) * len(shape), pipeline_mode=once)

    vec = pl.BlockSpec(memory_space=pltpu.VMEM)
    ins.add(N.core, pl.BlockSpec(memory_space=pltpu.SMEM))
    for name in (N.att, N.wo, N.wu, N.wd):
        ins.add(name, hbm)
    ins.add(N.g2, vec)
    scratch.add(N.att_v, pltpu.VMEM((t, d), BF))
    scratch.add(N.wo_v, pltpu.VMEM((d, d), BF))
    scratch.add(N.wu_v, pltpu.VMEM((count, d, cut), BF))
    scratch.add(N.wd_v, pltpu.VMEM((count, cut, d), BF))
    scratch.add(N.middle_v, pltpu.VMEM((t, d), F32))
    scratch.add(N.n2_v, pltpu.VMEM((t, d), BF))
    scratch.add(N.act_v, pltpu.VMEM((2, t, cut), BF))
    if not (forward and backward):
        scratch.add(N.slope_v, pltpu.VMEM((2, t, cut), BF))
    if forward:
        ins.add(N.x, hbm)
        for name in (N.bo, N.b2, N.bd):
            ins.add(name, vec)
        ins.add(N.bu, pl.BlockSpec((weights[N.bu].shape[0], cut), lambda j: (0, j)))
        outs.add(N.next, hbm, ((t // 2 if backward else t, d), F32))
        if backward:
            outs.add(N.next_low, hbm, ((t // 2, d), BF))
            scratch.add(N.dz_low, pltpu.VMEM((t // 2, d), BF))
        scratch.add(N.x_v, pltpu.VMEM((t, d), arrays[N.x].dtype))
        scratch.add(N.next_v, pltpu.VMEM((t, d), F32))
    if backward:
        for name in (N.dza, N.dzb) if N.dzb in arrays else (N.dza,):
            ins.add(name, hbm)
        if not forward:
            for name in (N.g, N.middle, N.n2, N.act, N.slope):
                ins.add(name, hbm)
        outs.add(N.dm, hbm, ((t, d), F32))
        outs.add(N.da, hbm, ((t, d), BF))
        outs.add(N.sums, whole((8, d)), ((8, d), F32))
        outs.add(N.sums_ff, pl.BlockSpec((8, cut), lambda j: (0, j)), ((8, ff), F32))
        for kind in (N.keep, N.send):
            outs.add(N.wo_ + kind, whole((d // 2, d)), ((d // 2, d), BF))
            outs.add(N.wu_ + kind, pl.BlockSpec((d // 2, cut), lambda j: (0, j)), ((d // 2, ff), BF))
            outs.add(N.wd_ + kind, pl.BlockSpec((cut // 2, d), lambda j: (j, 0)), ((ff // 2, d), BF))
        scratch.add(N.dz_v, pltpu.VMEM((t, d), BF))
        scratch.add(N.dn_v, pltpu.VMEM((t, d), F32))
        scratch.add(N.dh_v, pltpu.VMEM((t, d), BF))
        scratch.add(N.dm_v, pltpu.VMEM((t, d), F32))
        scratch.add(N.da_v, pltpu.VMEM((t, d), BF))
    else:
        outs.add(N.middle, hbm, ((t, d), F32))
        outs.add(N.n2, hbm, ((t, d), BF))
        outs.add(N.act, hbm, ((t, ff), BF))
        outs.add(N.slope, hbm, ((t, ff), BF))
    scratch.add(N.sems, pltpu.SemaphoreType.DMA((3 + 2 * count + (t // block) * (6 + 2 * count),)))
    everything = {**weights, **arrays}
    if sums is not None:
        for i, (array, spec) in enumerate(zip(sums.inputs(), sums.in_specs())):
            ins.add(tag(N.sum_i, i), spec)
            everything[tag(N.sum_i, i)] = array
        for i, (shape, spec) in enumerate(zip(sums.out_shapes(), sums.out_specs())):
            outs.add(tag(N.sum_o, i), spec, (shape.shape, shape.dtype))
        for i, shape in enumerate(sums.scratch()):
            scratch.add(tag(N.sum_s, i), shape)
    if sums is None:
        compiler_params = params(62)
    else:
        compiler_params = pltpu.CompilerParams(
            vmem_limit_bytes=62 << 20, collective_id=collective_id, has_side_effects=True
        )

    def kernel(*refs, names):
        ffn_kernel(
            layer,
            *refs,
            names=[N.layer] + names,
            forward=forward,
            backward=backward,
            block=block,
            chunks=(d // devices, ff // devices),
            sums=sums,
        )

    found = pl.pallas_call(
        functools.partial(kernel, names=ins.names + outs.names + scratch.names),
        grid=(count,),
        in_specs=ins.specs,
        out_specs=outs.specs,
        out_shape=[jax.ShapeDtypeStruct(*shape) for shape in outs.shapes],
        scratch_shapes=scratch.specs,
        compiler_params=compiler_params,
        cost_estimate=cost((10e9 if forward else 0) + (18e9 if backward else 0)),
        name=N.feed_forward + (N._both if forward and backward else N._back if backward else ""),
    )(*[everything[name] for name in ins.names])
    return dict(zip(outs.names, found))


N_VECTORS = 12


def joined_back_kernel(*refs, names, layer, rows, block, sums):
    r = dict(zip(names, refs))
    last = sums is not None
    t, d = r[N.x_v].shape
    spans = [slice(i, i + block) for i in range(0, t, block)]
    half = len(spans) // 2
    order = list(range(half, len(spans))) + list(range(half)) if last else list(range(len(spans)))
    copies = Copies(r[N.sems])
    copies.add((N.weight,), r[N.weight].at[layer], r[N.weight_v])
    for i, at in enumerate(spans):
        for name in (N.dq, N.x, N.dm, N.normed):
            copies.add((name, i), r[name].at[at], r[name + N._v].at[at])
        copies.add((N.dkv, i), r[N.dkv].at[:, at], r[N.dkv_v].at[:, at])
        copies.add((N.dkvi, i), r[N.dkvi].at[:, :, at], r[N.dkvi_v].at[:, :, at])
        if not last or i < half:
            copies.add((N.g, i), r[N.dm_v].at[at], r[N.g].at[at])
        if not last:
            copies.add((N.low, i), r[N.low_v].at[at], r[N.low].at[at])
    for i in order:
        for name in (N.dq, N.dkv, N.dkvi):
            copies.start(name, i)
        if not last:
            if i == order[0]:
                copies.start(N.weight)
            for name in (N.x, N.dm):
                copies.start(name, i)
    if last:
        copies.start(N.weight)
        for i in order:
            for name in (N.x, N.dm):
                copies.start(name, i)
            if i == order[half - 1]:
                for j in order:
                    copies.start(N.normed, j)
        place = Place(sums.count)
        parts = sums.parts(
            place, [], [ref for name, ref in r.items() if name.startswith(N.sum_o)], [ref for name, ref in r.items() if name.startswith(N.sum_s)]
        )
        trade = Trade(place, r[N.low_v].at[t // 2 :], r[N.got], r[N.trade_sems])
    else:
        for i in order:
            copies.start(N.normed, i)
    totals = [0.0] * 4

    def gather(i):
        at = spans[i]
        for name in (N.dq, N.dkv, N.dkvi):
            copies.wait(name, i)
        r[N.df_v][at, :d] = r[N.dq_v][at]
        for k in range(2):
            got = jnp.concatenate([r[N.dkvi_v][h, k, at] for h in range(d // 128)], axis=1)
            cols = slice((k + 1) * d, (k + 2) * d)
            r[N.df_v][at, cols] = (r[N.dkv_v][k, at].astype(F32) + got.astype(F32)).astype(BF)

    def back(i):
        at = spans[i]
        up = dot(r[N.df_v][at], r[N.weight_v][...], NT)
        copies.wait(N.x, i)
        copies.wait(N.dm, i)
        unit, inverse = normalise(r[N.x_v][at].astype(F32))
        found = (up * unit, up, r[N.df_v][at, :d].astype(F32), r[N.df_v][at, 2 * d :].astype(F32))
        for k in range(4):
            totals[k] = totals[k] + column_sum(found[k])
        g = r[N.dm_v][at] + norm_back(up, r[N.gain][layer : layer + 1, :], unit, inverse)
        r[N.dm_v][at] = g
        r[N.low_v][at] = g.astype(BF)
        if not last or i < half:
            copies.start(N.g, i)
        if not last:
            copies.start(N.low, i)

    def product(k):
        return grad_dot(r[N.normed_v][...], r[N.df_v][:, k * d : (k + 1) * d])

    if not last:
        copies.wait(N.weight)
        for i in order:
            gather(i)
            back(i)
        for i in order:
            copies.wait(N.normed, i)
        for k, total in enumerate(totals):
            r[N.sums][k : k + 1, :] = total
        core = r[N.core][0]
        for k in range(3):
            cols = slice(k * d, (k + 1) * d)
            deliver(core, product(k), rows, r[N.keep].at[:, cols], r[N.send].at[:, cols])
    else:
        vectors = r[N.vectors]

        def swap(stage):
            return pltpu.make_async_remote_copy(
                src_ref=r[N.vectors_s].at[stage],
                dst_ref=r[N.vectors_v].at[stage],
                send_sem=r[N.vector_sems].at[0, stage],
                recv_sem=r[N.vector_sems].at[1, stage],
                device_id=place.partner(path[stage]),
                device_id_type=pl.DeviceIdType.MESH,
            )

        path = [0] + list(range(2, sums.stages)) + [1]

        def send_vectors(stage):
            if stage > 0:
                swap(stage - 1).wait()
                vectors[...] += r[N.vectors_v][stage - 1]
            if stage < sums.stages:
                r[N.vectors_s][stage] = vectors[...]
                swap(stage).start()

        for i in order:
            gather(i)
        copies.wait(N.weight)
        for i in order[:half]:
            back(i)
        place.greet()
        trade.copy().start()
        for i in order:
            copies.wait(N.normed, i)
        each = len(parts) // 3
        for k in range(3):
            made = product(k)
            for n in range(each):
                parts[each * k + n].fill(made[:, n * (d // each) : (n + 1) * (d // each)], rows)
                parts[each * k + n].begin(0)
        for i in order[half:]:
            back(i)
        for k, total in enumerate(totals):
            vectors[k : k + 1, :] = total
        for l in range(2):
            base = N_VECTORS * l
            if l > 0:
                vectors[base : base + 4, :] = r[N.sums_in][0:4, :]
            vectors[base + 4 : base + 8, :] = r[tag(N.sums, l)][0:4, :]
            for k in range(4):
                vectors[base + 8 + k : base + 9 + k, :] = r[tag(N.sums_ff, l)][0:1, k * d : (k + 1) * d]
        send_vectors(0)
        for stage in range(1, sums.stages + 1):
            sums.advance(parts, stage)
            send_vectors(stage)
        trade.copy().wait()
    for i in order:
        if not last or i < half:
            copies.wait(N.g, i)
        if not last:
            copies.wait(N.low, i)


def joined_back_call(arrays, layer, devices, sums=None, collective_id=0):
    t, d = arrays[N.x].shape
    last = sums is not None
    block = min(BLOCK, t // 2)
    ins, outs, scratch = Names(), Names(), Names()
    hbm = pl.BlockSpec(memory_space=pl.ANY)
    vmem = pl.BlockSpec(memory_space=pltpu.VMEM)
    ins.add(N.core, pl.BlockSpec(memory_space=pltpu.SMEM))
    for name in (N.dq, N.dkv, N.dkvi, N.x, N.dm, N.normed, N.weight):
        ins.add(name, hbm)
        shape = arrays[name].shape
        scratch.add(name + N._v, pltpu.VMEM(shape[1:] if name == N.weight else shape, arrays[name].dtype))
    ins.add(N.gain, vmem)
    scratch.add(N.df_v, pltpu.VMEM((t, 3 * d), BF))
    scratch.add(N.low_v, pltpu.VMEM((t, d), BF))
    outs.add(N.g, hbm, ((t // 2 if last else t, d), F32))
    if last:
        for name in (N.sums_in, *(tag(x, l) for x in (N.sums, N.sums_ff) for l in range(2))):
            ins.add(name, vmem)
        outs.add(N.got, hbm, ((t // 2, d), BF))
        outs.add(N.vectors, vmem, ((2 * N_VECTORS, d), F32))
        for i, (shape, spec) in enumerate(zip(sums.out_shapes(), sums.out_specs())):
            outs.add(tag(N.sum_o, i), vmem, (shape.shape, shape.dtype))
        for i, shape in enumerate(sums.scratch()):
            scratch.add(tag(N.sum_s, i), shape)
        for name in (N.vectors_s, N.vectors_v):
            scratch.add(name, pltpu.VMEM((sums.stages, 2 * N_VECTORS, d), F32))
        scratch.add(N.vector_sems, pltpu.SemaphoreType.DMA((2, sums.stages)))
        scratch.add(N.trade_sems, pltpu.SemaphoreType.DMA((2,)))
        compiler_params = pltpu.CompilerParams(
            vmem_limit_bytes=62 << 20, collective_id=collective_id, has_side_effects=True
        )
    else:
        outs.add(N.low, hbm, ((t, d), BF))
        outs.add(N.sums, vmem, ((8, d), F32))
        for kind in (N.keep, N.send):
            outs.add(kind, vmem, ((d // 2, 3 * d), BF))
        compiler_params = params(62)
    scratch.add(N.sems, pltpu.SemaphoreType.DMA((1 + (t // block) * 8,)))
    found = pl.pallas_call(
        functools.partial(
            joined_back_kernel,
            names=ins.names + outs.names + scratch.names,
            layer=layer,
            rows=d // devices,
            block=block,
            sums=sums,
        ),
        grid=(1,),
        in_specs=ins.specs,
        out_specs=outs.specs,
        out_shape=[jax.ShapeDtypeStruct(*shape) for shape in outs.shapes],
        scratch_shapes=scratch.specs,
        compiler_params=compiler_params,
        cost_estimate=cost(18e9 if last else 8e9),
        name=N.joined_back + (N._sums if last else ""),
    )(*[arrays[name] for name in ins.names])
    return dict(zip(outs.names, found))


def finish_kernel(place, *refs, names, devices):
    r = dict(zip(names, refs))
    chip, index = place[0], place[1]
    sems = r[N.sems]
    plain = []
    for cells in (N.block, N.input):
        plain.append((r[cells + N._own], r[cells + N._out].at[chip]))
    for m in range(4):
        for l in range(2):
            plain.append((r[tag(N.m, m, l)], r[tag(N.mat, m)].at[l]))
    copies = [pltpu.make_async_copy(src, dst, sems.at[i]) for i, (src, dst) in enumerate(plain)]
    n = len(copies)
    for copy in copies:
        copy.start()
    outs = []
    for i, cells in enumerate((N.block, N.input)):
        r[cells + N._wide][...] = r[cells + N._got][...].astype(F32)
        copy = pltpu.make_async_copy(r[cells + N._wide], r[cells + N._out].at[1 - chip], sems.at[n + i])
        copy.start()
        outs.append(copy)
    v = r[N.vectors]
    d = v.shape[1]
    piece = d // devices

    def cut(x, start, width):
        return pltpu.roll(x, lax.rem(d - start, d), 1)[:, :width]

    for l in range(2):
        mine = v[N_VECTORS * l : N_VECTORS * l + 8, :]
        ff = v[N_VECTORS * l + 8 : N_VECTORS * l + 12, :]
        rows = cut(mine, index * piece, piece)
        for name, k in ((N.v0, 0), (N.v1, 1), (N.v4, 7), (N.v5, 5), (N.v6, 6), (N.v8, 4)):
            r[name][l : l + 1, :] = rows[k : k + 1]
        per = devices // 2
        qv = cut(mine, lax.rem(index, per) * (2 * piece), 2 * piece)
        r[N.qv][l : l + 1, :] = jnp.where(index < per, qv[2:3], qv[3:4])
        per = devices // 4
        up = cut(ff, lax.rem(index, per) * (4 * piece), 4 * piece)
        at = index // per
        r[N.up][l : l + 1, :] = jnp.where(
            at < 2, jnp.where(at == 0, up[0:1], up[1:2]), jnp.where(at == 2, up[2:3], up[3:4])
        )
    for copy in copies + outs:
        copy.wait()


def finish_call(place, arrays, devices, genes, ff):
    d = arrays[N.vectors].shape[1]
    piece = d // devices
    ins, outs, scratch = Names(), Names(), Names()
    hbm = pl.BlockSpec(memory_space=pl.ANY)
    vmem = pl.BlockSpec(memory_space=pltpu.VMEM)
    for name in arrays:
        ins.add(name, vmem)
    for cells in (N.block, N.input):
        outs.add(cells + N._out, hbm, ((2, genes, d), F32))
        scratch.add(cells + N._wide, pltpu.VMEM((genes, d), F32))
    for m in range(4):
        outs.add(tag(N.mat, m), hbm, ((2,) + arrays[tag(N.m, m, 0)].shape, F32))
    for name in (N.v0, N.v1, N.v4, N.v5, N.v6, N.v8):
        outs.add(name, vmem, ((2, piece), F32))
    outs.add(N.qv, vmem, ((2, 2 * piece), F32))
    outs.add(N.up, vmem, ((2, ff // devices), F32))
    scratch.add(N.sems, pltpu.SemaphoreType.DMA((12,)))
    found = pl.pallas_call(
        functools.partial(finish_kernel, names=ins.names + outs.names + scratch.names, devices=devices),
        grid=(1,),
        in_specs=[pl.BlockSpec(memory_space=pltpu.SMEM)] + ins.specs,
        out_specs=outs.specs,
        out_shape=[jax.ShapeDtypeStruct(*shape) for shape in outs.shapes],
        scratch_shapes=scratch.specs,
        compiler_params=params(62),
        cost_estimate=cost(2e9),
        name=N.finish,
    )(place, *[arrays[name] for name in ins.names])
    return dict(zip(outs.names, found))


def on_device(
    device_count,
    cell_tokens,
    first_gain,
    first_bias,
    joined_weight,
    query_value_bias,
    output_weight,
    output_bias,
    second_gain,
    second_bias,
    up_weight,
    up_bias,
    down_weight,
    down_bias,
    cotangent,
    gene_mask,
):
    _, genes, d = cell_tokens.shape
    layers = joined_weight.shape[0]
    seq = lax.axis_index(N.seq)
    index = lax.axis_index(N.dp) * 4 + seq
    chip, core = seq // 2, seq % 2
    core_ref = core.astype(jnp.int32).reshape(1)
    across = [(0, 2), (1, 3), (2, 0), (3, 1)]

    x = cell_tokens
    weights = dict(
        core=core_ref,
        wo=output_weight,
        wu=up_weight,
        wd=down_weight,
        bo=output_bias,
        g2=second_gain,
        b2=second_bias,
        bu=up_bias,
        bd=down_bias,
    )
    chunks = device_count
    saved = []
    for layer in range(layers):
        top = layer == layers - 1
        seeds = (cotangent, gene_mask) if layer == 0 else ()
        joined = qkv_call(x, layer, chunks, first_gain, first_bias, joined_weight, query_value_bias, 2 * layers + 1 + layer, seeds)
        if seeds:
            g = joined[N.seed_own], lax.ppermute(joined[N.seed_send], N.seq, across)
        normed, q, kv, kvo = (joined[name] for name in (N.normed, N.q, N.kv, N.kvo))
        x = joined.get(N.held, x)
        att, lse = attend_call(q, kv, kvo)
        arrays = dict(att=att, x=x)
        if top:
            arrays.update(dza=g[0], dzb=g[1])
        found = ffn_call(layer, chunks, arrays, weights, True, top)
        saved.append((x, normed, q, kv, kvo, att, lse, found))
        x = found[N.next]

    dp_bits = list(range(2, device_count.bit_length() - 1))
    orders = (
        [1] + dp_bits,
        dp_bits[:1] + dp_bits[1:-1] + [1] + dp_bits[-1:],
        dp_bits[1:-1] + [1] + dp_bits[:1] + dp_bits[-1:],
    )

    def job(keep, send):
        split = (chunks // 2, 2 * keep.shape[0] // chunks, keep.shape[1])
        return Job(keep.reshape(split), send.reshape(split), device_count, orders)

    final = {}
    waiting, back = None, None
    for layer in reversed(range(layers)):
        x, normed, q, kv, kvo, att, lse, found = saved[layer]
        top, bottom = layer == layers - 1, layer == 0
        if not top:
            arrays = dict(att=att, g=back[N.g], dza=back[N.low], **{k: found[k] for k in (N.middle, N.n2, N.act, N.slope)})
            found = ffn_call(layer, chunks, arrays, weights, False, True, Sums([waiting], device_count), layers + layer)
            final[tag(N.m, 0, layer + 1)] = found[tag(N.sum_o, 0)]
        jobs = [job(found[w + N._keep], found[w + N._send]) for w in (N.wo, N.wu, N.wd)]
        trade_out = found[N.next_low] if top else None
        dq, dkv, dkvi, *done = attend_back_call(
            q, kv, kvo, found[N.da], att, lse, Sums(jobs, device_count, trade_out, 3), layer
        )
        if top:
            final[N.block_own], final[N.block_got] = found[N.next], done.pop()
        for i in range(3):
            final[tag(N.m, i + 1, layer)] = done[i]
        final[tag(N.sums, layer)], final[tag(N.sums_ff, layer)] = found[N.sums], found[N.sums_ff]
        arrays = dict(
            core=core_ref, dq=dq, dkv=dkv, dkvi=dkvi, x=x, dm=found[N.dm], normed=normed, weight=joined_weight, gain=first_gain
        )
        if bottom:
            arrays.update(sums_in=back[N.sums])
            for l in range(2):
                arrays.update({tag(N.sums, l): final.pop(tag(N.sums, l)), tag(N.sums_ff, l): final.pop(tag(N.sums_ff, l))})
            late = (orders[1], dp_bits[1:-1] + dp_bits[:1] + [1] + dp_bits[-1:]) * 3
            made = Job(None, None, device_count, late, (d // chunks, 3 * d))
            back = joined_back_call(arrays, layer, chunks, Sums([made], device_count), 2 * layers)
        else:
            back = joined_back_call(arrays, layer, chunks)
            waiting = job(back[N.keep], back[N.send])
    final.update(
        **{tag(N.m, 0, 0): back[tag(N.sum_o, 0)]}, input_own=back[N.g], input_got=back[N.got], vectors=back[N.vectors]
    )
    place = jnp.stack([chip, index]).astype(jnp.int32)
    out = finish_call(place, final, device_count, genes, up_bias.shape[1])
    return tuple(
        out[name]
        for name in (
            N.block_out,
            N.input_out,
            N.v0,
            N.v1,
            tag(N.mat, 0),
            N.qv,
            tag(N.mat, 1),
            N.v4,
            N.v5,
            N.v6,
            tag(N.mat, 2),
            N.up,
            tag(N.mat, 3),
            N.v8,
        )
    )


def solution(mesh):
    split = P(None, (N.dp, N.seq))
    split_rows = P(None, (N.dp, N.seq), None)
    tokens = P(N.dp, N.seq, None)
    return jax.shard_map(
        functools.partial(on_device, mesh.size),
        mesh=mesh,
        in_specs=(tokens,) + (P(),) * 12 + (tokens, P(N.dp, N.seq)),
        out_specs=(
            tokens,
            tokens,
            split,
            split,
            split_rows,
            split,
            split_rows,
            split,
            split,
            split,
            split_rows,
            split,
            split_rows,
            split,
        ),
        check_vma=False,
    )
```

time: 549 us -> 451 us (0.82)
  waiting for transfers between devices: 43.5 us -> 0.01 us
  local copies, waits for them, and re-layouts: 18.2 us -> 0.91 us
  Pallas kernels: 457 us -> 443 us
  other arithmetic: 13.2 us -> 0.58 us
  starting transfers between devices: 6.66 us -> 1.15 us
    ppermute x6 -> x1, waiting for transfers between devices: 43.5 us -> 0.01 us  [on_device(): g = (joined[N.seed_own], lax.ppermute(joined[N.seed_send], N.seq, across))]
    pallas_call x2, Pallas kernels: 165 us -> 154 us  [attend_back_call(): pl.pallas_call(functools.partial(attend_back_kernel, chunk=min(256, t), s...]
    another operation x14 -> x1, other arithmetic: 7.96 us -> 0.58 us  [on_device(): place = jnp.stack([chip, index]).astype(jnp.int32)]
    ppermute x6 -> x1, starting transfers between devices: 6.66 us -> 1.15 us  [on_device(): g = (joined[N.seed_own], lax.ppermute(joined[N.seed_send], N.seq, across))]
    pallas_call x17 -> x8, Pallas kernels: 232 us -> 230 us  [the longest x3 116 us: ffn_call(): pl.pallas_call(functools.partial(kernel, names=ins.names + outs.names + s...]
  transfers between devices with their start and end apart: 6 -> 1, of which waited for: 5 -> 0; matrix products, arithmetic and copies ran while one was open for 3% -> 0% of each run, Pallas kernels for 11% -> 20%
where the time goes in v3:
time: 451 us; the launch traced here: 446 us
  Pallas kernels  443 us (98%)
    pallas_call x2, Pallas kernels, attend_back_call(): pl.pallas_call(functools.partial(attend_back_kernel, chunk=min(256, t), s...  154 us
    pallas_call x3, Pallas kernels, ffn_call(): pl.pallas_call(functools.partial(kernel, names=ins.names + outs.names + s...  116 us
    pallas_call x2, Pallas kernels, joined_back_call(): pl.pallas_call(functools.partial(joined_back_kernel, names=ins.names + ou...  70.5 us
    pallas_call x2, Pallas kernels, attend_call(): pl.pallas_call(functools.partial(attend_kernel, chunk=min(256, t)), grid=...  59.6 us
    pallas_call x2, Pallas kernels, qkv_call(): pl.pallas_call(functools.partial(qkv_kernel, names=ins.names + outs.names...  35.8 us
  transfers between devices with their start and end apart: 1, of which 0 were waited for; matrix products, arithmetic and copies ran while one was open for 0% of the time, Pallas kernels for 20%

profile of v3, /device:TPU:0, one launch (start us, length us, event | category | flops | bytes accessed | tf_op | source)
XLA Modules:
  0.0 446.3 jit_solution(16889996849977086991)
XLA Ops:
  0.6 26.6 %norm_qkv.2 = (bf16[1024,768]{1,0:T(8,128)(2,1)}, bf16[512,768]{1,0:T(8,128)(2,1)}, bf16[512,768]{1,0:T(8,128)(2,1)}, bf16[1024,768]{1,0:T(8,128)(2,1)}, bf16[10...) custom-call(bf16[2,512,768]{2,1,0:T(8,128)(2,1)} %refs_0_.1, ...), custom_call_target="tpu_custom_call" | custom-call | flops 24000000000 | tf_op jit(solution)/shard_map/norm_qkv/pallas_call | solution.py:209
  27.3 1.1 collective-permute-start
  28.4 29.7 %attend.2 = (bf16[1024,768]{1,0:T(8,128)(2,1)}, f32[6,8,1024]{2,1,0:T(8,128)}) custom-call(bf16[1024,768]{1,0:T(8,128)(2,1)} %get-tuple-element.93.q.refs_0_, bf16[2,1024,768]{2,1,0:T(8,128)(2,1)} %get-tuple-element.94.kv.refs_1_, bf16[2,1024,768]{2,1,0:T(8,128)(2,1)} %get-tuple-element.95.kvo.refs_2_), custom_call_target="tpu_custom_call" | custom-call | flops 32000000000 | tf_op jit(solution)/shard_map/attend/pallas_call | solution.py:285
  58.1 21.7 %feed_forward.1 = (f32[1024,768]{1,0:T(8,128)}, f32[1024,768]{1,0:T(8,128)}, bf16[1024,768]{1,0:T(8,128)(2,1)}, bf16[1024,3072]{1,0:T(8,128)(2,1)}, bf16[1024,3072]{1,0:T(8,128)(2,1)}) custom-call(s32[1]{0:T(128)} %bitcast.2.refs_0_, bf16[1024,768]{1,0:T(8,128)(2,1)} %get-tuple-element.96.refs_1_.refs_4_, bf16[2,768,768]{2,1,0:T(8,128)(2,1)} %refs_2_.9, ...), custom_call_target="tpu_custom_call" | custom-call | flops 20000000000 | tf_op jit(solution)/shard_map/feed_forward/pallas_call | solution.py:961
  79.8 9.1 %norm_qkv.3 = (bf16[1024,768]{1,0:T(8,128)(2,1)}, bf16[1024,768]{1,0:T(8,128)(2,1)}, bf16[2,1024,768]{2,1,0:T(8,128)(2,1)}, bf16[2,1024,768]{2,1,0:T(8,128)(2,1)}) custom-call(f32[1024,768]{1,0:T(8,128)} %get-tuple-element.98.refs_0_.refs_6_.refs_4_, bf16[2,768,2304]{2,1,0:T(8,128)(2,1)} %refs_7_.7, f32[2,768]{1,0:T(2,128)} %refs_8_.7, f32[2,768]{1,0:T(2,128)} %refs_3_.7, ...), custom_call_target="tpu_custom_call" | custom-call | flops 10000000000 | tf_op jit(solution)/shard_map/norm_qkv/pallas_call | solution.py:209
  89.0 29.9 %attend.3 = (bf16[1024,768]{1,0:T(8,128)(2,1)}, f32[6,8,1024]{2,1,0:T(8,128)}) custom-call(bf16[1024,768]{1,0:T(8,128)(2,1)} %get-tuple-element.99.q.refs_0_, bf16[2,1024,768]{2,1,0:T(8,128)(2,1)} %get-tuple-element.100.kv.refs_1_, bf16[2,1024,768]{2,1,0:T(8,128)(2,1)} %get-tuple-element.101.kvo.refs_2_), custom_call_target="tpu_custom_call" | custom-call | flops 32000000000 | tf_op jit(solution)/shard_map/attend/pallas_call | solution.py:285
  118.9 0.6 pad_add_fusion.place
  119.5 0.0 collective-permute-done.refs_12_
  119.5 0.0 copy-start
  119.5 0.9 copy-done
  120.4 52.2 %feed_forward_both.1 = (f32[512,768]{1,0:T(8,128)}, bf16[512,768]{1,0:T(8,128)(2,1)}, f32[1024,768]{1,0:T(8,128)}, bf16[1024,768]{1,0:T(8,128)(2,1)}, f32[8,768]...) custom-call(s32[1]{0:T(128)} %bitcast.2.refs_0_, ...), custom_call_target="tpu_custom_call" | custom-call | flops 56000000000 | tf_op jit(solution)/shard_map/feed_forward_both/pallas_call | solution.py:961
  172.6 78.0 %attend_back.2 = (bf16[1024,768]{1,0:T(8,128)(2,1)}, bf16[2,1024,768]{2,1,0:T(8,128)(2,1)}, bf16[6,2,1024,128]{3,2,1,0:T(8,128)(2,1)}, f32[24,768]{1,0:T(8,128)}...) custom-call(bf16[1024,768]{1,0:T(8,128)(2,1)} %get-tuple-element.99.q.refs_0_, ...), custom_call_target="tpu_custom_call" | custom-call | flops 73999998976 | tf_op jit(solution)/shard_map/attend_back/pallas_call | solution.py:576
  250.6 19.4 %joined_back.1 = (f32[1024,768]{1,0:T(8,128)}, bf16[1024,768]{1,0:T(8,128)(2,1)}, f32[8,768]{1,0:T(8,128)}, bf16[384,2304]{1,0:T(8,128)(2,1)}, bf16[384,2304]{1,0:T(8,128)(2,1)}) custom-call(s32[1]{0:T(128)} %bitcast.2.refs_0_, bf16[1024,768]{1,0:T(8,128)(2,1)} %get-tuple-element.119.refs_1_, bf16[2,1024,768]{2,1,0:T(8,128)(2,1)} %get-tuple-element.120.refs_2_, ...), custom_call_target="tpu_custom_call" | custom-call | flops 16000000000 | tf_op jit(solution)/shard_map/joined_back/pallas_call | solution.py:1165
  270.0 42.4 %feed_forward_back.1 = (f32[1024,768]{1,0:T(8,128)}, bf16[1024,768]{1,0:T(8,128)(2,1)}, f32[8,768]{1,0:T(8,128)}, f32[8,3072]{1,0:T(8,128)}, bf16[384,768]{1,0:T...) custom-call(s32[1]{0:T(128)} %bitcast.2.refs_0_, ...), custom_call_target="tpu_custom_call" | custom-call | flops 35999997952 | tf_op jit(solution)/shard_map/feed_forward_back/pallas_call | solution.py:961
  312.5 75.6 %attend_back.3 = (bf16[1024,768]{1,0:T(8,128)(2,1)}, bf16[2,1024,768]{2,1,0:T(8,128)(2,1)}, bf16[6,2,1024,128]{3,2,1,0:T(8,128)(2,1)}, f32[24,768]{1,0:T(8,128)}, f32[24,3072]{1,0:T(8,128)}, /*index=5*/f32[96,768]{1,0:T(8,128)}) custom-call(bf16[1024,768]{1,0:T(8,128)(2,1)} %get-tuple-element.93.q.refs_0_, ...), custom_call_target="tpu_custom_call" | custom-call | flops 73999998976 | tf_op jit(solution)/shard_map/attend_back/pallas_call | solution.py:576
  388.1 51.1 %joined_back_sums.1 = (f32[512,768]{1,0:T(8,128)}, bf16[512,768]{1,0:T(8,128)(2,1)}, f32[24,768]{1,0:T(8,128)}, f32[24,2304]{1,0:T(8,128)}) custom-call(s32[1]{0:T(128)} %bitcast.2.refs_0_, bf16[1024,768]{1,0:T(8,128)(2,1)} %get-tuple-element.144.refs_1_, bf16[2,1024,768]{2,1,0:T(8,128)(2,1)} %get-tuple-element.145.refs_2_, ...), custom_call_target="tpu_custom_call" | custom-call | flops 35999997952 | tf_op jit(solution)/shard_map/joined_back_sums/pallas_call | solution.py:1165
  439.2 6.9 %finish.1 = (f32[2,512,768]{2,1,0:T(8,128)}, f32[2,512,768]{2,1,0:T(8,128)}, f32[2,24,2304]{2,1,0:T(8,128)}, f32[2,24,768]{2,1,0:T(8,128)}, f32[2,24,3072]{2,1,0...) custom-call(s32[2]{0:T(128)} %pad_add_fusion.place, ...), custom_call_target="tpu_custom_call" | custom-call | flops 4000000000 | tf_op jit(solution)/shard_map/finish/pallas_call | solution.py:1250
Async XLA Ops:
  27.3 92.2 %collective-permute-start = (bf16[512,768]{1,0:T(8,128)(2,1)}, bf16[512,768]{1,0:T(8,128)(2,1)S(1)}, u32[]{:S(2)}, u32[]{:S(2)}) collective-permute-start(bf16[512,768]{1,0:T(8,128)(2,1)} %get-tuple-element.104), channel_id=1, source_target_pairs={{0,2},{1,3},{2,0},{3,1},{4,6},{5,7},{6,4},{7,5},{8,10},{9,11},{10,... | collective-permute-start | bytes 2359304 | tf_op jit(solution)/shard_map/ppermute | solution.py:1309
  119.5 0.9 copy-start

commit v4 on v3

--- a/solution.py
+++ b/solution.py
@@ -13,7 +13,7 @@
 F32 = jnp.float32
 NN = ((1,), (0,))
 NT = ((1,), (1,))
-SAFE = 80.0
+SAFE = 60
 BLOCK = 256
 SLOTS = (0, 2, 6, 8, 10)
 
@@ -118,8 +118,9 @@
     def parcel(i):
         return remote(r[N.kv_v].at[:, spans[i]], r[N.kvo].at[:, spans[i]], i, 0)
 
-    def trade():
-        return remote(r[N.x].at[1 - chip], r[N.x_v].at[t // 2 :], len(spans), 1)
+    def trade(i):
+        there = spans[half + i]
+        return remote(r[N.x].at[1 - chip, spans[i]], r[N.x_v].at[there], len(spans) + i, 1)
 
     for i in range(half if trading else len(spans)):
         copies.start(N.x, i)
@@ -128,7 +129,8 @@
                 copies.start(N.weight, k)
     place.greet(2)
     if trading:
-        trade().start()
+        for i in range(half):
+            trade(i).start()
         for i in range(2):
             copies.start(N.seed, i)
     waited = set()
@@ -147,11 +149,12 @@
                 copies.wait(N.seed, i)
                 r[N.seed_v][i] = r[N.seed_v][i] * mask.T[:, :1].astype(BF)
                 copies.start(N.seeded, i)
-            trade().wait()
         for i in group:
             at = spans[i]
             if not trading or i < half:
                 copies.wait(N.x, i)
+            else:
+                trade(i - half).wait()
             if trading:
                 copies.start(N.held, i)
             unit, _ = normalise(r[N.x_v][at].astype(F32))
@@ -205,7 +208,7 @@
     scratch.add(N.kv_v, pltpu.VMEM((2, t, d), BF))
     scratch.add(N.weight_v, pltpu.VMEM((3, d, d), BF))
     scratch.add(N.sems, pltpu.SemaphoreType.DMA((7 + 5 * blocks,)))
-    scratch.add(N.far_sems, pltpu.SemaphoreType.DMA((2, blocks + 1)))
+    scratch.add(N.far_sems, pltpu.SemaphoreType.DMA((2, 2 * blocks)))
     found = pl.pallas_call(
         functools.partial(
             qkv_kernel,
@@ -232,15 +235,7 @@
 def attend_kernel(q, kv, kvo, out, lse, *, chunk):
     t = q.shape[0]
     c = LOG2E * HEAD**-0.5
-    lane = lax.broadcasted_iota(jnp.int32, (128, 128), 0) // HEAD
-    pick = (lane == lax.broadcasted_iota(jnp.int32, (128, 128), 1)).astype(BF)
-
-    def squares(x):
-        x = x.astype(F32)
-        return jnp.max(dot((x * x).astype(BF), pick, NN), axis=0, keepdims=True)
-
-    bound = squares(q[...]) * jnp.maximum(squares(kv[0]), squares(kvo[0]))
-    fast = jnp.max(bound) * (c * c * 1.05) < SAFE * SAFE
+    lows, highs = [], []
 
     def run(stable):
         for head in range(2):
@@ -269,12 +264,18 @@
                     p = [jnp.exp2(x * c).astype(BF) for x in s]
                 total = dot(values[0], p[0], NN) + dot(values[1], p[1], NN)
                 level = total[HEAD : HEAD + 1]
+                if not stable:
+                    lows.append(level)
+                    highs.append(level)
                 cols = slice(j * chunk, (j + 1) * chunk)
                 out[cols, ls] = (total[:HEAD] / level).T.astype(BF)
                 lse[0, head : head + 1, cols] = shift + jnp.log2(level)
 
-    pl.when(fast)(lambda: run(False))
-    pl.when(jnp.logical_not(fast))(lambda: run(True))
+    run(False)
+    low = jnp.min(functools.reduce(jnp.minimum, lows))
+    high = jnp.max(functools.reduce(jnp.maximum, highs))
+    fine = jnp.logical_and(low >= 2.0**-SAFE, high <= 2.0**SAFE)
+    pl.when(jnp.logical_not(fine))(lambda: run(True))
 
 
 def attend_call(q, kv, kvo):
@@ -820,7 +821,7 @@
                     copies.start(N.next, i)
 
     if backward:
-        core = r[N.core][0] if sums is None else place.bit(0)
+        core = Place(2).bit(0)
         r[N.sums_ff][0:1, :] = ff_sum
         deliver(core, grad_dot(r[N.act_v][slot], r[N.dz_v][...]), chunks[1], r[N.wd_keep], r[N.wd_send])
         deliver(core, grad_dot(r[N.n2_v][...], r[N.dh_v][...]), chunks[0], r[N.wu_keep], r[N.wu_send])
@@ -881,7 +882,6 @@
         return pl.BlockSpec(shape, lambda j: (0,) * len(shape), pipeline_mode=once)
 
     vec = pl.BlockSpec(memory_space=pltpu.VMEM)
-    ins.add(N.core, pl.BlockSpec(memory_space=pltpu.SMEM))
     for name in (N.att, N.wo, N.wu, N.wd):
         ins.add(name, hbm)
     ins.add(N.g2, vec)
@@ -1002,13 +1002,12 @@
             for name in (N.x, N.dm):
                 copies.start(name, i)
     if last:
+        for i in order:
+            copies.start(N.normed, i)
         copies.start(N.weight)
         for i in order:
             for name in (N.x, N.dm):
                 copies.start(name, i)
-            if i == order[half - 1]:
-                for j in order:
-                    copies.start(N.normed, j)
         place = Place(sums.count)
         parts = sums.parts(
             place, [], [ref for name, ref in r.items() if name.startswith(N.sum_o)], [ref for name, ref in r.items() if name.startswith(N.sum_s)]
@@ -1058,7 +1057,7 @@
             copies.wait(N.normed, i)
         for k, total in enumerate(totals):
             r[N.sums][k : k + 1, :] = total
-        core = r[N.core][0]
+        core = Place(2).bit(0)
         for k in range(3):
             cols = slice(k * d, (k + 1) * d)
             deliver(core, product(k), rows, r[N.keep].at[:, cols], r[N.send].at[:, cols])
@@ -1087,11 +1086,6 @@
 
         for i in order:
             gather(i)
-        copies.wait(N.weight)
-        for i in order[:half]:
-            back(i)
-        place.greet()
-        trade.copy().start()
         for i in order:
             copies.wait(N.normed, i)
         each = len(parts) // 3
@@ -1099,7 +1093,14 @@
             made = product(k)
             for n in range(each):
                 parts[each * k + n].fill(made[:, n * (d // each) : (n + 1) * (d // each)], rows)
+                if k == n == 0:
+                    place.greet()
                 parts[each * k + n].begin(0)
+        copies.wait(N.weight)
+        for i in order[:half]:
+            back(i)
+        trade.copy().start()
+        sums.advance(parts, 1)
         for i in order[half:]:
             back(i)
         for k, total in enumerate(totals):
@@ -1113,7 +1114,8 @@
                 vectors[base + 8 + k : base + 9 + k, :] = r[tag(N.sums_ff, l)][0:1, k * d : (k + 1) * d]
         send_vectors(0)
         for stage in range(1, sums.stages + 1):
-            sums.advance(parts, stage)
+            if stage > 1:
+                sums.advance(parts, stage)
             send_vectors(stage)
         trade.copy().wait()
     for i in order:
@@ -1130,7 +1132,6 @@
     ins, outs, scratch = Names(), Names(), Names()
     hbm = pl.BlockSpec(memory_space=pl.ANY)
     vmem = pl.BlockSpec(memory_space=pltpu.VMEM)
-    ins.add(N.core, pl.BlockSpec(memory_space=pltpu.SMEM))
     for name in (N.dq, N.dkv, N.dkvi, N.x, N.dm, N.normed, N.weight):
         ins.add(name, hbm)
         shape = arrays[name].shape
@@ -1183,26 +1184,33 @@
     return dict(zip(outs.names, found))
 
 
-def finish_kernel(place, *refs, names, devices):
+def finish_kernel(*refs, names, devices):
     r = dict(zip(names, refs))
-    chip, index = place[0], place[1]
-    sems = r[N.sems]
-    plain = []
+    place = Place(devices)
+    chip, index = place.bit(1), place.dp * 4 + place.seq
+    copies, moves = Copies(r[N.sems]), []
     for cells in (N.block, N.input):
-        plain.append((r[cells + N._own], r[cells + N._out].at[chip]))
+        moves.append((cells + N._got, None, None))
+        moves.append((cells + N._own, cells + N._out, chip))
     for m in range(4):
         for l in range(2):
-            plain.append((r[tag(N.m, m, l)], r[tag(N.mat, m)].at[l]))
-    copies = [pltpu.make_async_copy(src, dst, sems.at[i]) for i, (src, dst) in enumerate(plain)]
-    n = len(copies)
-    for copy in copies:
-        copy.start()
-    outs = []
-    for i, cells in enumerate((N.block, N.input)):
-        r[cells + N._wide][...] = r[cells + N._got][...].astype(F32)
-        copy = pltpu.make_async_copy(r[cells + N._wide], r[cells + N._out].at[1 - chip], sems.at[n + i])
-        copy.start()
-        outs.append(copy)
+            moves.append((tag(N.m, m, l), tag(N.mat, m), l))
+    for name, out, at in moves:
+        copies.add((name, 0), r[name], r[name + N._v])
+        if out is not None:
+            copies.add((name, 1), r[name + N._v], r[out].at[at])
+    for cells in (N.block, N.input):
+        copies.add((cells,), r[cells + N._wide], r[cells + N._out].at[1 - chip])
+    for name, _, _ in moves:
+        copies.start(name, 0)
+    for name, out, _ in moves:
+        copies.wait(name, 0)
+        if out is not None:
+            copies.start(name, 1)
+        else:
+            cells = N.block if name == N.block_got else N.input
+            r[cells + N._wide][...] = r[name + N._v][...].astype(F32)
+            copies.start(cells)
     v = r[N.vectors]
     d = v.shape[1]
     piece = d // devices
@@ -1225,18 +1233,23 @@
         r[N.up][l : l + 1, :] = jnp.where(
             at < 2, jnp.where(at == 0, up[0:1], up[1:2]), jnp.where(at == 2, up[2:3], up[3:4])
         )
-    for copy in copies + outs:
-        copy.wait()
-
-
-def finish_call(place, arrays, devices, genes, ff):
+    for name, out, _ in moves:
+        if out is not None:
+            copies.wait(name, 1)
+    copies.wait(N.block)
+    copies.wait(N.input)
+
+
+def finish_call(arrays, devices, genes, ff):
     d = arrays[N.vectors].shape[1]
     piece = d // devices
     ins, outs, scratch = Names(), Names(), Names()
     hbm = pl.BlockSpec(memory_space=pl.ANY)
     vmem = pl.BlockSpec(memory_space=pltpu.VMEM)
-    for name in arrays:
-        ins.add(name, vmem)
+    for name, array in arrays.items():
+        ins.add(name, vmem if name == N.vectors else hbm)
+        if name != N.vectors:
+            scratch.add(name + N._v, pltpu.VMEM(array.shape, array.dtype))
     for cells in (N.block, N.input):
         outs.add(cells + N._out, hbm, ((2, genes, d), F32))
         scratch.add(cells + N._wide, pltpu.VMEM((genes, d), F32))
@@ -1246,18 +1259,18 @@
         outs.add(name, vmem, ((2, piece), F32))
     outs.add(N.qv, vmem, ((2, 2 * piece), F32))
     outs.add(N.up, vmem, ((2, ff // devices), F32))
-    scratch.add(N.sems, pltpu.SemaphoreType.DMA((12,)))
+    scratch.add(N.sems, pltpu.SemaphoreType.DMA((24,)))
     found = pl.pallas_call(
         functools.partial(finish_kernel, names=ins.names + outs.names + scratch.names, devices=devices),
         grid=(1,),
-        in_specs=[pl.BlockSpec(memory_space=pltpu.SMEM)] + ins.specs,
+        in_specs=ins.specs,
         out_specs=outs.specs,
         out_shape=[jax.ShapeDtypeStruct(*shape) for shape in outs.shapes],
         scratch_shapes=scratch.specs,
         compiler_params=params(62),
         cost_estimate=cost(2e9),
         name=N.finish,
-    )(place, *[arrays[name] for name in ins.names])
+    )(*[arrays[name] for name in ins.names])
     return dict(zip(outs.names, found))
 
 
@@ -1282,14 +1295,10 @@
     _, genes, d = cell_tokens.shape
     layers = joined_weight.shape[0]
     seq = lax.axis_index(N.seq)
-    index = lax.axis_index(N.dp) * 4 + seq
-    chip, core = seq // 2, seq % 2
-    core_ref = core.astype(jnp.int32).reshape(1)
     across = [(0, 2), (1, 3), (2, 0), (3, 1)]
 
     x = cell_tokens
     weights = dict(
-        core=core_ref,
         wo=output_weight,
         wu=up_weight,
         wd=down_weight,
@@ -1348,7 +1357,7 @@
             final[tag(N.m, i + 1, layer)] = done[i]
         final[tag(N.sums, layer)], final[tag(N.sums_ff, layer)] = found[N.sums], found[N.sums_ff]
         arrays = dict(
-            core=core_ref, dq=dq, dkv=dkv, dkvi=dkvi, x=x, dm=found[N.dm], normed=normed, weight=joined_weight, gain=first_gain
+            dq=dq, dkv=dkv, dkvi=dkvi, x=x, dm=found[N.dm], normed=normed, weight=joined_weight, gain=first_gain
         )
         if bottom:
             arrays.update(sums_in=back[N.sums])
@@ -1363,8 +1372,7 @@
     final.update(
         **{tag(N.m, 0, 0): back[tag(N.sum_o, 0)]}, input_own=back[N.g], input_got=back[N.got], vectors=back[N.vectors]
     )
-    place = jnp.stack([chip, index]).astype(jnp.int32)
-    out = finish_call(place, final, device_count, genes, up_bias.shape[1])
+    out = finish_call(final, device_count, genes, up_bias.shape[1])
     return tuple(
         out[name]
         for name in (

time: 451 us -> 437 us (0.969)
  Pallas kernels: 443 us -> 430 us
    pallas_call x2, Pallas kernels: 70.5 us -> 64.3 us  [joined_back_call(): pl.pallas_call(functools.partial(joined_back_kernel, names=ins.names + ou...]
    pallas_call x2, Pallas kernels: 59.6 us -> 53.7 us  [attend_call(): pl.pallas_call(functools.partial(attend_kernel, chunk=min(256, t)), grid=...]
where the time goes in v4:
time: 437 us; the launch traced here: 433 us
  Pallas kernels  430 us (98%)
    pallas_call x2, Pallas kernels, attend_back_call(): pl.pallas_call(functools.partial(attend_back_kernel, chunk=min(256, t), s...  154 us
    pallas_call x3, Pallas kernels, ffn_call(): pl.pallas_call(functools.partial(kernel, names=ins.names + outs.names + s...  116 us
    pallas_call x2, Pallas kernels, joined_back_call(): pl.pallas_call(functools.partial(joined_back_kernel, names=ins.names + ou...  64.3 us
    pallas_call x2, Pallas kernels, attend_call(): pl.pallas_call(functools.partial(attend_kernel, chunk=min(256, t)), grid=...  53.7 us
    pallas_call x2, Pallas kernels, qkv_call(): pl.pallas_call(functools.partial(qkv_kernel, names=ins.names + outs.names...  34.8 us
  transfers between devices with their start and end apart: 1, of which 0 were waited for; matrix products, arithmetic and copies ran while one was open for 0% of the time, Pallas kernels for 20%

profile of v4, /device:TPU:0, one launch (start us, length us, event | category | flops | bytes accessed | tf_op | source)
XLA Modules:
  0.0 432.7 jit_solution(8080085316072354350)
XLA Ops:
  0.6 25.6 %norm_qkv.2 = (bf16[1024,768]{1,0:T(8,128)(2,1)}, bf16[512,768]{1,0:T(8,128)(2,1)}, bf16[512,768]{1,0:T(8,128)(2,1)}, bf16[1024,768]{1,0:T(8,128)(2,1)}, bf16[10...) custom-call(bf16[2,512,768]{2,1,0:T(8,128)(2,1)} %refs_0_.1, ...), custom_call_target="tpu_custom_call" | custom-call | flops 24000000000 | tf_op jit(solution)/shard_map/norm_qkv/pallas_call | solution.py:212
  26.2 1.2 collective-permute-start
  27.4 26.7 %attend.2 = (bf16[1024,768]{1,0:T(8,128)(2,1)}, f32[6,8,1024]{2,1,0:T(8,128)}) custom-call(bf16[1024,768]{1,0:T(8,128)(2,1)} %get-tuple-element.93.q.refs_0_, bf16[2,1024,768]{2,1,0:T(8,128)(2,1)} %get-tuple-element.94.kv.refs_1_, bf16[2,1024,768]{2,1,0:T(8,128)(2,1)} %get-tuple-element.95.kvo.refs_2_), custom_call_target="tpu_custom_call" | custom-call | flops 32000000000 | tf_op jit(solution)/shard_map/attend/pallas_call | solution.py:286
  54.1 21.7 %feed_forward.1 = (f32[1024,768]{1,0:T(8,128)}, f32[1024,768]{1,0:T(8,128)}, bf16[1024,768]{1,0:T(8,128)(2,1)}, bf16[1024,3072]{1,0:T(8,128)(2,1)}, bf16[1024,3072]{1,0:T(8,128)(2,1)}) custom-call(bf16[1024,768]{1,0:T(8,128)(2,1)} %get-tuple-element.96.refs_0_.refs_4_, bf16[2,768,768]{2,1,0:T(8,128)(2,1)} %refs_1_.9, bf16[2,768,3072]{2,1,0:T(8,128)(2,1)} %refs_2_.9, ...), custom_call_target="tpu_custom_call" | custom-call | flops 20000000000 | tf_op jit(solution)/shard_map/feed_forward/pallas_call | solution.py:961
  75.8 9.2 %norm_qkv.3 = (bf16[1024,768]{1,0:T(8,128)(2,1)}, bf16[1024,768]{1,0:T(8,128)(2,1)}, bf16[2,1024,768]{2,1,0:T(8,128)(2,1)}, bf16[2,1024,768]{2,1,0:T(8,128)(2,1)}) custom-call(f32[1024,768]{1,0:T(8,128)} %get-tuple-element.98.refs_0_.refs_5_.refs_3_, bf16[2,768,2304]{2,1,0:T(8,128)(2,1)} %refs_6_.9, f32[2,768]{1,0:T(2,128)} %refs_7_.7, f32[2,768]{1,0:T(2,128)} %refs_3_.7, ...), custom_call_target="tpu_custom_call" | custom-call | flops 10000000000 | tf_op jit(solution)/shard_map/norm_qkv/pallas_call | solution.py:212
  85.0 27.0 %attend.3 = (bf16[1024,768]{1,0:T(8,128)(2,1)}, f32[6,8,1024]{2,1,0:T(8,128)}) custom-call(bf16[1024,768]{1,0:T(8,128)(2,1)} %get-tuple-element.99.q.refs_0_, bf16[2,1024,768]{2,1,0:T(8,128)(2,1)} %get-tuple-element.100.kv.refs_1_, bf16[2,1024,768]{2,1,0:T(8,128)(2,1)} %get-tuple-element.101.kvo.refs_2_), custom_call_target="tpu_custom_call" | custom-call | flops 32000000000 | tf_op jit(solution)/shard_map/attend/pallas_call | solution.py:286
  112.0 0.0 collective-permute-done.refs_11_
  112.0 0.0 copy-start
  112.0 0.9 copy-done
  112.9 52.2 %feed_forward_both.1 = (f32[512,768]{1,0:T(8,128)}, bf16[512,768]{1,0:T(8,128)(2,1)}, f32[1024,768]{1,0:T(8,128)}, bf16[1024,768]{1,0:T(8,128)(2,1)}, f32[8,768]...) custom-call(bf16[1024,768]{1,0:T(8,128)(2,1)} %get-tuple-element.102, ...), custom_call_target="tpu_custom_call" | custom-call | flops 56000000000 | tf_op jit(solution)/shard_map/feed_forward_both/pallas_call | solution.py:961
  165.1 78.0 %attend_back.2 = (bf16[1024,768]{1,0:T(8,128)(2,1)}, bf16[2,1024,768]{2,1,0:T(8,128)(2,1)}, bf16[6,2,1024,128]{3,2,1,0:T(8,128)(2,1)}, f32[24,768]{1,0:T(8,128)}...) custom-call(bf16[1024,768]{1,0:T(8,128)(2,1)} %get-tuple-element.99.q.refs_0_, ...), custom_call_target="tpu_custom_call" | custom-call | flops 73999998976 | tf_op jit(solution)/shard_map/attend_back/pallas_call | solution.py:577
  243.2 19.4 %joined_back.1 = (f32[1024,768]{1,0:T(8,128)}, bf16[1024,768]{1,0:T(8,128)(2,1)}, f32[8,768]{1,0:T(8,128)}, bf16[384,2304]{1,0:T(8,128)(2,1)}, bf16[384,2304]{1,0:T(8,128)(2,1)}) custom-call(bf16[1024,768]{1,0:T(8,128)(2,1)} %get-tuple-element.119.refs_0_, bf16[2,1024,768]{2,1,0:T(8,128)(2,1)} %get-tuple-element.120.refs_1_, ...), custom_call_target="tpu_custom_call" | custom-call | flops 16000000000 | tf_op jit(solution)/shard_map/joined_back/pallas_call | solution.py:1166
  262.6 42.4 %feed_forward_back.1 = (f32[1024,768]{1,0:T(8,128)}, bf16[1024,768]{1,0:T(8,128)(2,1)}, f32[8,768]{1,0:T(8,128)}, f32[8,3072]{1,0:T(8,128)}, bf16[384,768]{1,0:T...) custom-call(bf16[1024,768]{1,0:T(8,128)(2,1)} %get-tuple-element.96., ...), custom_call_target="tpu_custom_call" | custom-call | flops 35999997952 | tf_op jit(solution)/shard_map/feed_forward_back/pallas_call | solution.py:961
  305.0 75.6 %attend_back.3 = (bf16[1024,768]{1,0:T(8,128)(2,1)}, bf16[2,1024,768]{2,1,0:T(8,128)(2,1)}, bf16[6,2,1024,128]{3,2,1,0:T(8,128)(2,1)}, f32[24,768]{1,0:T(8,128)}, f32[24,3072]{1,0:T(8,128)}, /*index=5*/f32[96,768]{1,0:T(8,128)}) custom-call(bf16[1024,768]{1,0:T(8,128)(2,1)} %get-tuple-element.93.q.refs_0_, ...), custom_call_target="tpu_custom_call" | custom-call | flops 73999998976 | tf_op jit(solution)/shard_map/attend_back/pallas_call | solution.py:577
  380.6 44.9 %joined_back_sums.1 = (f32[512,768]{1,0:T(8,128)}, bf16[512,768]{1,0:T(8,128)(2,1)}, f32[24,768]{1,0:T(8,128)}, f32[24,2304]{1,0:T(8,128)}) custom-call(bf16[1024,768]{1,0:T(8,128)(2,1)} %get-tuple-element.144.refs_0_, bf16[2,1024,768]{2,1,0:T(8,128)(2,1)} %get-tuple-element.145.refs_1_, bf16[6,2,1024,128]{3,2,1,0:T(8,128)(2,1)} %get-tuple-element.146.refs_2_, ...), custom_call_target="tpu_custom_call" | custom-call | flops 35999997952 | tf_op jit(solution)/shard_map/joined_back_sums/pallas_call | solution.py:1166
  425.5 6.9 %finish.1 = (f32[2,512,768]{2,1,0:T(8,128)}, f32[2,512,768]{2,1,0:T(8,128)}, f32[2,24,2304]{2,1,0:T(8,128)}, f32[2,24,768]{2,1,0:T(8,128)}, f32[2,24,3072]{2,1,0...) custom-call(f32[512,768]{1,0:T(8,128)} %get-tuple-element.105.refs_0, ...), custom_call_target="tpu_custom_call" | custom-call | flops 4000000000 | tf_op jit(solution)/shard_map/finish/pallas_call | solution.py:1263
Async XLA Ops:
  26.2 85.8 %collective-permute-start = (bf16[512,768]{1,0:T(8,128)(2,1)}, bf16[512,768]{1,0:T(8,128)(2,1)S(1)}, u32[]{:S(2)}, u32[]{:S(2)}) collective-permute-start(bf16[512,768]{1,0:T(8,128)(2,1)} %get-tuple-element.104), channel_id=1, source_target_pairs={{0,2},{1,3},{2,0},{3,1},{4,6},{5,7},{6,4},{7,5},{8,10},{9,11},{10,... | collective-permute-start | bytes 2359304 | tf_op jit(solution)/shard_map/ppermute | solution.py:1318
  112.0 0.9 copy-start

commit v5 on v4

--- a/solution.py
+++ b/solution.py
@@ -319,13 +319,12 @@
 
 
 class Job:
-    def __init__(self, keep, send, count, orders, shape=None):
+    def __init__(self, both, count, orders, shape=None):
         self.lead = count.bit_length() - 2
-        self.made = keep is None
+        self.made = both is None
         if not self.made:
-            self.keep = keep.reshape((2,) * self.lead + keep.shape[1:])
-            self.send = send.reshape((2,) * self.lead + send.shape[1:])
-        self.rows, self.cols = shape or keep.shape[1:]
+            self.both = both.reshape((2,) * (self.lead + 1) + both.shape[2:])
+        self.rows, self.cols = shape or both.shape[2:]
         self.orders = orders
         self.wide = self.cols // len(orders)
         self.dtype = BF
@@ -334,9 +333,7 @@
         out = []
         for _ in self.orders:
             block = (self.rows, self.wide)
-            out.append(pltpu.VMEM((2,) * self.lead + block, self.dtype))
-            if self.made:
-                out.append(pltpu.VMEM((2,) * self.lead + block, self.dtype))
+            out.append(pltpu.VMEM((2,) * (self.lead + self.made) + block, self.dtype))
             for left in range(self.lead, -1, -1):
                 out.append(pltpu.VMEM((2,) * left + block, self.dtype))
         return out
@@ -346,27 +343,24 @@
 
 
 class Part:
-    def __init__(self, place, job, at, keep, send, out, scratch, sems, first_sem):
-        self.place, self.job, self.keep, self.send, self.out = place, job, keep, send, out
+    def __init__(self, place, job, at, both, out, scratch, sems, first_sem):
+        self.place, self.job, self.both, self.out = place, job, both, out
         self.order = job.orders[at]
         self.cols = slice(at * job.wide, (at + 1) * job.wide)
         self.total, self.got = scratch[0], scratch[1:]
         self.sems, self.first = sems, first_sem
+        self.every = (slice(None),) * (job.lead + 1)
+        self.pre = (place.bit(0),) if job.made else ()
 
     def fill(self, out, rows):
         lead = self.job.lead
-        for core in range(2):
-
-            @pl.when(self.place.bit(0) == core)
-            def _(core=core):
-                for at in range(2 << lead):
-                    index = tuple((at >> (b + 1)) & 1 for b in reversed(range(lead)))
-                    into = self.total if at % 2 == core else self.send
-                    into[index] = out[at * rows : (at + 1) * rows].astype(BF)
+        for at in range(2 << lead):
+            index = (at % 2,) + tuple((at >> (b + 1)) & 1 for b in reversed(range(lead)))
+            self.total[index] = out[at * rows : (at + 1) * rows].astype(BF)
 
     def own(self):
         return pltpu.make_async_copy(
-            self.keep.at[(slice(None),) * (self.job.lead + 1) + (self.cols,)], self.total, self.sems.at[0, self.first]
+            self.both.at[(self.place.bit(0),) + self.every + (self.cols,)], self.total, self.sems.at[0, self.first]
         )
 
     def index(self, stage, away):
@@ -382,12 +376,12 @@
         return tuple(out)
 
     def copy(self, stage):
-        if stage == 0 and self.keep is None:
-            bit, src = 0, self.send
+        if stage == 0 and self.job.made:
+            bit, src = 0, self.total.at[1 - self.place.bit(0)]
         elif stage == 0:
-            bit, src = 0, self.send.at[(slice(None),) * (self.job.lead + 1) + (self.cols,)]
+            bit, src = 0, self.both.at[(1 - self.place.bit(0),) + self.every + (self.cols,)]
         else:
-            bit, src = self.order[stage - 1], self.total.at[self.index(stage, True)]
+            bit, src = self.order[stage - 1], self.total.at[self.pre + self.index(stage, True)]
         return pltpu.make_async_remote_copy(
             src_ref=src,
             dst_ref=self.got[stage],
@@ -398,19 +392,20 @@
         )
 
     def begin(self, stage):
-        if stage == 0 and self.keep is not None:
+        if stage == 0 and not self.job.made:
             self.own().start()
         self.copy(stage).start()
 
     def end(self, stage):
-        if stage == 0 and self.keep is not None:
+        if stage == 0 and not self.job.made:
             self.own().wait()
         self.copy(stage).wait()
-        index = self.index(stage, False)
+        index = self.pre + self.index(stage, False)
         if stage == len(self.order):
             self.out[:, self.cols] = self.total[index].astype(F32) + self.got[stage][...].astype(F32)
         elif stage == 0:
-            self.total[...] = self.total[...] + self.got[0][...]
+            index = self.pre + self.every
+            self.total[index] = self.total[index] + self.got[0][...]
         else:
             self.total[index] = self.total[index] + self.got[stage][...]
 
@@ -432,13 +427,13 @@
         self.stages = count.bit_length() - 1
 
     def n_ins(self):
-        return 2 * sum(not job.made for job in self.jobs) + (self.trade is not None)
+        return sum(not job.made for job in self.jobs) + (self.trade is not None)
 
     def n_outs(self):
         return len(self.jobs) + (self.trade is not None)
 
     def inputs(self):
-        return [x for job in self.jobs if not job.made for x in (job.keep, job.send)] + ([] if self.trade is None else [self.trade])
+        return [job.both for job in self.jobs if not job.made] + ([] if self.trade is None else [self.trade])
 
     def n_parts(self):
         return sum(len(job.orders) for job in self.jobs)
@@ -466,13 +461,9 @@
         self.swap = None if self.trade is None else Trade(place, ins[-1], outs[-1], trade_sems)
         for i, job in enumerate(self.jobs):
             for at in range(len(job.orders)):
-                size = job.lead + 2 + job.made
-                mine, scratch = scratch[:size], scratch[size:]
-                if job.made:
-                    keep, send = None, mine.pop(1)
-                else:
-                    keep, send = ins[2 * i], ins[2 * i + 1]
-                found.append(Part(place, job, at, keep, send, outs[i], mine, sems, len(found) * self.stages))
+                mine, scratch = scratch[: job.lead + 2], scratch[job.lead + 2 :]
+                both = None if job.made else ins[i]
+                found.append(Part(place, job, at, both, outs[i], mine, sems, len(found) * self.stages))
         return found
 
     def advance(self, parts, stage):
@@ -601,18 +592,8 @@
     return even, odd
 
 
-def deliver(core, out, rows, keep, send):
-    even, odd = split_rows(out, rows)
-
-    @pl.when(core == 0)
-    def _():
-        keep[...] = even
-        send[...] = odd
-
-    @pl.when(core == 1)
-    def _():
-        keep[...] = odd
-        send[...] = even
+def deliver(out, rows, both):
+    both[0], both[1] = split_rows(out, rows)
 
 
 def grad_dot(a, b):
@@ -821,10 +802,9 @@
                     copies.start(N.next, i)
 
     if backward:
-        core = Place(2).bit(0)
         r[N.sums_ff][0:1, :] = ff_sum
-        deliver(core, grad_dot(r[N.act_v][slot], r[N.dz_v][...]), chunks[1], r[N.wd_keep], r[N.wd_send])
-        deliver(core, grad_dot(r[N.n2_v][...], r[N.dh_v][...]), chunks[0], r[N.wu_keep], r[N.wu_send])
+        deliver(grad_dot(r[N.act_v][slot], r[N.dz_v][...]), chunks[1], r[N.wd_both])
+        deliver(grad_dot(r[N.n2_v][...], r[N.dh_v][...]), chunks[0], r[N.wu_both])
 
     @pl.when(final)
     def _():
@@ -852,7 +832,7 @@
                 r[N.sums][3:4, :] += column_sum(dy.astype(F32))
                 r[N.da_v][at] = dot(dy, r[N.wo_v][...], NT).astype(BF)
                 copies.start(N.da, i)
-            deliver(core, grad_dot(r[N.att_v][...], r[N.dh_v][...]), chunks[0], r[N.wo_keep], r[N.wo_send])
+            deliver(grad_dot(r[N.att_v][...], r[N.dh_v][...]), chunks[0], r[N.wo_both])
         for i in every:
             if forward:
                 copies.wait(N.next, i)
@@ -915,10 +895,9 @@
         outs.add(N.da, hbm, ((t, d), BF))
         outs.add(N.sums, whole((8, d)), ((8, d), F32))
         outs.add(N.sums_ff, pl.BlockSpec((8, cut), lambda j: (0, j)), ((8, ff), F32))
-        for kind in (N.keep, N.send):
-            outs.add(N.wo_ + kind, whole((d // 2, d)), ((d // 2, d), BF))
-            outs.add(N.wu_ + kind, pl.BlockSpec((d // 2, cut), lambda j: (0, j)), ((d // 2, ff), BF))
-            outs.add(N.wd_ + kind, pl.BlockSpec((cut // 2, d), lambda j: (j, 0)), ((ff // 2, d), BF))
+        outs.add(N.wo_both, whole((2, d // 2, d)), ((2, d // 2, d), BF))
+        outs.add(N.wu_both, pl.BlockSpec((2, d // 2, cut), lambda j: (0, 0, j)), ((2, d // 2, ff), BF))
+        outs.add(N.wd_both, pl.BlockSpec((2, cut // 2, d), lambda j: (0, j, 0)), ((2, ff // 2, d), BF))
         scratch.add(N.dz_v, pltpu.VMEM((t, d), BF))
         scratch.add(N.dn_v, pltpu.VMEM((t, d), F32))
         scratch.add(N.dh_v, pltpu.VMEM((t, d), BF))
@@ -1057,10 +1036,8 @@
             copies.wait(N.normed, i)
         for k, total in enumerate(totals):
             r[N.sums][k : k + 1, :] = total
-        core = Place(2).bit(0)
         for k in range(3):
-            cols = slice(k * d, (k + 1) * d)
-            deliver(core, product(k), rows, r[N.keep].at[:, cols], r[N.send].at[:, cols])
+            deliver(product(k), rows, r[N.both].at[:, :, k * d : (k + 1) * d])
     else:
         vectors = r[N.vectors]
 
@@ -1159,8 +1136,7 @@
     else:
         outs.add(N.low, hbm, ((t, d), BF))
         outs.add(N.sums, vmem, ((8, d), F32))
-        for kind in (N.keep, N.send):
-            outs.add(kind, vmem, ((d // 2, 3 * d), BF))
+        outs.add(N.both, vmem, ((2, d // 2, 3 * d), BF))
         compiler_params = params(62)
     scratch.add(N.sems, pltpu.SemaphoreType.DMA((1 + (t // block) * 8,)))
     found = pl.pallas_call(
@@ -1333,9 +1309,9 @@
         dp_bits[1:-1] + [1] + dp_bits[:1] + dp_bits[-1:],
     )
 
-    def job(keep, send):
-        split = (chunks // 2, 2 * keep.shape[0] // chunks, keep.shape[1])
-        return Job(keep.reshape(split), send.reshape(split), device_count, orders)
+    def job(both):
+        split = (2, chunks // 2, 2 * both.shape[1] // chunks, both.shape[2])
+        return Job(both.reshape(split), device_count, orders)
 
     final = {}
     waiting, back = None, None
@@ -1346,7 +1322,7 @@
             arrays = dict(att=att, g=back[N.g], dza=back[N.low], **{k: found[k] for k in (N.middle, N.n2, N.act, N.slope)})
             found = ffn_call(layer, chunks, arrays, weights, False, True, Sums([waiting], device_count), layers + layer)
             final[tag(N.m, 0, layer + 1)] = found[tag(N.sum_o, 0)]
-        jobs = [job(found[w + N._keep], found[w + N._send]) for w in (N.wo, N.wu, N.wd)]
+        jobs = [job(found[w + N._both]) for w in (N.wo, N.wu, N.wd)]
         trade_out = found[N.next_low] if top else None
         dq, dkv, dkvi, *done = attend_back_call(
             q, kv, kvo, found[N.da], att, lse, Sums(jobs, device_count, trade_out, 3), layer
@@ -1364,11 +1340,11 @@
             for l in range(2):
                 arrays.update({tag(N.sums, l): final.pop(tag(N.sums, l)), tag(N.sums_ff, l): final.pop(tag(N.sums_ff, l))})
             late = (orders[1], dp_bits[1:-1] + dp_bits[:1] + [1] + dp_bits[-1:]) * 3
-            made = Job(None, None, device_count, late, (d // chunks, 3 * d))
+            made = Job(None, device_count, late, (d // chunks, 3 * d))
             back = joined_back_call(arrays, layer, chunks, Sums([made], device_count), 2 * layers)
         else:
             back = joined_back_call(arrays, layer, chunks)
-            waiting = job(back[N.keep], back[N.send])
+            waiting = job(back[N.both])
     final.update(
         **{tag(N.m, 0, 0): back[tag(N.sum_o, 0)]}, input_own=back[N.g], input_got=back[N.got], vectors=back[N.vectors]
     )

time: 437 us -> 426 us (0.975)
  Pallas kernels: 430 us -> 419 us
    pallas_call x3, Pallas kernels: 116 us -> 107 us  [ffn_call(): pl.pallas_call(functools.partial(kernel, names=ins.names + outs.names + s...]
where the time goes in v5:
time: 426 us; the launch traced here: 422 us
  Pallas kernels  419 us (98%)
    pallas_call x2, Pallas kernels, attend_back_call(): pl.pallas_call(functools.partial(attend_back_kernel, chunk=min(256, t), s...  153 us
    pallas_call x3, Pallas kernels, ffn_call(): pl.pallas_call(functools.partial(kernel, names=ins.names + outs.names + s...  107 us
    pallas_call x2, Pallas kernels, joined_back_call(): pl.pallas_call(functools.partial(joined_back_kernel, names=ins.names + ou...  62.4 us
    pallas_call x2, Pallas kernels, attend_call(): pl.pallas_call(functools.partial(attend_kernel, chunk=min(256, t)), grid=...  53.9 us
    pallas_call x2, Pallas kernels, qkv_call(): pl.pallas_call(functools.partial(qkv_kernel, names=ins.names + outs.names...  34.8 us
  transfers between devices with their start and end apart: 1, of which 0 were waited for; matrix products, arithmetic and copies ran while one was open for 0% of the time, Pallas kernels for 20%

profile of v5, /device:TPU:0, one launch (start us, length us, event | category | flops | bytes accessed | tf_op | source)
XLA Modules:
  0.0 421.8 jit_solution(10998315734484371153)
XLA Ops:
  0.6 25.6 %norm_qkv.2 = (bf16[1024,768]{1,0:T(8,128)(2,1)}, bf16[512,768]{1,0:T(8,128)(2,1)}, bf16[512,768]{1,0:T(8,128)(2,1)}, bf16[1024,768]{1,0:T(8,128)(2,1)}, bf16[10...) custom-call(bf16[2,512,768]{2,1,0:T(8,128)(2,1)} %refs_0_.1, ...), custom_call_target="tpu_custom_call" | custom-call | flops 24000000000 | tf_op jit(solution)/shard_map/norm_qkv/pallas_call | solution.py:212
  26.2 1.2 collective-permute-start
  27.4 26.8 %attend.2 = (bf16[1024,768]{1,0:T(8,128)(2,1)}, f32[6,8,1024]{2,1,0:T(8,128)}) custom-call(bf16[1024,768]{1,0:T(8,128)(2,1)} %get-tuple-element.86.q.refs_0_, bf16[2,1024,768]{2,1,0:T(8,128)(2,1)} %get-tuple-element.87.kv.refs_1_, bf16[2,1024,768]{2,1,0:T(8,128)(2,1)} %get-tuple-element.88.kvo.refs_2_), custom_call_target="tpu_custom_call" | custom-call | flops 32000000000 | tf_op jit(solution)/shard_map/attend/pallas_call | solution.py:286
  54.2 21.7 %feed_forward.1 = (f32[1024,768]{1,0:T(8,128)}, f32[1024,768]{1,0:T(8,128)}, bf16[1024,768]{1,0:T(8,128)(2,1)}, bf16[1024,3072]{1,0:T(8,128)(2,1)}, bf16[1024,3072]{1,0:T(8,128)(2,1)}) custom-call(bf16[1024,768]{1,0:T(8,128)(2,1)} %get-tuple-element.89.refs_0_.refs_4_, bf16[2,768,768]{2,1,0:T(8,128)(2,1)} %refs_1_.9, bf16[2,768,3072]{2,1,0:T(8,128)(2,1)} %refs_2_.9, ...), custom_call_target="tpu_custom_call" | custom-call | flops 20000000000 | tf_op jit(solution)/shard_map/feed_forward/pallas_call | solution.py:940
  75.9 9.2 %norm_qkv.3 = (bf16[1024,768]{1,0:T(8,128)(2,1)}, bf16[1024,768]{1,0:T(8,128)(2,1)}, bf16[2,1024,768]{2,1,0:T(8,128)(2,1)}, bf16[2,1024,768]{2,1,0:T(8,128)(2,1)}) custom-call(f32[1024,768]{1,0:T(8,128)} %get-tuple-element.91.refs_0_.refs_5_.refs_3_, bf16[2,768,2304]{2,1,0:T(8,128)(2,1)} %refs_6_.9, f32[2,768]{1,0:T(2,128)} %refs_7_.7, f32[2,768]{1,0:T(2,128)} %refs_3_.7, ...), custom_call_target="tpu_custom_call" | custom-call | flops 10000000000 | tf_op jit(solution)/shard_map/norm_qkv/pallas_call | solution.py:212
  85.1 27.1 %attend.3 = (bf16[1024,768]{1,0:T(8,128)(2,1)}, f32[6,8,1024]{2,1,0:T(8,128)}) custom-call(bf16[1024,768]{1,0:T(8,128)(2,1)} %get-tuple-element.92.q.refs_0_, bf16[2,1024,768]{2,1,0:T(8,128)(2,1)} %get-tuple-element.93.kv.refs_1_, bf16[2,1024,768]{2,1,0:T(8,128)(2,1)} %get-tuple-element.94.kvo.refs_2_), custom_call_target="tpu_custom_call" | custom-call | flops 32000000000 | tf_op jit(solution)/shard_map/attend/pallas_call | solution.py:286
  112.2 0.0 collective-permute-done.refs_11_
  112.2 0.0 copy-start
  112.2 0.9 copy-done
  113.1 47.0 %feed_forward_both.1 = (f32[512,768]{1,0:T(8,128)}, bf16[512,768]{1,0:T(8,128)(2,1)}, f32[1024,768]{1,0:T(8,128)}, bf16[1024,768]{1,0:T(8,128)(2,1)}, f32[8,768]...) custom-call(bf16[1024,768]{1,0:T(8,128)(2,1)} %get-tuple-element.95., ...), custom_call_target="tpu_custom_call" | custom-call | flops 56000000000 | tf_op jit(solution)/shard_map/feed_forward_both/pallas_call | solution.py:940
  160.1 77.8 %attend_back.2 = (bf16[1024,768]{1,0:T(8,128)(2,1)}, bf16[2,1024,768]{2,1,0:T(8,128)(2,1)}, bf16[6,2,1024,128]{3,2,1,0:T(8,128)(2,1)}, f32[24,768]{1,0:T(8,128)}...) custom-call(bf16[1024,768]{1,0:T(8,128)(2,1)} %get-tuple-element.92.q.refs_0_, ...), custom_call_target="tpu_custom_call" | custom-call | flops 73999998976 | tf_op jit(solution)/shard_map/attend_back/pallas_call | solution.py:568
  237.9 17.9 %joined_back.1 = (f32[1024,768]{1,0:T(8,128)}, bf16[1024,768]{1,0:T(8,128)(2,1)}, f32[8,768]{1,0:T(8,128)}, bf16[2,384,2304]{2,1,0:T(8,128)(2,1)}) custom-call(bf16[1024,768]{1,0:T(8,128)(2,1)} %get-tuple-element.109.refs_0_, bf16[2,1024,768]{2,1,0:T(8,128)(2,1)} %get-tuple-element.110.refs_1_, bf16[6,2,1024,128]{3,2,1,0:T(8,128)(2,1)} %get-tuple-element.111.refs_2_, ...), custom_call_target="tpu_custom_call" | custom-call | flops 16000000000 | tf_op jit(solution)/shard_map/joined_back/pallas_call | solution.py:1142
  255.8 38.7 %feed_forward_back.1 = (f32[1024,768]{1,0:T(8,128)}, bf16[1024,768]{1,0:T(8,128)(2,1)}, f32[8,768]{1,0:T(8,128)}, f32[8,3072]{1,0:T(8,128)}, bf16[2,384,768]{2,1...) custom-call(bf16[1024,768]{1,0:T(8,128)(2,1)} %get-tuple-element.89.refs_0_.refs_, ...), custom_call_target="tpu_custom_call" | custom-call | flops 35999997952 | tf_op jit(solution)/shard_map/feed_forward_back/pallas_call | solution.py:940
  294.5 75.3 %attend_back.3 = (bf16[1024,768]{1,0:T(8,128)(2,1)}, bf16[2,1024,768]{2,1,0:T(8,128)(2,1)}, bf16[6,2,1024,128]{3,2,1,0:T(8,128)(2,1)}, f32[24,768]{1,0:T(8,128)}, f32[24,3072]{1,0:T(8,128)}, /*index=5*/f32[96,768]{1,0:T(8,128)}) custom-call(bf16[1024,768]{1,0:T(8,128)(2,1)} %get-tuple-element.86.q.refs_0_, ...), custom_call_target="tpu_custom_call" | custom-call | flops 73999998976 | tf_op jit(solution)/shard_map/attend_back/pallas_call | solution.py:568
  369.9 44.5 %joined_back_sums.1 = (f32[512,768]{1,0:T(8,128)}, bf16[512,768]{1,0:T(8,128)(2,1)}, f32[24,768]{1,0:T(8,128)}, f32[24,2304]{1,0:T(8,128)}) custom-call(bf16[1024,768]{1,0:T(8,128)(2,1)} %get-tuple-element.130.refs_0_, bf16[2,1024,768]{2,1,0:T(8,128)(2,1)} %get-tuple-element.131.refs_1_, bf16[6,2,1024,128]{3,2,1,0:T(8,128)(2,1)} %get-tuple-element.132.refs_2_, ...), custom_call_target="tpu_custom_call" | custom-call | flops 35999997952 | tf_op jit(solution)/shard_map/joined_back_sums/pallas_call | solution.py:1142
  414.4 6.9 %finish.1 = (f32[2,512,768]{2,1,0:T(8,128)}, f32[2,512,768]{2,1,0:T(8,128)}, f32[2,24,2304]{2,1,0:T(8,128)}, f32[2,24,768]{2,1,0:T(8,128)}, f32[2,24,3072]{2,1,0...) custom-call(f32[512,768]{1,0:T(8,128)} %get-tuple-element.98.refs_0_, ...), custom_call_target="tpu_custom_call" | custom-call | flops 4000000000 | tf_op jit(solution)/shard_map/finish/pallas_call | solution.py:1239
Async XLA Ops:
  26.2 86.0 %collective-permute-start = (bf16[512,768]{1,0:T(8,128)(2,1)}, bf16[512,768]{1,0:T(8,128)(2,1)S(1)}, u32[]{:S(2)}, u32[]{:S(2)}) collective-permute-start(bf16[512,768]{1,0:T(8,128)(2,1)} %get-tuple-element.97), channel_id=1, source_target_pairs={{0,2},{1,3},{2,0},{3,1},{4,6},{5,7},{6,4},{7,5},{8,10},{9,11},{10,... | collective-permute-start | bytes 2359304 | tf_op jit(solution)/shard_map/ppermute | solution.py:1294
  112.2 0.9 copy-start

commit v6 on v5

--- a/solution.py
+++ b/solution.py
@@ -853,7 +853,7 @@
     t, d = arrays[N.att].shape
     ff = weights[N.wu].shape[2]
     cut, count = d, ff // d
-    block = min(BLOCK, t)
+    block = min(2 * BLOCK, t // 2)
     once = pl.Buffered(1)
     ins, outs, scratch = Names(), Names(), Names()
     hbm = pl.BlockSpec(memory_space=pl.ANY)
@@ -1305,7 +1305,7 @@
     dp_bits = list(range(2, device_count.bit_length() - 1))
     orders = (
         [1] + dp_bits,
-        dp_bits[:1] + dp_bits[1:-1] + [1] + dp_bits[-1:],
+        dp_bits + [1],
         dp_bits[1:-1] + [1] + dp_bits[:1] + dp_bits[-1:],
     )
 
@@ -1339,7 +1339,10 @@
             arrays.update(sums_in=back[N.sums])
             for l in range(2):
                 arrays.update({tag(N.sums, l): final.pop(tag(N.sums, l)), tag(N.sums_ff, l): final.pop(tag(N.sums_ff, l))})
-            late = (orders[1], dp_bits[1:-1] + dp_bits[:1] + [1] + dp_bits[-1:]) * 3
+            late = (
+                dp_bits[:-1] + [1] + dp_bits[-1:],
+                dp_bits[1:-1] + dp_bits[:1] + [1] + dp_bits[-1:],
+            ) * 3
             made = Job(None, device_count, late, (d // chunks, 3 * d))
             back = joined_back_call(arrays, layer, chunks, Sums([made], device_count), 2 * layers)
         else:

time: 426 us -> 420 us (0.986)
  Pallas kernels: 419 us -> 412 us
    pallas_call x2, Pallas kernels: 153 us -> 146 us  [attend_back_call(): pl.pallas_call(functools.partial(attend_back_kernel, chunk=min(256, t), s...]
where the time goes in v6:
time: 420 us; the launch traced here: 416 us
  Pallas kernels  412 us (98%)
    pallas_call x2, Pallas kernels, attend_back_call(): pl.pallas_call(functools.partial(attend_back_kernel, chunk=min(256, t), s...  146 us
    pallas_call x3, Pallas kernels, ffn_call(): pl.pallas_call(functools.partial(kernel, names=ins.names + outs.names + s...  107 us
    pallas_call x2, Pallas kernels, joined_back_call(): pl.pallas_call(functools.partial(joined_back_kernel, names=ins.names + ou...  63.7 us
    pallas_call x2, Pallas kernels, attend_call(): pl.pallas_call(functools.partial(attend_kernel, chunk=min(256, t)), grid=...  53.9 us
    pallas_call x2, Pallas kernels, qkv_call(): pl.pallas_call(functools.partial(qkv_kernel, names=ins.names + outs.names...  34.8 us
  transfers between devices with their start and end apart: 1, of which 0 were waited for; matrix products, arithmetic and copies ran while one was open for 0% of the time, Pallas kernels for 20%

profile of v6, /device:TPU:0, one launch (start us, length us, event | category | flops | bytes accessed | tf_op | source)
XLA Modules:
  0.0 415.6 jit_solution(13433956000840815722)
XLA Ops:
  0.6 25.6 %norm_qkv.2 = (bf16[1024,768]{1,0:T(8,128)(2,1)}, bf16[512,768]{1,0:T(8,128)(2,1)}, bf16[512,768]{1,0:T(8,128)(2,1)}, bf16[1024,768]{1,0:T(8,128)(2,1)}, bf16[10...) custom-call(bf16[2,512,768]{2,1,0:T(8,128)(2,1)} %refs_0_.1, ...), custom_call_target="tpu_custom_call" | custom-call | flops 24000000000 | tf_op jit(solution)/shard_map/norm_qkv/pallas_call | solution.py:212
  26.2 1.2 collective-permute-start
  27.4 26.8 %attend.2 = (bf16[1024,768]{1,0:T(8,128)(2,1)}, f32[6,8,1024]{2,1,0:T(8,128)}) custom-call(bf16[1024,768]{1,0:T(8,128)(2,1)} %get-tuple-element.86.q.refs_0_, bf16[2,1024,768]{2,1,0:T(8,128)(2,1)} %get-tuple-element.87.kv.refs_1_, bf16[2,1024,768]{2,1,0:T(8,128)(2,1)} %get-tuple-element.88.kvo.refs_2_), custom_call_target="tpu_custom_call" | custom-call | flops 32000000000 | tf_op jit(solution)/shard_map/attend/pallas_call | solution.py:286
  54.2 21.3 %feed_forward.1 = (f32[1024,768]{1,0:T(8,128)}, f32[1024,768]{1,0:T(8,128)}, bf16[1024,768]{1,0:T(8,128)(2,1)}, bf16[1024,3072]{1,0:T(8,128)(2,1)}, bf16[1024,3072]{1,0:T(8,128)(2,1)}) custom-call(bf16[1024,768]{1,0:T(8,128)(2,1)} %get-tuple-element.89.refs_0_.refs_4_, bf16[2,768,768]{2,1,0:T(8,128)(2,1)} %refs_1_.9, bf16[2,768,3072]{2,1,0:T(8,128)(2,1)} %refs_2_.9, ...), custom_call_target="tpu_custom_call" | custom-call | flops 20000000000 | tf_op jit(solution)/shard_map/feed_forward/pallas_call | solution.py:940
  75.5 9.2 %norm_qkv.3 = (bf16[1024,768]{1,0:T(8,128)(2,1)}, bf16[1024,768]{1,0:T(8,128)(2,1)}, bf16[2,1024,768]{2,1,0:T(8,128)(2,1)}, bf16[2,1024,768]{2,1,0:T(8,128)(2,1)}) custom-call(f32[1024,768]{1,0:T(8,128)} %get-tuple-element.91.refs_0_.refs_5_.refs_3_, bf16[2,768,2304]{2,1,0:T(8,128)(2,1)} %refs_6_.9, f32[2,768]{1,0:T(2,128)} %refs_7_.7, f32[2,768]{1,0:T(2,128)} %refs_3_.7, ...), custom_call_target="tpu_custom_call" | custom-call | flops 10000000000 | tf_op jit(solution)/shard_map/norm_qkv/pallas_call | solution.py:212
  84.7 27.1 %attend.3 = (bf16[1024,768]{1,0:T(8,128)(2,1)}, f32[6,8,1024]{2,1,0:T(8,128)}) custom-call(bf16[1024,768]{1,0:T(8,128)(2,1)} %get-tuple-element.92.q.refs_0_, bf16[2,1024,768]{2,1,0:T(8,128)(2,1)} %get-tuple-element.93.kv.refs_1_, bf16[2,1024,768]{2,1,0:T(8,128)(2,1)} %get-tuple-element.94.kvo.refs_2_), custom_call_target="tpu_custom_call" | custom-call | flops 32000000000 | tf_op jit(solution)/shard_map/attend/pallas_call | solution.py:286
  111.8 0.0 collective-permute-done.refs_11_
  111.8 0.0 copy-start
  111.8 0.9 copy-done
  112.7 47.2 %feed_forward_both.1 = (f32[512,768]{1,0:T(8,128)}, bf16[512,768]{1,0:T(8,128)(2,1)}, f32[1024,768]{1,0:T(8,128)}, bf16[1024,768]{1,0:T(8,128)(2,1)}, f32[8,768]...) custom-call(bf16[1024,768]{1,0:T(8,128)(2,1)} %get-tuple-element.95., ...), custom_call_target="tpu_custom_call" | custom-call | flops 56000000000 | tf_op jit(solution)/shard_map/feed_forward_both/pallas_call | solution.py:940
  159.9 74.0 %attend_back.2 = (bf16[1024,768]{1,0:T(8,128)(2,1)}, bf16[2,1024,768]{2,1,0:T(8,128)(2,1)}, bf16[6,2,1024,128]{3,2,1,0:T(8,128)(2,1)}, f32[24,768]{1,0:T(8,128)}...) custom-call(bf16[1024,768]{1,0:T(8,128)(2,1)} %get-tuple-element.92.q.refs_0_, ...), custom_call_target="tpu_custom_call" | custom-call | flops 73999998976 | tf_op jit(solution)/shard_map/attend_back/pallas_call | solution.py:568
  233.9 17.9 %joined_back.1 = (f32[1024,768]{1,0:T(8,128)}, bf16[1024,768]{1,0:T(8,128)(2,1)}, f32[8,768]{1,0:T(8,128)}, bf16[2,384,2304]{2,1,0:T(8,128)(2,1)}) custom-call(bf16[1024,768]{1,0:T(8,128)(2,1)} %get-tuple-element.109.refs_0_, bf16[2,1024,768]{2,1,0:T(8,128)(2,1)} %get-tuple-element.110.refs_1_, bf16[6,2,1024,128]{3,2,1,0:T(8,128)(2,1)} %get-tuple-element.111.refs_2_, ...), custom_call_target="tpu_custom_call" | custom-call | flops 16000000000 | tf_op jit(solution)/shard_map/joined_back/pallas_call | solution.py:1142
  251.7 38.4 %feed_forward_back.1 = (f32[1024,768]{1,0:T(8,128)}, bf16[1024,768]{1,0:T(8,128)(2,1)}, f32[8,768]{1,0:T(8,128)}, f32[8,3072]{1,0:T(8,128)}, bf16[2,384,768]{2,1...) custom-call(bf16[1024,768]{1,0:T(8,128)(2,1)} %get-tuple-element.89.refs_0_.refs_, ...), custom_call_target="tpu_custom_call" | custom-call | flops 35999997952 | tf_op jit(solution)/shard_map/feed_forward_back/pallas_call | solution.py:940
  290.1 72.2 %attend_back.3 = (bf16[1024,768]{1,0:T(8,128)(2,1)}, bf16[2,1024,768]{2,1,0:T(8,128)(2,1)}, bf16[6,2,1024,128]{3,2,1,0:T(8,128)(2,1)}, f32[24,768]{1,0:T(8,128)}, f32[24,3072]{1,0:T(8,128)}, /*index=5*/f32[96,768]{1,0:T(8,128)}) custom-call(bf16[1024,768]{1,0:T(8,128)(2,1)} %get-tuple-element.86.q.refs_0_, ...), custom_call_target="tpu_custom_call" | custom-call | flops 73999998976 | tf_op jit(solution)/shard_map/attend_back/pallas_call | solution.py:568
  362.3 45.9 %joined_back_sums.1 = (f32[512,768]{1,0:T(8,128)}, bf16[512,768]{1,0:T(8,128)(2,1)}, f32[24,768]{1,0:T(8,128)}, f32[24,2304]{1,0:T(8,128)}) custom-call(bf16[1024,768]{1,0:T(8,128)(2,1)} %get-tuple-element.130.refs_0_, bf16[2,1024,768]{2,1,0:T(8,128)(2,1)} %get-tuple-element.131.refs_1_, bf16[6,2,1024,128]{3,2,1,0:T(8,128)(2,1)} %get-tuple-element.132.refs_2_, ...), custom_call_target="tpu_custom_call" | custom-call | flops 35999997952 | tf_op jit(solution)/shard_map/joined_back_sums/pallas_call | solution.py:1142
  408.2 6.9 %finish.1 = (f32[2,512,768]{2,1,0:T(8,128)}, f32[2,512,768]{2,1,0:T(8,128)}, f32[2,24,2304]{2,1,0:T(8,128)}, f32[2,24,768]{2,1,0:T(8,128)}, f32[2,24,3072]{2,1,0...) custom-call(f32[512,768]{1,0:T(8,128)} %get-tuple-element.98.refs_0_, ...), custom_call_target="tpu_custom_call" | custom-call | flops 4000000000 | tf_op jit(solution)/shard_map/finish/pallas_call | solution.py:1239
Async XLA Ops:
  26.2 85.6 %collective-permute-start = (bf16[512,768]{1,0:T(8,128)(2,1)}, bf16[512,768]{1,0:T(8,128)(2,1)S(1)}, u32[]{:S(2)}, u32[]{:S(2)}) collective-permute-start(bf16[512,768]{1,0:T(8,128)(2,1)} %get-tuple-element.97), channel_id=1, source_target_pairs={{0,2},{1,3},{2,0},{3,1},{4,6},{5,7},{6,4},{7,5},{8,10},{9,11},{10,... | collective-permute-start | bytes 2359304 | tf_op jit(solution)/shard_map/ppermute | solution.py:1294
  111.8 0.9 copy-start
